TPU v7x, 512 devices: a whole 4x4x16 slice. The times are simulated.
512 devices in a mesh: row: 32 (over x, y, core), col: 16 (over z).
Axes of the slice: x: 4, y: 4, z: 16, core: 2. Of those that a mesh axis runs over, the one named last changes fastest.
Arguments:
- inputs: bfloat16 [512, 16384], P('col', 'row'), may hold values from -6 to 6
- out_grad: bfloat16 [512, 16384], P('col', 'row'), may hold values from -6 to 6
- gate_weight: bfloat16 [16384, 13312], P('row', 'col'), may hold values from -0.046875 to 0.046875
- up_weight: bfloat16 [16384, 13312], P('row', 'col'), may hold values from -0.046875 to 0.046875
- down_weight: bfloat16 [13312, 16384], P('col', 'row'), may hold values from -0.0546875 to 0.0546875
Outputs:
- input_grad: bfloat16 [512, 16384], P('col', 'row')
- gate_grad: bfloat16 [16384, 13312], P('row', 'col')
- up_grad: bfloat16 [16384, 13312], P('row', 'col')
- down_grad: bfloat16 [13312, 16384], P('col', 'row')
All inputs are finite; a program needn't handle non-finite values.
Results may differ from a plain program's by a relative error of at most 0.0049.
Values may be sent and summed in bfloat16 or wider, within the bound.
No kernel may reach another device: no remote copies, remote signals or barrier semaphores. Data moves between devices by JAX's collectives and lax.ppermute only.
A program may use at most 64 MiB of HBM per device.

v0:
```python
import jax
import jax.numpy as jnp
from jax import lax
from jax.sharding import PartitionSpec as P


def nonlinear(gate, up, hidden_grad):
    sig = jax.nn.sigmoid(gate)
    silu = gate * sig
    hidden = (silu * up).astype(jnp.bfloat16)
    gate_delta = (hidden_grad * up * sig * (1.0 + gate * (1.0 - sig))).astype(jnp.bfloat16)
    up_delta = (hidden_grad * silu).astype(jnp.bfloat16)
    return (hidden, gate_delta, up_delta)


def contract(left, right, left_dim, right_dim):
    return lax.dot_general(
        left, right, (((left_dim,), (right_dim,)), ((), ())), preferred_element_type=jnp.float32
    )


def per_device(inputs, out_grad, gate_weight, up_weight, down_weight):
    all_inputs, all_grads = (
        lax.all_gather(inputs, "col", axis=0, tiled=True),
        lax.all_gather(out_grad, "col", axis=0, tiled=True),
    )
    gate = jnp.dot(all_inputs, gate_weight, preferred_element_type=jnp.float32)
    up = jnp.dot(all_inputs, up_weight, preferred_element_type=jnp.float32)
    hidden_grad = contract(all_grads, down_weight, 1, 1)
    gate, up, hidden_grad = lax.psum((gate, up, hidden_grad), "row")
    hidden, gate_delta, up_delta = nonlinear(gate, up, hidden_grad)
    down_grad = contract(hidden, all_grads, 0, 0).astype(jnp.bfloat16)
    gate_grad = contract(all_inputs, gate_delta, 0, 0).astype(jnp.bfloat16)
    up_grad = contract(all_inputs, up_delta, 0, 0).astype(jnp.bfloat16)
    input_grad = lax.psum_scatter(
        contract(gate_delta, gate_weight, 1, 1) + contract(up_delta, up_weight, 1, 1),
        "col",
        scatter_dimension=0,
        tiled=True,
    )
    return (input_grad.astype(jnp.bfloat16), gate_grad, up_grad, down_grad)


def solution(mesh):
    return jax.shard_map(
        per_device,
        mesh=mesh,
        in_specs=(
            P("col", "row"),
            P("col", "row"),
            P("row", "col"),
            P("row", "col"),
            P("col", "row"),
        ),
        out_specs=(P("col", "row"), P("row", "col"), P("row", "col"), P("col", "row")),
        check_vma=False,
    )
```

profile of v0, /device:TPU:8, one launch (start us, length us, event | category | flops | bytes accessed | tf_op | source)
XLA Modules:
  0.0 308.4 jit_solution(14608846012540892973)
XLA Ops:
  7.2 0.0 copy-start
  7.2 0.0 all-reduce.3.cloned.1.call-start
  7.2 39.0 %all_gather.7 = bf16[512,512]{1,0:T(8,128)(2,1)S(1)} all-gather(bf16[32,512]{1,0:T(8,128)(2,1)} %param.5), channel_id=1, replica_groups=mesh['row'=32,'col'=16] {'col'}, dimensions={0}, use_global_device_ids=true | all-gather | bytes 557056 | tf_op jit(solution)/shard_map/all_gather | solution.py:24
  46.2 0.0 copy-start.1
  46.2 29.3 %all_gather.6 = bf16[512,512]{1,0:T(8,128)(2,1)S(1)} all-gather(bf16[32,512]{1,0:T(8,128)(2,1)} %param.6), channel_id=1, replica_groups=mesh['row'=32,'col'=16] {'col'}, dimensions={0}, use_global_device_ids=true | all-gather | bytes 557056 | tf_op jit(solution)/shard_map/all_gather | solution.py:25
  75.5 0.0 copy-done
  75.5 0.0 copy-start.2
  75.5 1.9 fusion.7
  77.4 0.0 copy-done.1
  77.4 0.0 copy-start.6
  77.4 1.9 fusion.6
  79.3 0.0 copy-done.2
  79.3 0.0 copy-done.6
  79.3 1.9 fusion.5
  81.2 0.0 all-reduce.3.cloned.1.call-update
  81.2 0.0 reduce-scatter.2.cloned.1.call-start
  81.3 140.8 %all-reduce.3.cloned.1.call-done = (f32[512,832]{0,1:T(8,128)}, f32[512,832]{0,1:T(8,128)}, f32[512,832]{0,1:T(8,128)}) async-done(((f32[512,832]{0,1:T(8,128)}, f32[512,832]{0,1:T(8,128)}, f32[512,832]{0,1:T(8,128)}), (f32[512,832]{0,1:T(8,128)}, f32[512,832]{0,1:T(8,128)}, f32[512,832]{0,1:T(8,128)})) %all-reduce.3.cloned.1.call-update) | async-done | bytes 5111824 | tf_op jit(solution)/shard_map/psum | solution.py:30
  222.1 3.5 %multiply_convert_fusion.1 = (bf16[512,832]{0,1:T(8,128)(2,1)S(1)}, bf16[512,832]{0,1:T(8,128)(2,1)S(1)}) fusion(f32[512,832]{0,1:T(8,128)} %get-tuple-element.5, f32[512,832]{0,1:T(8,128)} %get-tuple-element.4, f32[512,832]{0,1:T(8,128)} %get-tuple-element.6), kind=kLoop, calls=%fused_computation.1 | loop fusion | flops 5537792 | bytes 6815744 | tf_op jit(solution)/shard_map/convert_element_type | solution.py:12
  225.6 0.0 copy-start.7
  225.6 0.9 copy-done.7
  226.5 0.7 fusion.8
  227.2 1.7 convolution_add_fusion
  228.9 0.0 reduce-scatter.2.cloned.1.call-update
  228.9 0.0 copy-start.5
  228.9 1.5 fusion.2
  230.4 2.8 fusion.1
  233.3 0.0 copy-done.5
  233.3 0.0 copy-done.3
  233.3 0.0 copy-done.4
  233.3 1.5 convolution_convert_fusion
  234.8 65.3 %reduce-scatter.2.cloned.1.call-done = f32[32,512]{1,0:T(8,128)} async-done(((f32[512,512]{1,0:T(8,128)}), f32[32,512]{1,0:T(8,128)}) %reduce-scatter.2.cloned.1.call-update) | async-done | bytes 65552 | tf_op jit(solution)/shard_map/reduce_scatter | solution.py:35
  300.1 1.5 convert_element_type.29
  (2 shorter events, 0.0 us)
Async XLA Ops:
  7.2 68.4 %copy-start = (bf16[512,832]{0,1:T(8,128)(2,1)S(1)}, bf16[512,832]{0,1:T(8,128)(2,1)}, u32[]{:S(2)}) copy-start(bf16[512,832]{0,1:T(8,128)(2,1)} %param.7) | copy-start | bytes 2555908
  7.2 214.9 %all-reduce.3.cloned.1.call-start = ((), (), s32[]{:S(2)}) async-start(), calls=%async_computation.2 | async-start | bytes 10223616 | tf_op jit(solution)/shard_map/psum | solution.py:30
  46.2 31.2 %copy-start.1 = (bf16[512,832]{0,1:T(8,128)(2,1)S(1)}, bf16[512,832]{0,1:T(8,128)(2,1)}, u32[]{:S(2)}) copy-start(bf16[512,832]{0,1:T(8,128)(2,1)} %param.8) | copy-start | bytes 2555908
  75.5 3.8 %copy-start.2 = (bf16[512,512]{1,0:T(8,128)(2,1)}, bf16[512,512]{1,0:T(8,128)(2,1)S(1)}, u32[]{:S(2)}) copy-start(bf16[512,512]{1,0:T(8,128)(2,1)S(1)} %all_gather.6) | copy-start | bytes 1572868
  77.4 1.9 copy-start.6
  81.2 218.9 %reduce-scatter.2.cloned.1.call-start = ((), (), s32[]{:S(2)}) async-start(), calls=%async_computation.1 | async-start | bytes 1114112 | tf_op jit(solution)/shard_map/reduce_scatter | solution.py:35
  225.6 0.9 copy-start.7
  228.9 4.3 %copy-start.5 = (f32[512,832]{0,1:T(8,128)S(1)}, f32[512,832]{0,1:T(8,128)}, u32[]{:S(2)}) copy-start(f32[512,832]{0,1:T(8,128)} %get-tuple-element.6) | copy-start | bytes 5111812
  230.4 2.8 copy-start.3
  230.4 2.8 copy-start.4
Sparse Core Ops, SparseCore 0:
  81.3 140.7 all-reduce.2
  229.0 70.9 reduce-scatter.1
where the time goes:
time: 309 us; the launch traced here: 308 us
  waiting for transfers between devices  206 us (67%)
  blocking collectives  68.3 us (22%)
  between operations  14.1 us (5%)
  matrix products  13.9 us (4%)
  other arithmetic  4.92 us (2%)
    psum x1, waiting for transfers between devices, per_device(): gate, up, hidden_grad = lax.psum((gate, up, hidden_grad), 'row')  141 us
    reduce_scatter x1, waiting for transfers between devices, per_device(): lax.psum_scatter(contract(gate_delta, gate_weight, 1, 1) + contract(up_de...  65.3 us
    all_gather x1, blocking collectives, per_device(): lax.all_gather(inputs, 'col', axis=0, tiled=True)  39 us
    all_gather x1, blocking collectives, per_device(): lax.all_gather(out_grad, 'col', axis=0, tiled=True)  29.3 us
    dot_general x6, matrix products, contract(): lax.dot_general(left, right, (((left_dim,), (right_dim,)), ((), ())), pre...  10.2 us
  transfers between devices with their start and end apart: 2, of which 2 were waited for; matrix products, arithmetic and copies ran while one was open for 2% of the time, Pallas kernels for 0%

commit v1 on v0

v1 whole, which is shorter than its diff:
```python
import jax
import jax.numpy as jnp
from jax import lax
from jax.sharding import Mesh, PartitionSpec as P

BF16, F32 = jnp.bfloat16, jnp.float32
XY = ("x", "y")


def nonlinear(gate, up, hidden_grad):
    sig = jax.nn.sigmoid(gate)
    silu = gate * sig
    hidden = (silu * up).astype(BF16)
    gate_delta = (hidden_grad * up * sig * (1.0 + gate * (1.0 - sig))).astype(BF16)
    up_delta = (hidden_grad * silu).astype(BF16)
    return (hidden, gate_delta, up_delta)


def contract(left, right, left_dim, right_dim):
    return lax.dot_general(
        left, right, (((left_dim,), (right_dim,)), ((), ())), preferred_element_type=F32
    )


def spread(block, axes, n):
    return lax.all_to_all(jnp.broadcast_to(block, (n, *block.shape)), axes, 0, 0)


def swap_cores(value):
    return jax.tree.map(lambda v: lax.ppermute(v, "core", [(0, 1), (1, 0)]), value)


def per_device(inputs, out_grad, gate_weight, up_weight, down_weight):
    tokens, width = inputs.shape
    hidden_units = gate_weight.shape[1]
    core = lax.axis_index("core")
    both = jnp.stack([inputs, out_grad])
    near = spread(both, "z_hi", 4)
    every = spread(near, "z_lo", 4)
    half = 8 * tokens
    halves = every.transpose(2, 0, 1, 3, 4).reshape(2, 2, half, width)

    def pick(which):
        part = lax.dynamic_index_in_dim(halves, which, 1, keepdims=False)
        return part[0], part[1]

    x_own, g_own = pick(core)
    x_other, g_other = pick(1 - core)

    def products(x, g):
        return (
            jnp.dot(x, gate_weight, preferred_element_type=F32),
            jnp.dot(x, up_weight, preferred_element_type=F32),
            contract(g, down_weight, 1, 1),
        )

    arrived = swap_cores(products(x_other, g_other))
    sums = [(a + b).astype(BF16) for a, b in zip(products(x_own, g_own), arrived, strict=True)]
    n = 16
    parts = jnp.stack([s.reshape(n, half // n, hidden_units) for s in sums], axis=1)
    parts = lax.all_to_all(parts, XY, 0, 0)
    total = jnp.sum(parts.astype(F32), axis=0)
    result = jnp.stack(nonlinear(total[0], total[1], total[2]))
    own = spread(result, XY, n)
    own = own.transpose(1, 0, 2, 3).reshape(3, half, hidden_units)
    other = swap_cores(own)

    def input_part(deltas):
        return contract(deltas[1], gate_weight, 1, 1) + contract(deltas[2], up_weight, 1, 1)

    grads_in = jnp.zeros((2, half, width), BF16)
    for which, deltas in ((core, own), (1 - core, other)):
        grads_in = lax.dynamic_update_index_in_dim(
            grads_in, input_part(deltas).astype(BF16), which, 0
        )
    pieces = lax.all_to_all(grads_in.reshape(16, tokens, width), ("z_lo", "z_hi"), 0, 0)
    input_grad = jnp.sum(pieces.astype(F32), axis=0).astype(BF16)

    down_grad = contract(own[0], g_own, 0, 0) + contract(other[0], g_other, 0, 0)
    gate_grad = contract(x_own, own[1], 0, 0) + contract(x_other, other[1], 0, 0)
    up_grad = contract(x_own, own[2], 0, 0) + contract(x_other, other[2], 0, 0)
    return (input_grad, gate_grad.astype(BF16), up_grad.astype(BF16), down_grad.astype(BF16))


def solution(mesh):
    grid = Mesh(
        mesh.devices.reshape(4, 4, 2, 4, 4), ("x", "y", "core", "z_hi", "z_lo")
    )
    row, col = ("x", "y", "core"), ("z_hi", "z_lo")
    return jax.shard_map(
        per_device,
        mesh=grid,
        in_specs=(P(col, row), P(col, row), P(row, col), P(row, col), P(col, row)),
        out_specs=(P(col, row), P(row, col), P(row, col), P(col, row)),
        check_vma=False,
    )
```

time: 309 us -> 191 us (0.62)
  the two profiles are of different devices: /device:TPU:8 before, /device:TPU:64 now
where the time goes in v1:
time: 191 us; the launch traced here: 190 us
  blocking collectives  85.7 us (45%)
  waiting for transfers between devices  46.8 us (25%)
  matrix products  20.7 us (11%)
  starting transfers between devices  20.3 us (11%)
  local copies, waits for them, and re-layouts  12.9 us (7%)
  other arithmetic  3.04 us (2%)
    all_to_all x2, blocking collectives, spread(): lax.all_to_all(jnp.broadcast_to(block, (n, *block.shape)), axes, 0, 0)  57.9 us
    all_to_all x1, blocking collectives, per_device(): parts = lax.all_to_all(parts, XY, 0, 0)  27.9 us
    all_to_all x1, waiting for transfers between devices, per_device(): lax.all_to_all(grads_in.reshape(16, tokens, width), ('z_lo', 'z_hi'), 0, 0)  25.2 us
    all_to_all x1, waiting for transfers between devices, spread(): lax.all_to_all(jnp.broadcast_to(block, (n, *block.shape)), axes, 0, 0)  21.6 us
    dot_general x12, matrix products, contract(): lax.dot_general(left, right, (((left_dim,), (right_dim,)), ((), ())), pre...  13.4 us
    ppermute x4, starting transfers between devices, swap_cores(): lax.ppermute(v, 'core', [(0, 1), (1, 0)])  8.39 us
    all_to_all x1, starting transfers between devices, per_device(): lax.all_to_all(grads_in.reshape(16, tokens, width), ('z_lo', 'z_hi'), 0, 0)  7.68 us
    convert_element_type x3, local copies, waits for them, and re-layouts, per_device(): (a + b).astype(BF16)  4.48 us
  transfers between devices with their start and end apart: 6, of which 2 were waited for; matrix products, arithmetic and copies ran while one was open for 10% of the time, Pallas kernels for 0%

profile of v1, /device:TPU:64, one launch (start us, length us, event | category | flops | bytes accessed | tf_op | source)
XLA Modules:
  0.0 190.3 jit_solution(11546391097931957456)
XLA Ops:
  0.6 0.9 pad_maximum_fusion.2
  1.5 34.5 %all_to_all.25 = bf16[4,2,32,512]{3,2,1,0:T(8,128)(2,1)S(1)} all-to-all(bf16[4,2,32,512]{3,2,1,0:T(8,128)(2,1)S(1)} %broadcast_in_dim.20), channel_id=1, replica_groups=mesh['x'=4,'y'=4,'core'=2,'z_hi'=4,'z_lo'=4] {'z_hi'}, dimensions={0} | all-to-all | bytes 524288 | tf_op jit(solution)/shard_map/all_to_all | solution.py:26
  36.0 1.1 broadcast_in_dim.21
  37.1 4.2 %all-to-all-start.1 = ((bf16[4,4,2,32,512]{4,3,1,2,0:T(8,128)(2,1)}), bf16[4,4,2,32,512]{4,3,1,2,0:T(8,128)(2,1)S(1)}, u32[]{:S(2)}, u32[]{:S(2)}) async-start(bf16[4,4,2,32,512]{4,3,1,2,0:T(8,128)(2,1)} %broadcast_in_dim.21), calls=%async_computation.1 | async-start | bytes 2097152 | tf_op jit(solution)/shard_map/all_to_all | solution.py:26
  41.3 21.6 %all-to-all-done.1 = bf16[4,4,2,32,512]{4,3,1,2,0:T(8,128)(2,1)S(1)} async-done(((bf16[4,4,2,32,512]{4,3,1,2,0:T(8,128)(2,1)}), bf16[4,4,2,32,512]{4,3,1,2,0:T(8,128)(2,1)S(1)}, u32[]{:S(2)}, u32[]{:S(2)}) %all-to-all-start.1) | async-done | bytes 1048608 | tf_op jit(solution)/shard_map/all_to_all | solution.py:26
  63.0 2.5 %fusion.11 = f32[256,832]{0,1:T(8,128)} fusion(bf16[832,512]{1,0:T(8,128)(2,1)} %param.9, bf16[2,2,256,512]{3,2,1,0:T(8,128)(2,1)S(1)} %bitcast.68, s32[]{:T(128)S(6)} %add.57, s32[]{:T(128)S(6)} %select_n.11), kind=kOutput, calls=%fused_computation.28 | convolution fusion | flops 218103808 | bytes 1966088 | tf_op jit(solution)/shard_map/dot_general | solution.py:20
  65.4 2.0 %collective-permute-start.2 = (f32[256,832]{0,1:T(8,128)}, f32[256,832]{0,1:T(8,128)}, u32[]{:S(2)}, u32[]{:S(2)}) collective-permute-start(f32[256,832]{0,1:T(8,128)} %fusion.11), channel_id=1, source_target_pairs={{0,16},{16,0},{1,17},{17,1},{2,18},{18,2},{3,19},{19,3},{4,20},{20... | collective-permute-start | bytes 2555912 | tf_op jit(solution)/shard_map/ppermute | solution.py:30
  67.5 1.3 fusion.14
  68.8 2.4 %collective-permute-start.1 = (f32[256,832]{0,1:T(8,128)}, f32[256,832]{0,1:T(8,128)}, u32[]{:S(2)}, u32[]{:S(2)}) collective-permute-start(f32[256,832]{0,1:T(8,128)} %fusion.14), channel_id=1, source_target_pairs={{0,16},{16,0},{1,17},{17,1},{2,18},{18,2},{3,19},{19,3},{4,20},{20... | collective-permute-start | bytes 2555912 | tf_op jit(solution)/shard_map/ppermute | solution.py:30
  71.2 1.3 fusion.15
  72.5 1.9 %collective-permute-start = (f32[256,832]{0,1:T(8,128)}, f32[256,832]{0,1:T(8,128)}, u32[]{:S(2)}, u32[]{:S(2)}) collective-permute-start(f32[256,832]{0,1:T(8,128)} %fusion.15), channel_id=1, source_target_pairs={{0,16},{16,0},{1,17},{17,1},{2,18},{18,2},{3,19},{19,3},{4,20},{20... | collective-permute-start | bytes 2555912 | tf_op jit(solution)/shard_map/ppermute | solution.py:30
  74.5 2.6 %fusion.2 = bf16[256,832]{0,1:T(8,128)(2,1)} fusion(f32[256,832]{0,1:T(8,128)} %collective-permute-done.2, bf16[832,512]{1,0:T(8,128)(2,1)} %param.9, bf16[2,2,256,512]{3,2,1,0:T(8,128)(2,1)S(1)} %bitcast.71, s32[]{:T(128)S(6)} %add.57, s32[]{:T(128)S(6)} %select_n.10), kind=kOutput, calls=%fused_computation.10 | convolution fusion | flops 218529792 | bytes 2392072 | tf_op jit(solution)/shard_map/dot_general | solution.py:20
  77.1 1.2 copy.16
  78.3 2.3 %fusion.1 = bf16[256,832]{0,1:T(8,128)(2,1)} fusion(f32[256,832]{0,1:T(8,128)} %collective-permute-done.1, bf16[512,832]{0,1:T(8,128)(2,1)S(1)} %copy-done, bf16[2,2,256,512]{3,2,1,0:T(8,128)(2,1)S(1)} %bitcast.72, s32[]{:T(128)S(6)} %select_n.10), kind=kOutput, calls=%fused_computation.9 | convolution fusion | flops 218529792 | bytes 2392068 | tf_op jit(solution)/shard_map/dot_general | solution.py:53
  80.7 2.0 %copy.15 = bf16[256,832]{1,0:T(8,128)(2,1)} copy(bf16[256,832]{0,1:T(8,128)(2,1)} %fusion.1) | data formatting | bytes 851968 | tf_op jit(solution)/shard_map/convert_element_type | solution.py:58
  82.7 2.3 %fusion = bf16[256,832]{0,1:T(8,128)(2,1)} fusion(f32[256,832]{0,1:T(8,128)} %collective-permute-done, bf16[512,832]{0,1:T(8,128)(2,1)S(1)} %copy-done.1, bf16[2,2,256,512]{3,2,1,0:T(8,128)(2,1)S(1)} %bitcast.73, s32[]{:T(128)S(6)} %select_n.10), kind=kOutput, calls=%fused_computation.8 | convolution fusion | flops 218529792 | bytes 2392068 | tf_op jit(solution)/shard_map/dot_general | solution.py:52
  85.0 1.2 copy.14
  86.3 1.2 pad_maximum_fusion
  87.6 27.9 %all_to_all.26 = bf16[16,3,16,832]{3,2,1,0:T(8,128)(2,1)S(1)} all-to-all(bf16[16,3,16,832]{3,2,1,0:T(8,128)(2,1)S(1)} %copy.17), channel_id=1, replica_groups=mesh['x'=4,'y'=4,'core'=2,'z_hi'=4,'z_lo'=4] {'x','y'}, dimensions={0} | all-to-all | bytes 2555904 | tf_op jit(solution)/shard_map/all_to_all | solution.py:61
  115.9 23.4 %all_to_all.27 = bf16[16,3,16,832]{3,2,1,0:T(8,128)(2,1)S(1)} all-to-all(bf16[16,3,16,832]{3,2,1,0:T(8,128)(2,1)S(1)} %broadcast_in_dim.22), channel_id=1, replica_groups=mesh['x'=4,'y'=4,'core'=2,'z_hi'=4,'z_lo'=4] {'x','y'}, dimensions={0} | all-to-all | bytes 2555904 | tf_op jit(solution)/shard_map/all_to_all | solution.py:26
  139.3 1.2 copy.18
  140.5 2.5 %copy.19 = bf16[3,256,832]{1,2,0:T(8,128)(2,1)} copy(bf16[3,256,832]{2,1,0:T(8,128)(2,1)} %bitcast.82) | data formatting | bytes 2555904 | tf_op jit(solution)/shard_map/reshape | solution.py:65
  143.0 2.0 %collective-permute-start.3 = (bf16[3,256,832]{1,2,0:T(8,128)(2,1)}, bf16[3,256,832]{1,2,0:T(8,128)(2,1)S(1)}, u32[]{:S(2)}, u32[]{:S(2)}) collective-permute-start(bf16[3,256,832]{1,2,0:T(8,128)(2,1)} %copy.19), channel_id=1, source_target_pairs={{0,16},{16,0},{1,17},{17,1},{2,18},{18,2},{3,19},{19,3},{4,20},{20... | collective-permute-start | bytes 3833864 | tf_op jit(solution)/shard_map/ppermute | solution.py:30
  145.1 0.9 fusion.29
  146.4 0.8 broadcast_in_dim.19
  147.2 1.2 fusion.8
  148.9 1.2 fusion.6
  150.1 7.7 %all-to-all-start.4 = ((bf16[16,32,512]{2,1,0:T(8,128)(2,1)}), bf16[16,32,512]{2,1,0:T(8,128)(2,1)S(1)}, u32[]{:S(2)}, u32[]{:S(2)}) async-start(bf16[16,32,512]{2,1,0:T(8,128)(2,1)} %bitcast.20), calls=%async_computation.4 | async-start | bytes 1048576 | tf_op jit(solution)/shard_map/all_to_all | solution.py:76
  160.6 1.3 add_convert_fusion.2
  161.9 1.3 add_convert_fusion.1
  163.1 1.3 add_convert_fusion
  164.4 25.2 %all-to-all-done.4 = bf16[16,32,512]{2,1,0:T(8,128)(2,1)S(1)} async-done(((bf16[16,32,512]{2,1,0:T(8,128)(2,1)}), bf16[16,32,512]{2,1,0:T(8,128)(2,1)S(1)}, u32[]{:S(2)}, u32[]{:S(2)}) %all-to-all-start.4) | async-done | bytes 524320 | tf_op jit(solution)/shard_map/all_to_all | solution.py:76
  (38 shorter events, 5.0 us)
Async XLA Ops:
  0.6 66.9 %copy-start = (bf16[512,832]{0,1:T(8,128)(2,1)S(1)}, bf16[512,832]{0,1:T(8,128)(2,1)}, u32[]{:S(2)}) copy-start(bf16[512,832]{0,1:T(8,128)(2,1)} %param.8) | copy-start | bytes 2555908
  37.1 25.8 %all-to-all-start.1 = ((bf16[4,4,2,32,512]{4,3,1,2,0:T(8,128)(2,1)}), bf16[4,4,2,32,512]{4,3,1,2,0:T(8,128)(2,1)S(1)}, u32[]{:S(2)}, u32[]{:S(2)}) async-start(bf16[4,4,2,32,512]{4,3,1,2,0:T(8,128)(2,1)} %broadcast_in_dim.21), calls=%async_computation.1 | async-start | bytes 2097152 | tf_op jit(solution)/shard_map/all_to_all | solution.py:26
  65.4 5.8 %copy-start.1 = (bf16[512,832]{0,1:T(8,128)(2,1)S(1)}, bf16[512,832]{0,1:T(8,128)(2,1)}, u32[]{:S(2)}) copy-start(bf16[512,832]{0,1:T(8,128)(2,1)} %param.7) | copy-start | bytes 2555908
  65.4 9.1 %collective-permute-start.2 = (f32[256,832]{0,1:T(8,128)}, f32[256,832]{0,1:T(8,128)}, u32[]{:S(2)}, u32[]{:S(2)}) collective-permute-start(f32[256,832]{0,1:T(8,128)} %fusion.11), channel_id=1, source_target_pairs={{0,16},{16,0},{1,17},{17,1},{2,18},{18,2},{3,19},{19,3},{4,20},{20... | collective-permute-start | bytes 2555912 | tf_op jit(solution)/shard_map/ppermute | solution.py:30
  68.8 9.5 %collective-permute-start.1 = (f32[256,832]{0,1:T(8,128)}, f32[256,832]{0,1:T(8,128)}, u32[]{:S(2)}, u32[]{:S(2)}) collective-permute-start(f32[256,832]{0,1:T(8,128)} %fusion.14), channel_id=1, source_target_pairs={{0,16},{16,0},{1,17},{17,1},{2,18},{18,2},{3,19},{19,3},{4,20},{20... | collective-permute-start | bytes 2555912 | tf_op jit(solution)/shard_map/ppermute | solution.py:30
  72.5 10.1 %collective-permute-start = (f32[256,832]{0,1:T(8,128)}, f32[256,832]{0,1:T(8,128)}, u32[]{:S(2)}, u32[]{:S(2)}) collective-permute-start(f32[256,832]{0,1:T(8,128)} %fusion.15), channel_id=1, source_target_pairs={{0,16},{16,0},{1,17},{17,1},{2,18},{18,2},{3,19},{19,3},{4,20},{20... | collective-permute-start | bytes 2555912 | tf_op jit(solution)/shard_map/ppermute | solution.py:30
  143.0 2.9 %copy-start.2 = (bf16[512,832]{0,1:T(8,128)(2,1)S(1)}, bf16[512,832]{0,1:T(8,128)(2,1)}, u32[]{:S(2)}) copy-start(bf16[512,832]{0,1:T(8,128)(2,1)} %param.7) | copy-start | bytes 2555908
  143.0 5.4 %collective-permute-start.3 = (bf16[3,256,832]{1,2,0:T(8,128)(2,1)}, bf16[3,256,832]{1,2,0:T(8,128)(2,1)S(1)}, u32[]{:S(2)}, u32[]{:S(2)}) collective-permute-start(bf16[3,256,832]{1,2,0:T(8,128)(2,1)} %copy.19), channel_id=1, source_target_pairs={{0,16},{16,0},{1,17},{17,1},{2,18},{18,2},{3,19},{19,3},{4,20},{20... | collective-permute-start | bytes 3833864 | tf_op jit(solution)/shard_map/ppermute | solution.py:30
  145.9 2.5 %copy-start.3 = (bf16[1,16,16,832]{3,2,0,1:T(8,128)(2,1)}, bf16[1,16,16,832]{3,2,0,1:T(8,128)(2,1)S(1)}, u32[]{:S(2)}) copy-start(bf16[1,16,16,832]{3,2,0,1:T(8,128)(2,1)S(1)} %get-tuple-element.5) | copy-start | bytes 1277956
  145.9 2.5 %copy-start.5 = (bf16[1,16,16,832]{3,2,0,1:T(8,128)(2,1)}, bf16[1,16,16,832]{3,2,0,1:T(8,128)(2,1)S(1)}, u32[]{:S(2)}) copy-start(bf16[1,16,16,832]{3,2,0,1:T(8,128)(2,1)S(1)} %get-tuple-element.6) | copy-start | bytes 1277956
  148.4 1.7 copy-start.8
  148.9 8.9 %copy-start.6 = (bf16[1,16,16,832]{3,2,0,1:T(8,128)(2,1)S(1)}, bf16[1,16,16,832]{3,2,0,1:T(8,128)(2,1)}, u32[]{:S(2)}) copy-start(bf16[1,16,16,832]{3,2,0,1:T(8,128)(2,1)} %copy-done.5) | copy-start | bytes 1277956
  150.1 39.5 %all-to-all-start.4 = ((bf16[16,32,512]{2,1,0:T(8,128)(2,1)}), bf16[16,32,512]{2,1,0:T(8,128)(2,1)S(1)}, u32[]{:S(2)}, u32[]{:S(2)}) async-start(bf16[16,32,512]{2,1,0:T(8,128)(2,1)} %bitcast.20), calls=%async_computation.4 | async-start | bytes 1048576 | tf_op jit(solution)/shard_map/all_to_all | solution.py:76
  157.8 1.0 copy-start.4
  158.8 1.0 copy-start.7
  159.2 1.3 copy-start.9

commit v2 on v0

v2 whole, which is shorter than its diff:
```python
import functools

import jax
import jax.numpy as jnp
from jax import lax
from jax.experimental import pallas as pl
from jax.experimental.pallas import tpu as pltpu
from jax.sharding import Mesh, PartitionSpec as P

BF16, F32 = jnp.bfloat16, jnp.float32
XY = ("x", "y")
FAR = 4
OFFSETS = (0, 1, -1, 2)
VMEM = pl.BlockSpec(memory_space=pltpu.VMEM)
SMEM = pl.BlockSpec(memory_space=pltpu.SMEM)


def nonlinear(gate, up, hidden_grad):
    sig = jax.nn.sigmoid(gate)
    silu = gate * sig
    hidden = (silu * up).astype(BF16)
    gate_delta = (hidden_grad * up * sig * (1.0 + gate * (1.0 - sig))).astype(BF16)
    up_delta = (hidden_grad * silu).astype(BF16)
    return (hidden, gate_delta, up_delta)


def contract(left, right, left_dim, right_dim):
    return lax.dot_general(
        left, right, (((left_dim,), (right_dim,)), ((), ())), preferred_element_type=F32
    )


def call(body, outs, flops, *args):
    moved = sum(a.size * a.dtype.itemsize for a in (*args, *jax.tree.leaves(outs)))
    return pl.pallas_call(
        body,
        out_shape=outs,
        in_specs=[SMEM if a.dtype == jnp.int32 else VMEM for a in args],
        out_specs=jax.tree.map(lambda _: VMEM, outs),
        compiler_params=pltpu.CompilerParams(vmem_limit_bytes=28 * 2**20),
        cost_estimate=pl.CostEstimate(flops=flops, bytes_accessed=moved, transcendentals=0),
    )(*args)


def half_rows(which, kind, near, second_low, second_high):
    rows = []
    for far in range(2):
        rows += [ref[2 * which + far, kind] for ref in near]
        rows.append(jnp.where(which == 0, second_low[far, kind], second_high[far, kind]))
    return jnp.concatenate(rows, 0)


def send_body(kind, where, a, b, c, d, e, weight, out):
    rows = half_rows(1 - where[0], kind, (a, b, c), d, e)
    out[...] = contract(rows, weight[...], 1, 1).reshape(out.shape)


def keep_body(where, a, b, c, d, e, pair, down, got_pair, got_down, out):
    blocks, rows, _ = out.shape
    wide = pair.shape[0]
    for kind, weight, got, lanes in (
        (0, pair, got_pair, slice(0, wide)),
        (1, down, got_down, slice(wide, None)),
    ):
        mine = half_rows(where[0], kind, (a, b, c), d, e)
        total = contract(mine, weight[...], 1, 1).reshape(blocks, rows, -1)
        out[:, :, lanes] = (total + got[...]).astype(BF16)


def middle_body(parts, out):
    units = parts.shape[2] // 3
    total = parts[0].astype(F32)
    for i in range(1, parts.shape[0]):
        total += parts[i].astype(F32)
    hid, gate_delta, up_delta = nonlinear(
        total[:, :units], total[:, units : 2 * units], total[:, 2 * units :]
    )
    row = jnp.concatenate([gate_delta, up_delta, hid], 1)
    out[...] = jnp.broadcast_to(row[None], out.shape)


def own_body(deltas, pair, out):
    out[...] = contract(deltas[:, : pair.shape[0]], pair[...], 1, 0).astype(BF16)


def other_body(where, deltas, pair, own, out):
    other = contract(deltas[:, : pair.shape[0]], pair[...], 1, 0).astype(BF16)
    tokens = out.shape[2]
    mine = own[...]
    for far in range(2):
        for k, offset in enumerate(OFFSETS):
            start = (far * FAR + k) * tokens
            group = lax.rem(where[1] + FAR + offset, FAR)
            out[2 * where[0] + far, group] = mine[start : start + tokens]
            out[2 * (1 - where[0]) + far, group] = other[start : start + tokens]


def swap_cores(value):
    return lax.ppermute(value, "core", [(0, 1), (1, 0)])


def shift(value, by):
    return lax.ppermute(value, "col", [((i + by) % 16, i) for i in range(16)])


def per_device(inputs, out_grad, gate_weight, up_weight, down_weight):
    tokens, width = inputs.shape
    units = gate_weight.shape[1]
    n = 16
    half = n * tokens // 2
    core, col = lax.axis_index("core"), lax.axis_index("col")
    where = jnp.stack([core, lax.rem(col, FAR)]).astype(jnp.int32)
    pair = jnp.concatenate([gate_weight.T, up_weight.T], 0)

    both = jnp.stack([inputs, out_grad])
    apart = [[r + FAR * i for i in range(FAR)] for r in range(FAR)]
    first = lax.all_to_all(
        jnp.broadcast_to(both, (FAR, *both.shape)), "col", 0, 0, axis_index_groups=apart
    )
    after, before = shift(first, 1), shift(first, -1)
    low, high = shift(first[:2], 2), shift(first[2:], -2)
    held = (first, after, before, low, high)

    flops = 2 * half * units * width
    sds = jax.ShapeDtypeStruct
    sent = [
        swap_cores(
            call(
                functools.partial(send_body, kind),
                sds((n, half // n, weight.shape[0]), F32),
                flops * (2 - kind),
                where,
                *held,
                weight,
            )
        )
        for kind, weight in ((0, pair), (1, down_weight))
    ]
    parts = call(
        keep_body, sds((n, half // n, 3 * units), BF16), 3 * flops, where, *held, pair, down_weight, *sent
    )
    parts = lax.all_to_all(parts, XY, 0, 0)
    row = call(middle_body, sds(parts.shape, BF16), 40 * half // n * units, parts)
    row = lax.all_to_all(row, XY, 0, 0).reshape(half, 3 * units)
    other = swap_cores(row)
    own_part = call(own_body, sds((half, width), BF16), 2 * flops, row, pair)
    pieces = call(
        other_body, sds((FAR, FAR, tokens, width), BF16), 2 * flops, where, other, pair, own_part
    )
    pieces = lax.all_to_all(pieces.reshape(n, tokens, width), "col", 0, 0)
    input_grad = jnp.sum(pieces.astype(F32), axis=0).astype(BF16)

    def ordered(kind):
        last = jnp.concatenate([low, high], 0)
        groups = [g[:, kind] for g in (first, after, before, last)]
        return jnp.stack(groups, axis=1).reshape(2 * half, width)

    def grad(lanes, value):
        total = contract(row[:, lanes], lax.dynamic_slice_in_dim(value, core * half, half, 0), 0, 0)
        others = lax.dynamic_slice_in_dim(value, (1 - core) * half, half, 0)
        rest = contract(other[:, lanes], others, 0, 0)
        return (total + rest).astype(BF16)

    pair_grad = grad(slice(0, 2 * units), ordered(0))
    down_grad = grad(slice(2 * units, None), ordered(1))
    return (input_grad, pair_grad[:units].T, pair_grad[units:].T, down_grad)


def solution(mesh):
    grid = Mesh(mesh.devices.reshape(4, 4, 2, 16), ("x", "y", "core", "col"))
    row = ("x", "y", "core")
    return jax.shard_map(
        per_device,
        mesh=grid,
        in_specs=(P("col", row), P("col", row), P(row, "col"), P(row, "col"), P("col", row)),
        out_specs=(P("col", row), P(row, "col"), P(row, "col"), P("col", row)),
        check_vma=False,
    )
```

time: 309 us -> 166 us (0.54)
  the two profiles are of different devices: /device:TPU:8 before, /device:TPU:32 now
where the time goes in v2:
time: 166 us
  blocking collectives  85 us (51%)
  waiting for transfers between devices  28.2 us (17%)
  starting transfers between devices  25.9 us (16%)
  local copies, waits for them, and re-layouts  11.7 us (7%)
  Pallas kernels  5.78 us (3%)
  matrix products  5.1 us (3%)
  other arithmetic  3.03 us (2%)
    all_to_all x1, blocking collectives, per_device(): lax.all_to_all(jnp.broadcast_to(both, (FAR, *both.shape)), 'col', 0, 0, a...  35.3 us
    all_to_all x1, blocking collectives, per_device(): parts = lax.all_to_all(parts, XY, 0, 0)  27.1 us
    all_to_all x1, waiting for transfers between devices, per_device(): pieces = lax.all_to_all(pieces.reshape(n, tokens, width), 'col', 0, 0)  23.2 us
    all_to_all x1, blocking collectives, per_device(): row = lax.all_to_all(row, XY, 0, 0).reshape(half, 3 * units)  22.6 us
    ppermute x4, starting transfers between devices, shift(): return lax.ppermute(value, 'col', [((i + by) % 16, i) for i in range(16)])  13.8 us
    ppermute x3, starting transfers between devices, swap_cores(): return lax.ppermute(value, 'core', [(0, 1), (1, 0)])  6.23 us
    all_to_all x1, starting transfers between devices, per_device(): pieces = lax.all_to_all(pieces.reshape(n, tokens, width), 'col', 0, 0)  5.89 us
    pallas_call x6, Pallas kernels, call(): pl.pallas_call(body, out_shape=outs, in_specs=[SMEM if a.dtype == jnp.int...  5.78 us
  transfers between devices with their start and end apart: 8, of which 4 were waited for; matrix products, arithmetic and copies ran while one was open for 7% of the time, Pallas kernels for 1%

profile of v2, /device:TPU:32, one launch (start us, length us, event | category | flops | bytes accessed | tf_op | source)
XLA Modules:
  0.0 165.6 jit_solution(12419061089868430300)
XLA Ops:
  0.6 0.9 pad_maximum_fusion.3
  1.5 35.3 %all_to_all.20.a = bf16[4,2,32,512]{3,2,1,0:T(8,128)(2,1)S(1)} all-to-all(bf16[4,2,32,512]{3,2,1,0:T(8,128)(2,1)S(1)} %broadcast_in_dim.3), channel_id=1, replica_groups={{0,4,8,12},{1,5,9,13},{2,6,10,14},{3,7,11,15},{16,20,24,28},{17,21,25,2..., dimensions={0} | all-to-all | bytes 524288 | tf_op jit(solution)/shard_map/all_to_all | solution.py:117
  36.8 1.9 %collective-permute-start.3 = (bf16[2,2,32,512]{3,2,1,0:T(8,128)(2,1)S(1)}, bf16[2,2,32,512]{3,2,1,0:T(8,128)(2,1)S(1)}, u32[]{:S(2)}, u32[]{:S(2)}) collective-permute-start(bf16[2,2,32,512]{3,2,1,0:T(8,128)(2,1)S(1)} %get-tuple-element.14), channel_id=1, source_target_pairs={{14,0},{15,1},{0,2},{1,3},{2,4},{3,5},{4,6},{5,7},{6,8},{7,9},{8,1... | collective-permute-start | bytes 393224 | tf_op jit(solution)/shard_map/ppermute | solution.py:103
  38.7 6.0 %collective-permute-start.2 = (bf16[2,2,32,512]{3,2,1,0:T(8,128)(2,1)S(1)}, bf16[2,2,32,512]{3,2,1,0:T(8,128)(2,1)S(1)}, u32[]{:S(2)}, u32[]{:S(2)}) collective-permute-start(bf16[2,2,32,512]{3,2,1,0:T(8,128)(2,1)S(1)} %get-tuple-element.15), channel_id=1, source_target_pairs={{2,0},{3,1},{4,2},{5,3},{6,4},{7,5},{8,6},{9,7},{10,8},{11,9},{12,... | collective-permute-start | bytes 393224 | tf_op jit(solution)/shard_map/ppermute | solution.py:103
  44.8 1.9 %collective-permute-start.1 = (bf16[4,2,32,512]{3,2,1,0:T(8,128)(2,1)S(1)}, bf16[4,2,32,512]{3,2,1,0:T(8,128)(2,1)S(1)}, u32[]{:S(2)}, u32[]{:S(2)}) collective-permute-start(bf16[4,2,32,512]{3,2,1,0:T(8,128)(2,1)S(1)} %all_to_all.20.a), channel_id=1, source_target_pairs={{15,0},{0,1},{1,2},{2,3},{3,4},{4,5},{5,6},{6,7},{7,8},{8,9},{9,10... | collective-permute-start | bytes 786440 | tf_op jit(solution)/shard_map/ppermute | solution.py:103
  46.7 3.9 %collective-permute-start = (bf16[4,2,32,512]{3,2,1,0:T(8,128)(2,1)S(1)}, bf16[4,2,32,512]{3,2,1,0:T(8,128)(2,1)S(1)}, u32[]{:S(2)}, u32[]{:S(2)}) collective-permute-start(bf16[4,2,32,512]{3,2,1,0:T(8,128)(2,1)S(1)} %all_to_all.20.a), channel_id=1, source_target_pairs={{1,0},{2,1},{3,2},{4,3},{5,4},{6,5},{7,6},{8,7},{9,8},{10,9},{11,1... | collective-permute-start | bytes 786440 | tf_op jit(solution)/shard_map/ppermute | solution.py:103
  50.6 1.3 pad_maximum_fusion.weight.pair
  52.0 1.0 collective-permute-done.1.c
  53.0 1.9 %collective-permute-done.b = bf16[4,2,32,512]{3,2,1,0:T(8,128)(2,1)S(1)} collective-permute-done((bf16[4,2,32,512]{3,2,1,0:T(8,128)(2,1)S(1)}, bf16[4,2,32,512]{3,2,1,0:T(8,128)(2,1)S(1)}, u32[]{:S(2)}, u32[]{:S(2)}) %collective-permute-start) | collective-permute-done | bytes 262176 | tf_op jit(solution)/shard_map/ppermute | solution.py:103
  55.0 1.2 shard_map.84
  56.2 1.9 %collective-permute-start.4 = (f32[16,16,1664]{2,1,0:T(8,128)S(1)}, f32[16,16,1664]{2,1,0:T(8,128)S(1)}, u32[]{:S(2)}, u32[]{:S(2)}) collective-permute-start(f32[16,16,1664]{2,1,0:T(8,128)S(1)} %shard_map.84), channel_id=1, source_target_pairs={{0,16},{16,0},{1,17},{17,1},{2,18},{18,2},{3,19},{19,3},{4,20},{20... | collective-permute-start | bytes 5111816 | tf_op jit(solution)/shard_map/ppermute | solution.py:99
  58.1 1.0 shard_map.85
  59.2 2.4 %collective-permute-start.5 = (f32[16,16,832]{2,1,0:T(8,128)S(1)}, f32[16,16,832]{2,1,0:T(8,128)S(1)}, u32[]{:S(2)}, u32[]{:S(2)}) collective-permute-start(f32[16,16,832]{2,1,0:T(8,128)S(1)} %shard_map.85), channel_id=1, source_target_pairs={{0,16},{16,0},{1,17},{17,1},{2,18},{18,2},{3,19},{19,3},{4,20},{20... | collective-permute-start | bytes 2555912 | tf_op jit(solution)/shard_map/ppermute | solution.py:99
  61.6 2.1 %collective-permute-done.5.got_down = f32[16,16,832]{2,1,0:T(8,128)S(1)} collective-permute-done((f32[16,16,832]{2,1,0:T(8,128)S(1)}, f32[16,16,832]{2,1,0:T(8,128)S(1)}, u32[]{:S(2)}, u32[]{:S(2)}) %collective-permute-start.5) | collective-permute-done | bytes 852000 | tf_op jit(solution)/shard_map/ppermute | solution.py:99
  63.7 0.9 copy-done.2
  64.6 1.5 shard_map.86
  66.1 27.1 %all_to_all.21.parts = bf16[16,16,2496]{2,1,0:T(8,128)(2,1)S(1)} all-to-all(bf16[16,16,2496]{2,1,0:T(8,128)(2,1)S(1)} %shard_map.86), channel_id=1, replica_groups=mesh['x'=4,'y'=4,'core'=2,'col'=16] {'x','y'}, dimensions={0} | all-to-all | bytes 2555904 | tf_op jit(solution)/shard_map/all_to_all | solution.py:142
  93.5 22.6 %all_to_all.22 = bf16[16,16,2496]{2,1,0:T(8,128)(2,1)S(1)} all-to-all(bf16[16,16,2496]{2,1,0:T(8,128)(2,1)S(1)} %shard_map.87), channel_id=1, replica_groups=mesh['x'=4,'y'=4,'core'=2,'col'=16] {'x','y'}, dimensions={0} | all-to-all | bytes 2555904 | tf_op jit(solution)/shard_map/all_to_all | solution.py:144
  116.1 1.5 copy.9
  117.6 1.9 %collective-permute-start.6 = (bf16[256,2496]{0,1:T(8,128)(2,1)}, bf16[256,2496]{0,1:T(8,128)(2,1)}, u32[]{:S(2)}, u32[]{:S(2)}) collective-permute-start(bf16[256,2496]{0,1:T(8,128)(2,1)} %copy.9), channel_id=1, source_target_pairs={{0,16},{16,0},{1,17},{17,1},{2,18},{18,2},{3,19},{19,3},{4,20},{20... | collective-permute-start | bytes 3833864 | tf_op jit(solution)/shard_map/ppermute | solution.py:99
  119.5 0.7 fusion.14
  120.2 0.9 constant_dynamic-update-slice_fusion.1
  121.1 0.9 constant_dynamic-update-slice_fusion
  123.4 2.5 %copy.10.deltas = bf16[256,2496]{1,0:T(8,128)(2,1)} copy(bf16[256,2496]{0,1:T(8,128)(2,1)} %collective-permute-done.6) | data formatting | bytes 2555904 | tf_op jit(solution)/shard_map/ppermute | solution.py:99
  125.9 1.3 copy-done
  127.2 1.2 shard_map.89
  128.4 0.8 copy-done.7
  129.2 5.9 %all-to-all-start.3 = ((bf16[16,32,512]{2,1,0:T(8,128)(2,1)}), bf16[16,32,512]{2,1,0:T(8,128)(2,1)S(1)}, u32[]{:S(2)}, u32[]{:S(2)}) async-start(bf16[16,32,512]{2,1,0:T(8,128)(2,1)} %bitcast.18), calls=%async_computation.3 | async-start | bytes 1048576 | tf_op jit(solution)/shard_map/all_to_all | solution.py:150
  136.4 1.8 %add_convert_fusion = bf16[1664,512]{1,0:T(8,128)(2,1)S(1)} fusion(f32[1664,512]{1,0:T(8,128)S(1)} %fusion.1, bf16[256,2496]{0,1:T(8,128)(2,1)} %collective-permute-done.6, bf16[512,512]{1,0:T(8,128)(2,1)S(1)} %bitcast.20, s32[]{:T(128)S(6)} %select_n.9), kind=kOutput, calls=%fused_computation | convolution fusion | flops 437911552 | bytes 6225924 | tf_op jit(solution)/shard_map/dot_general | solution.py:28
  138.2 1.3 slice_bitcast_fusion
  139.4 2.3 %add_convert_fusion.1 = bf16[832,512]{1,0:T(8,128)(2,1)} fusion(f32[832,512]{1,0:T(8,128)S(1)} %fusion.3, bf16[256,2496]{0,1:T(8,128)(2,1)} %collective-permute-done.6, bf16[512,512]{1,0:T(8,128)(2,1)S(1)} %bitcast.22, s32[]{:T(128)S(6)} %select_n.9), kind=kOutput, calls=%fused_computation.2 | convolution fusion | flops 218955776 | bytes 3244036 | tf_op jit(solution)/shard_map/dot_general | solution.py:28
  141.7 23.2 %all-to-all-done.3 = bf16[16,32,512]{2,1,0:T(8,128)(2,1)S(1)} async-done(((bf16[16,32,512]{2,1,0:T(8,128)(2,1)}), bf16[16,32,512]{2,1,0:T(8,128)(2,1)S(1)}, u32[]{:S(2)}, u32[]{:S(2)}) %all-to-all-start.3) | async-done | bytes 524320 | tf_op jit(solution)/shard_map/all_to_all | solution.py:150
  (39 shorter events, 3.7 us)
Async XLA Ops:
  0.6 50.0 %copy-start.8 = (bf16[512,832]{0,1:T(8,128)(2,1)S(1)}, bf16[512,832]{0,1:T(8,128)(2,1)}, u32[]{:S(2)}) copy-start(bf16[512,832]{0,1:T(8,128)(2,1)} %param.8) | copy-start | bytes 2555908
  36.8 15.2 %collective-permute-start.3 = (bf16[2,2,32,512]{3,2,1,0:T(8,128)(2,1)S(1)}, bf16[2,2,32,512]{3,2,1,0:T(8,128)(2,1)S(1)}, u32[]{:S(2)}, u32[]{:S(2)}) collective-permute-start(bf16[2,2,32,512]{3,2,1,0:T(8,128)(2,1)S(1)} %get-tuple-element.14), channel_id=1, source_target_pairs={{14,0},{15,1},{0,2},{1,3},{2,4},{3,5},{4,6},{5,7},{6,8},{7,9},{8,1... | collective-permute-start | bytes 393224 | tf_op jit(solution)/shard_map/ppermute | solution.py:103
  38.7 13.3 %collective-permute-start.2 = (bf16[2,2,32,512]{3,2,1,0:T(8,128)(2,1)S(1)}, bf16[2,2,32,512]{3,2,1,0:T(8,128)(2,1)S(1)}, u32[]{:S(2)}, u32[]{:S(2)}) collective-permute-start(bf16[2,2,32,512]{3,2,1,0:T(8,128)(2,1)S(1)} %get-tuple-element.15), channel_id=1, source_target_pairs={{2,0},{3,1},{4,2},{5,3},{6,4},{7,5},{8,6},{9,7},{10,8},{11,9},{12,... | collective-permute-start | bytes 393224 | tf_op jit(solution)/shard_map/ppermute | solution.py:103
  44.8 8.3 %collective-permute-start.1 = (bf16[4,2,32,512]{3,2,1,0:T(8,128)(2,1)S(1)}, bf16[4,2,32,512]{3,2,1,0:T(8,128)(2,1)S(1)}, u32[]{:S(2)}, u32[]{:S(2)}) collective-permute-start(bf16[4,2,32,512]{3,2,1,0:T(8,128)(2,1)S(1)} %all_to_all.20.a), channel_id=1, source_target_pairs={{15,0},{0,1},{1,2},{2,3},{3,4},{4,5},{5,6},{6,7},{7,8},{8,9},{9,10... | collective-permute-start | bytes 786440 | tf_op jit(solution)/shard_map/ppermute | solution.py:103
  46.7 8.3 %collective-permute-start = (bf16[4,2,32,512]{3,2,1,0:T(8,128)(2,1)S(1)}, bf16[4,2,32,512]{3,2,1,0:T(8,128)(2,1)S(1)}, u32[]{:S(2)}, u32[]{:S(2)}) collective-permute-start(bf16[4,2,32,512]{3,2,1,0:T(8,128)(2,1)S(1)} %all_to_all.20.a), channel_id=1, source_target_pairs={{1,0},{2,1},{3,2},{4,3},{5,4},{6,5},{7,6},{8,7},{9,8},{10,9},{11,1... | collective-permute-start | bytes 786440 | tf_op jit(solution)/shard_map/ppermute | solution.py:103
  52.0 6.1 %copy-start.4 = (bf16[832,512]{1,0:T(8,128)(2,1)S(1)}, bf16[832,512]{1,0:T(8,128)(2,1)}, u32[]{:S(2)}) copy-start(bf16[832,512]{1,0:T(8,128)(2,1)} %down.1) | copy-start | bytes 2555908
  52.0 11.6 %copy-start.5 = (bf16[2,2,32,512]{3,2,1,0:T(8,128)(2,1)}, bf16[2,2,32,512]{3,2,1,0:T(8,128)(2,1)S(1)}, u32[]{:S(2)}) copy-start(bf16[2,2,32,512]{3,2,1,0:T(8,128)(2,1)S(1)} %collective-permute-done.3.e) | copy-start | bytes 393220
  52.0 11.6 %copy-start.6 = (bf16[2,2,32,512]{3,2,1,0:T(8,128)(2,1)}, bf16[2,2,32,512]{3,2,1,0:T(8,128)(2,1)S(1)}, u32[]{:S(2)}) copy-start(bf16[2,2,32,512]{3,2,1,0:T(8,128)(2,1)S(1)} %collective-permute-done.2.d) | copy-start | bytes 393220
  55.0 3.1 %copy-start.1 = (bf16[4,2,32,512]{3,2,1,0:T(8,128)(2,1)}, bf16[4,2,32,512]{3,2,1,0:T(8,128)(2,1)S(1)}, u32[]{:S(2)}) copy-start(bf16[4,2,32,512]{3,2,1,0:T(8,128)(2,1)S(1)} %collective-permute-done.b) | copy-start | bytes 786436
  56.2 7.4 %collective-permute-start.4 = (f32[16,16,1664]{2,1,0:T(8,128)S(1)}, f32[16,16,1664]{2,1,0:T(8,128)S(1)}, u32[]{:S(2)}, u32[]{:S(2)}) collective-permute-start(f32[16,16,1664]{2,1,0:T(8,128)S(1)} %shard_map.84), channel_id=1, source_target_pairs={{0,16},{16,0},{1,17},{17,1},{2,18},{18,2},{3,19},{19,3},{4,20},{20... | collective-permute-start | bytes 5111816 | tf_op jit(solution)/shard_map/ppermute | solution.py:99
  59.2 4.5 %collective-permute-start.5 = (f32[16,16,832]{2,1,0:T(8,128)S(1)}, f32[16,16,832]{2,1,0:T(8,128)S(1)}, u32[]{:S(2)}, u32[]{:S(2)}) collective-permute-start(f32[16,16,832]{2,1,0:T(8,128)S(1)} %shard_map.85), channel_id=1, source_target_pairs={{0,16},{16,0},{1,17},{17,1},{2,18},{18,2},{3,19},{19,3},{4,20},{20... | collective-permute-start | bytes 2555912 | tf_op jit(solution)/shard_map/ppermute | solution.py:99
  63.6 1.0 copy-start.2
  117.6 5.8 %collective-permute-start.6 = (bf16[256,2496]{0,1:T(8,128)(2,1)}, bf16[256,2496]{0,1:T(8,128)(2,1)}, u32[]{:S(2)}, u32[]{:S(2)}) collective-permute-start(bf16[256,2496]{0,1:T(8,128)(2,1)} %copy.9), channel_id=1, source_target_pairs={{0,16},{16,0},{1,17},{17,1},{2,18},{18,2},{3,19},{19,3},{4,20},{20... | collective-permute-start | bytes 3833864 | tf_op jit(solution)/shard_map/ppermute | solution.py:99
  125.9 1.3 copy-start
  128.4 0.8 copy-start.7
  129.2 5.9 %copy-start.3 = (bf16[4,2,32,512]{3,2,1,0:T(8,128)(2,1)S(1)}, bf16[4,2,32,512]{3,2,1,0:T(8,128)(2,1)}, u32[]{:S(2)}) copy-start(bf16[4,2,32,512]{3,2,1,0:T(8,128)(2,1)} %copy-done.1) | copy-start | bytes 786436
  129.2 6.0 %copy-start.9 = (bf16[4,1,32,512]{3,2,1,0:T(8,128)(2,1)S(1)}, bf16[4,1,32,512]{3,2,1,0:T(8,128)(2,1)}, u32[]{:S(2)}) copy-start(bf16[4,1,32,512]{3,2,1,0:T(8,128)(2,1)} %get-tuple-element.6) | copy-start | bytes 393220
  129.2 6.0 %copy-start.10 = (bf16[4,1,32,512]{3,2,1,0:T(8,128)(2,1)S(1)}, bf16[4,1,32,512]{3,2,1,0:T(8,128)(2,1)}, u32[]{:S(2)}) copy-start(bf16[4,1,32,512]{3,2,1,0:T(8,128)(2,1)} %get-tuple-element.7) | copy-start | bytes 393220
  129.2 6.0 %copy-start.11 = (bf16[4,1,32,512]{3,2,1,0:T(8,128)(2,1)S(1)}, bf16[4,1,32,512]{3,2,1,0:T(8,128)(2,1)}, u32[]{:S(2)}) copy-start(bf16[4,1,32,512]{3,2,1,0:T(8,128)(2,1)} %get-tuple-element.12) | copy-start | bytes 393220
  129.2 6.0 %copy-start.12 = (bf16[4,1,32,512]{3,2,1,0:T(8,128)(2,1)S(1)}, bf16[4,1,32,512]{3,2,1,0:T(8,128)(2,1)}, u32[]{:S(2)}) copy-start(bf16[4,1,32,512]{3,2,1,0:T(8,128)(2,1)} %get-tuple-element.13) | copy-start | bytes 393220
  129.2 35.7 %all-to-all-start.3 = ((bf16[16,32,512]{2,1,0:T(8,128)(2,1)}), bf16[16,32,512]{2,1,0:T(8,128)(2,1)S(1)}, u32[]{:S(2)}, u32[]{:S(2)}) async-start(bf16[16,32,512]{2,1,0:T(8,128)(2,1)} %bitcast.18), calls=%async_computation.3 | async-start | bytes 1048576 | tf_op jit(solution)/shard_map/all_to_all | solution.py:150

commit v3 on v2

v3 whole, which is shorter than its diff:
```python
import jax
import jax.numpy as jnp
from jax import lax
from jax.experimental import pallas as pl
from jax.experimental.pallas import tpu as pltpu
from jax.sharding import Mesh, PartitionSpec as P

BF16, F32 = jnp.bfloat16, jnp.float32
XY = ("x", "y")
VMEM = pl.BlockSpec(memory_space=pltpu.VMEM)
SMEM = pl.BlockSpec(memory_space=pltpu.SMEM)


def nonlinear(gate, up, hidden_grad):
    sig = jax.nn.sigmoid(gate)
    silu = gate * sig
    hidden = (silu * up).astype(BF16)
    gate_delta = (hidden_grad * up * sig * (1.0 + gate * (1.0 - sig))).astype(BF16)
    up_delta = (hidden_grad * silu).astype(BF16)
    return (hidden, gate_delta, up_delta)


def contract(left, right, left_dim, right_dim):
    return lax.dot_general(
        left, right, (((left_dim,), (right_dim,)), ((), ())), preferred_element_type=F32
    )


def call(body, outs, flops, *args):
    moved = sum(a.size * a.dtype.itemsize for a in (*args, *jax.tree.leaves(outs)))
    return pl.pallas_call(
        body,
        out_shape=outs,
        in_specs=[SMEM if a.dtype == jnp.int32 else VMEM for a in args],
        out_specs=jax.tree.map(lambda _: VMEM, outs),
        compiler_params=pltpu.CompilerParams(vmem_limit_bytes=28 * 2**20),
        cost_estimate=pl.CostEstimate(flops=flops, bytes_accessed=moved, transcendentals=0),
    )(*args)


def half_inputs(which, first):
    devices, tokens = first.shape[0] // 2, 32
    return first[pl.ds(which * devices, devices), :tokens].reshape(devices * tokens, -1)


def half_grads(which, first, second):
    devices = first.shape[0] // 2
    span = pl.ds(which * devices, devices)
    rows = jnp.concatenate([first[span, 32:], second[span]], 1)
    return rows.reshape(devices * 32, -1)


def send_x_body(where, first, weight, out, rows_out):
    rows = half_inputs(1 - where[0], first)
    rows_out[...] = rows
    out[...] = contract(rows, weight[...], 1, 1).reshape(out.shape)


def send_g_body(where, first, second, weight, out, rows_out):
    rows = half_grads(1 - where[0], first, second)
    rows_out[...] = rows
    out[...] = contract(rows, weight[...], 1, 1).reshape(out.shape)


def keep_body(where, first, second, pair, down, got_pair, got_down, out, x_out, g_out):
    blocks, rows, _ = out.shape
    wide = pair.shape[0]
    mine = half_inputs(where[0], first)
    x_out[...] = mine
    total = contract(mine, pair[...], 1, 1).reshape(blocks, rows, -1)
    out[:, :, :wide] = (total + got_pair[...]).astype(BF16)
    mine = half_grads(where[0], first, second)
    g_out[...] = mine
    total = contract(mine, down[...], 1, 1).reshape(blocks, rows, -1)
    out[:, :, wide:] = (total + got_down[...]).astype(BF16)


def middle_body(parts, deltas, hidden):
    units = parts.shape[2] // 3
    total = parts[0].astype(F32)
    for i in range(1, parts.shape[0]):
        total += parts[i].astype(F32)
    hid, gate_delta, up_delta = nonlinear(
        total[:, :units], total[:, units : 2 * units], total[:, 2 * units :]
    )
    hidden[...] = hid
    row = jnp.concatenate([gate_delta, up_delta], 1)
    deltas[...] = jnp.broadcast_to(row[None], deltas.shape)


def part_of(deltas, pair):
    lanes = pair.shape[0]
    rows = deltas[...].reshape(-1, deltas.shape[-1])[:, :lanes]
    return contract(rows, pair[...], 1, 0).astype(BF16)


def own_body(deltas, pair, out):
    out[...] = part_of(deltas, pair)


def other_body(where, deltas, pair, own, out):
    out[where[0]] = own[...]
    out[1 - where[0]] = part_of(deltas, pair)


def swap_cores(value):
    return lax.ppermute(value, "core", [(0, 1), (1, 0)])


def per_device(inputs, out_grad, gate_weight, up_weight, down_weight):
    tokens, width = inputs.shape
    units = gate_weight.shape[1]
    n = 16
    half = n * tokens // 2
    core = lax.axis_index("core")
    where = core.astype(jnp.int32).reshape(1)
    pair = jnp.concatenate([gate_weight.T, up_weight.T], 0)

    early = tokens // 2
    second = lax.all_to_all(
        jnp.broadcast_to(out_grad[early:], (n, tokens - early, width)), "col", 0, 0
    )
    first = lax.all_gather(jnp.concatenate([inputs, out_grad[:early]], 0), "col", axis=0)

    flops = 2 * half * units * width
    sds = jax.ShapeDtypeStruct
    rows = sds((half, width), BF16)
    sent_x, x_other = call(
        send_x_body, (sds((n, half // n, 2 * units), F32), rows), 2 * flops, where, first, pair
    )
    got_x = swap_cores(sent_x)
    sent_g, g_other = call(
        send_g_body,
        (sds((n, half // n, units), F32), rows),
        flops,
        where,
        first,
        second,
        down_weight,
    )
    got_g = swap_cores(sent_g)
    parts, x_own, g_own = call(
        keep_body,
        (sds((n, half // n, 3 * units), BF16), rows, rows),
        3 * flops,
        where,
        first,
        second,
        pair,
        down_weight,
        got_x,
        got_g,
    )
    parts = lax.all_to_all(parts, XY, 0, 0)
    own, hidden = call(
        middle_body,
        (sds((n, half // n, 2 * units), BF16), sds((half // n, units), BF16)),
        40 * half // n * units,
        parts,
    )
    own = lax.all_to_all(own, XY, 0, 0)
    other = swap_cores(own)
    own_part = call(own_body, rows, 2 * flops, own, pair)
    pieces = call(
        other_body, sds((2, half, width), BF16), 2 * flops, where, other, pair, own_part
    )
    pieces = lax.all_to_all(pieces.reshape(n, tokens, width), "col", 0, 0)
    input_grad = jnp.sum(pieces.astype(F32), axis=0).astype(BF16)
    pair_grad = contract(own.reshape(half, -1), x_own, 0, 0)
    pair_grad = (pair_grad + contract(other.reshape(half, -1), x_other, 0, 0)).astype(BF16)
    hidden = lax.all_gather(hidden, ("x", "y", "core"), axis=0).reshape(n, 2, half // n, units)
    hidden_own = lax.dynamic_index_in_dim(hidden, core, 1, keepdims=False).reshape(half, units)
    hidden_other = lax.dynamic_index_in_dim(hidden, 1 - core, 1, keepdims=False)
    down_grad = contract(hidden_own, g_own, 0, 0)
    down_grad = down_grad + contract(hidden_other.reshape(half, units), g_other, 0, 0)
    return (input_grad, pair_grad[:units].T, pair_grad[units:].T, down_grad.astype(BF16))
def solution(mesh):
    grid = Mesh(mesh.devices.reshape(4, 4, 2, 16), ("x", "y", "core", "col"))
    row = ("x", "y", "core")
    return jax.shard_map(
        per_device,
        mesh=grid,
        in_specs=(P("col", row), P("col", row), P(row, "col"), P(row, "col"), P("col", row)),
        out_specs=(P("col", row), P(row, "col"), P(row, "col"), P("col", row)),
        check_vma=False,
    )
```

time: 166 us -> 167 us (level)
  the two profiles are of different devices: /device:TPU:32 before, /device:TPU:1 now
where the time goes in v3:
time: 167 us; the launch traced here: 166 us
  blocking collectives  101 us (60%)
  starting transfers between devices  41.4 us (25%)
  Pallas kernels  7.31 us (4%)
  local copies, waits for them, and re-layouts  5.89 us (4%)
  waiting for transfers between devices  3.78 us (2%)
  matrix products  3 us (2%)
  other arithmetic  2.72 us (2%)
    all_gather x1, blocking collectives, per_device(): lax.all_gather(jnp.concatenate([inputs, out_grad[:early]], 0), 'col', axi...  35.7 us
    all_to_all x1, blocking collectives, per_device(): parts = lax.all_to_all(parts, XY, 0, 0)  25.7 us
    all_gather x1, blocking collectives, per_device(): lax.all_gather(hidden, ('x', 'y', 'core'), axis=0)  23.5 us
    all_to_all x1, blocking collectives, per_device(): own = lax.all_to_all(own, XY, 0, 0)  16 us
    all_to_all x1, starting transfers between devices, per_device(): lax.all_to_all(jnp.broadcast_to(out_grad[early:], (n, tokens - early, wid...  15.8 us
    ppermute x3, starting transfers between devices, swap_cores(): return lax.ppermute(value, 'core', [(0, 1), (1, 0)])  15.4 us
    all_to_all x1, starting transfers between devices, per_device(): pieces = lax.all_to_all(pieces.reshape(n, tokens, width), 'col', 0, 0)  10.2 us
    pallas_call x6, Pallas kernels, call(): pl.pallas_call(body, out_shape=outs, in_specs=[SMEM if a.dtype == jnp.int...  7.31 us
  transfers between devices with their start and end apart: 5, of which 2 were waited for; matrix products, arithmetic and copies ran while one was open for 4% of the time, Pallas kernels for 2%

profile of v3, /device:TPU:1, one launch (start us, length us, event | category | flops | bytes accessed | tf_op | source)
XLA Modules:
  0.0 165.8 jit_solution(6333247163711912922)
XLA Ops:
  0.6 0.8 fusion
  1.5 0.7 broadcast_in_dim.3
  2.2 15.8 %all-to-all-start = ((bf16[16,16,512]{2,1,0:T(8,128)(2,1)}), bf16[16,16,512]{2,1,0:T(8,128)(2,1)}, u32[]{:S(2)}, u32[]{:S(2)}) async-start(bf16[16,16,512]{2,1,0:T(8,128)(2,1)} %broadcast_in_dim.3), calls=%async_computation | async-start | bytes 524288 | tf_op jit(solution)/shard_map/all_to_all | solution.py:120
  18.0 0.8 pad_maximum_fusion.1
  18.8 35.7 %all-gather = bf16[768,512]{1,0:T(8,128)(2,1)S(1)} all-gather(bf16[48,512]{1,0:T(8,128)(2,1)S(1)} %pad_maximum_fusion.1), channel_id=2, replica_groups=mesh['x'=4,'y'=4,'core'=2,'col'=16] {'col'}, dimensions={0}, use_global_device_ids=true | all-gather | bytes 835584 | tf_op jit(solution)/shard_map/all_gather | solution.py:123
  54.4 1.3 pad_maximum_fusion.weight.pair
  55.7 1.9 %shard_map.84 = (f32[16,16,1664]{2,1,0:T(8,128)}, bf16[256,512]{1,0:T(8,128)(2,1)S(1)}) custom-call(s32[1]{0:T(128)} %bitcast.where, bf16[16,48,512]{2,1,0:T(8,128)(2,1)S(1)} %bitcast.22, bf16[1664,512]{1,0:T(8,128)(2,1)S(1)} %pad_maximum_fusion.weight.pair), custom_call_target="tpu_custom_call" | custom-call | flops 436207616 | bytes 4456452 | tf_op jit(solution)/shard_map/pallas_call | solution.py:31
  57.6 0.7 copy-done.2
  58.3 8.4 %collective-permute-start = (f32[16,16,1664]{2,1,0:T(8,128)}, f32[16,16,1664]{2,1,0:T(8,128)}, u32[]{:S(2)}, u32[]{:S(2)}) collective-permute-start(f32[16,16,1664]{2,1,0:T(8,128)} %get-tuple-element.13), channel_id=1, source_target_pairs={{0,16},{16,0},{1,17},{17,1},{2,18},{18,2},{3,19},{19,3},{4,20},{20... | collective-permute-start | bytes 5111816 | tf_op jit(solution)/shard_map/ppermute | solution.py:107
  66.8 1.4 shard_map.85
  68.2 0.7 copy-done.4
  68.9 1.9 %collective-permute-start.1 = (f32[16,16,832]{2,1,0:T(8,128)S(1)}, f32[16,16,832]{2,1,0:T(8,128)S(1)}, u32[]{:S(2)}, u32[]{:S(2)}) collective-permute-start(f32[16,16,832]{2,1,0:T(8,128)S(1)} %get-tuple-element.14), channel_id=1, source_target_pairs={{0,16},{16,0},{1,17},{17,1},{2,18},{18,2},{3,19},{19,3},{4,20},{20... | collective-permute-start | bytes 2555912 | tf_op jit(solution)/shard_map/ppermute | solution.py:107
  70.8 2.4 %collective-permute-done.1.got_down = f32[16,16,832]{2,1,0:T(8,128)S(1)} collective-permute-done((f32[16,16,832]{2,1,0:T(8,128)S(1)}, f32[16,16,832]{2,1,0:T(8,128)S(1)}, u32[]{:S(2)}, u32[]{:S(2)}) %collective-permute-start.1) | collective-permute-done | bytes 852000 | tf_op jit(solution)/shard_map/ppermute | solution.py:107
  73.2 2.5 %shard_map.86 = (bf16[16,16,2496]{2,1,0:T(8,128)(2,1)S(1)}, bf16[256,512]{1,0:T(8,128)(2,1)S(1)}, bf16[256,512]{1,0:T(8,128)(2,1)S(1)}) custom-call(s32[1]{0:T(128)} %bitcast.where, bf16[16,48,512]{2,1,0:T(8,128)(2,1)S(1)} %bitcast.24, bf16[16,16,512]{2,1,0:T(8,128)(2,1)} %all-to-all-done.second, bf16[1664,512]{1,0:T(8,128)(2,1)S(1)} %pad_maximum_fusion.weight.pair, ...), custom_call_target="tpu_custom_call" | custom-call | flops 654311424 | bytes 7962628 | tf_op jit(solution)/shard_map/pallas_call | solution.py:31
  75.8 25.7 %all_to_all.20.parts = bf16[16,16,2496]{2,1,0:T(8,128)(2,1)S(1)} all-to-all(bf16[16,16,2496]{2,1,0:T(8,128)(2,1)S(1)} %get-tuple-element.15), channel_id=1, replica_groups=mesh['x'=4,'y'=4,'core'=2,'col'=16] {'x','y'}, dimensions={0} | all-to-all | bytes 2555904 | tf_op jit(solution)/shard_map/all_to_all | solution.py:154
  101.5 0.3 shard_map.87
  101.8 16.0 %all_to_all.21.deltas = bf16[16,16,1664]{2,1,0:T(8,128)(2,1)S(1)} all-to-all(bf16[16,16,1664]{2,1,0:T(8,128)(2,1)S(1)} %get-tuple-element.16), channel_id=1, replica_groups=mesh['x'=4,'y'=4,'core'=2,'col'=16] {'x','y'}, dimensions={0} | all-to-all | bytes 1703936 | tf_op jit(solution)/shard_map/all_to_all | solution.py:161
  117.8 5.0 %collective-permute-start.2 = (bf16[16,16,1664]{2,1,0:T(8,128)(2,1)S(1)}, bf16[16,16,1664]{2,1,0:T(8,128)(2,1)S(1)}, u32[]{:S(2)}, u32[]{:S(2)}) collective-permute-start(bf16[16,16,1664]{2,1,0:T(8,128)(2,1)S(1)} %all_to_all.21.deltas), channel_id=1, source_target_pairs={{0,16},{16,0},{1,17},{17,1},{2,18},{18,2},{3,19},{19,3},{4,20},{20... | collective-permute-start | bytes 2555912 | tf_op jit(solution)/shard_map/ppermute | solution.py:107
  122.8 0.6 shard_map.88.own
  123.5 1.3 collective-permute-done.2.deltas
  124.8 0.6 shard_map.89
  125.5 0.8 copy-done.1
  126.3 10.2 %all-to-all-start.3 = ((bf16[16,32,512]{2,1,0:T(8,128)(2,1)}), bf16[16,32,512]{2,1,0:T(8,128)(2,1)S(1)}, u32[]{:S(2)}, u32[]{:S(2)}) async-start(bf16[16,32,512]{2,1,0:T(8,128)(2,1)} %bitcast.27), calls=%async_computation.3 | async-start | bytes 1048576 | tf_op jit(solution)/shard_map/all_to_all | solution.py:167
  136.5 23.5 %all-gather.1 = bf16[512,832]{1,0:T(8,128)(2,1)S(1)} all-gather(bf16[16,832]{1,0:T(8,128)(2,1)S(1)} %get-tuple-element.19), channel_id=3, replica_groups=mesh['x'=4,'y'=4,'core'=2,'col'=16] {'x','y','core'}, dimensions={0}, use_global_device_ids=true | all-gather | bytes 878592 | tf_op jit(solution)/shard_map/all_gather | solution.py:171
  160.1 0.4 fusion.2
  160.5 0.4 copy-done.9
  160.9 1.3 add_convert_fusion.1
  162.3 0.6 fusion.1
  162.9 0.3 copy-done.7
  163.2 0.6 add_convert_fusion
  163.9 1.3 slice_bitcast_fusion
  165.2 0.7 reduce_sum.12
  (21 shorter events, 0.1 us)
Async XLA Ops:
  0.6 53.8 %copy-start.10 = (bf16[512,832]{0,1:T(8,128)(2,1)S(1)}, bf16[512,832]{0,1:T(8,128)(2,1)}, u32[]{:S(2)}) copy-start(bf16[512,832]{0,1:T(8,128)(2,1)} %param.8) | copy-start | bytes 2555908
  2.2 64.6 %all-to-all-start = ((bf16[16,16,512]{2,1,0:T(8,128)(2,1)}), bf16[16,16,512]{2,1,0:T(8,128)(2,1)}, u32[]{:S(2)}, u32[]{:S(2)}) async-start(bf16[16,16,512]{2,1,0:T(8,128)(2,1)} %broadcast_in_dim.3), calls=%async_computation | async-start | bytes 524288 | tf_op jit(solution)/shard_map/all_to_all | solution.py:120
  55.7 11.0 %copy-start = (bf16[832,512]{1,0:T(8,128)(2,1)S(1)}, bf16[832,512]{1,0:T(8,128)(2,1)}, u32[]{:S(2)}) copy-start(bf16[832,512]{1,0:T(8,128)(2,1)} %down.1) | copy-start | bytes 2555908
  57.6 0.7 copy-start.2
  58.3 12.5 %collective-permute-start = (f32[16,16,1664]{2,1,0:T(8,128)}, f32[16,16,1664]{2,1,0:T(8,128)}, u32[]{:S(2)}, u32[]{:S(2)}) collective-permute-start(f32[16,16,1664]{2,1,0:T(8,128)} %get-tuple-element.13), channel_id=1, source_target_pairs={{0,16},{16,0},{1,17},{17,1},{2,18},{18,2},{3,19},{19,3},{4,20},{20... | collective-permute-start | bytes 5111816 | tf_op jit(solution)/shard_map/ppermute | solution.py:107
  68.2 0.7 copy-start.4
  68.9 4.4 %collective-permute-start.1 = (f32[16,16,832]{2,1,0:T(8,128)S(1)}, f32[16,16,832]{2,1,0:T(8,128)S(1)}, u32[]{:S(2)}, u32[]{:S(2)}) collective-permute-start(f32[16,16,832]{2,1,0:T(8,128)S(1)} %get-tuple-element.14), channel_id=1, source_target_pairs={{0,16},{16,0},{1,17},{17,1},{2,18},{18,2},{3,19},{19,3},{4,20},{20... | collective-permute-start | bytes 2555912 | tf_op jit(solution)/shard_map/ppermute | solution.py:107
  75.7 26.0 %copy-start.6 = (bf16[256,512]{1,0:T(8,128)(2,1)}, bf16[256,512]{1,0:T(8,128)(2,1)S(1)}, u32[]{:S(2)}) copy-start(bf16[256,512]{1,0:T(8,128)(2,1)S(1)} %get-tuple-element.17) | copy-start | bytes 786436
  75.8 26.0 %copy-start.8 = (bf16[256,512]{1,0:T(8,128)(2,1)}, bf16[256,512]{1,0:T(8,128)(2,1)S(1)}, u32[]{:S(2)}) copy-start(bf16[256,512]{1,0:T(8,128)(2,1)S(1)} %get-tuple-element.20) | copy-start | bytes 786436
  117.8 7.0 %collective-permute-start.2 = (bf16[16,16,1664]{2,1,0:T(8,128)(2,1)S(1)}, bf16[16,16,1664]{2,1,0:T(8,128)(2,1)S(1)}, u32[]{:S(2)}, u32[]{:S(2)}) collective-permute-start(bf16[16,16,1664]{2,1,0:T(8,128)(2,1)S(1)} %all_to_all.21.deltas), channel_id=1, source_target_pairs={{0,16},{16,0},{1,17},{17,1},{2,18},{18,2},{3,19},{19,3},{4,20},{20... | collective-permute-start | bytes 2555912 | tf_op jit(solution)/shard_map/ppermute | solution.py:107
  125.4 0.8 copy-start.1
  126.2 33.8 %copy-start.5 = (bf16[256,512]{1,0:T(8,128)(2,1)S(1)}, bf16[256,512]{1,0:T(8,128)(2,1)}, u32[]{:S(2)}) copy-start(bf16[256,512]{1,0:T(8,128)(2,1)} %copy-done.4) | copy-start | bytes 786436
  126.3 38.9 %all-to-all-start.3 = ((bf16[16,32,512]{2,1,0:T(8,128)(2,1)}), bf16[16,32,512]{2,1,0:T(8,128)(2,1)S(1)}, u32[]{:S(2)}, u32[]{:S(2)}) async-start(bf16[16,32,512]{2,1,0:T(8,128)(2,1)} %bitcast.27), calls=%async_computation.3 | async-start | bytes 1048576 | tf_op jit(solution)/shard_map/all_to_all | solution.py:167
  160.0 1.0 copy-start.9
  160.5 1.8 %copy-start.3 = (bf16[256,512]{1,0:T(8,128)(2,1)S(1)}, bf16[256,512]{1,0:T(8,128)(2,1)}, u32[]{:S(2)}) copy-start(bf16[256,512]{1,0:T(8,128)(2,1)} %copy-done.2) | copy-start | bytes 786436
  162.3 1.0 copy-start.7

commit v4 on v2

v4 whole, which is shorter than its diff:
```python
import jax
import jax.numpy as jnp
from jax import lax
from jax.experimental import pallas as pl
from jax.experimental.pallas import tpu as pltpu
from jax.sharding import Mesh, PartitionSpec as P

BF16, F32 = jnp.bfloat16, jnp.float32
XY = ("x", "y")
FAR = 4
OFFSETS = (0, 1, -1, 2)
VMEM = pl.BlockSpec(memory_space=pltpu.VMEM)
SMEM = pl.BlockSpec(memory_space=pltpu.SMEM)


def nonlinear(gate, up, hidden_grad):
    sig = jax.nn.sigmoid(gate)
    silu = gate * sig
    hidden = (silu * up).astype(BF16)
    gate_delta = (hidden_grad * up * sig * (1.0 + gate * (1.0 - sig))).astype(BF16)
    up_delta = (hidden_grad * silu).astype(BF16)
    return (hidden, gate_delta, up_delta)


def contract(left, right, left_dim, right_dim):
    return lax.dot_general(
        left, right, (((left_dim,), (right_dim,)), ((), ())), preferred_element_type=F32
    )


def call(body, outs, flops, *args):
    moved = sum(a.size * a.dtype.itemsize for a in (*args, *jax.tree.leaves(outs)))
    return pl.pallas_call(
        body,
        out_shape=outs,
        in_specs=[SMEM if a.dtype == jnp.int32 else VMEM for a in args],
        out_specs=jax.tree.map(lambda _: VMEM, outs),
        compiler_params=pltpu.CompilerParams(vmem_limit_bytes=20 * 2**20),
        cost_estimate=pl.CostEstimate(flops=flops, bytes_accessed=moved, transcendentals=0),
    )(*args)


def half_rows(which, kind, near, second_low, second_high):
    rows = []
    for far in range(2):
        rows += [ref[2 * which + far, kind] for ref in near]
        rows.append(jnp.where(which == 0, second_low[far, kind], second_high[far, kind]))
    return jnp.concatenate(rows, 0)


def send_body(where, a, b, c, d, e, pair, down, pair_out, down_out):
    for kind, weight, out in ((0, pair, pair_out), (1, down, down_out)):
        rows = half_rows(1 - where[0], kind, (a, b, c), d, e)
        out[...] = contract(rows, weight[...], 1, 1).reshape(out.shape)


def keep_body(where, a, b, c, d, e, pair, down, got_pair, got_down, out):
    blocks, rows, _ = out.shape
    wide = pair.shape[0]
    for kind, weight, got, lanes in (
        (0, pair, got_pair, slice(0, wide)),
        (1, down, got_down, slice(wide, None)),
    ):
        mine = half_rows(where[0], kind, (a, b, c), d, e)
        total = contract(mine, weight[...], 1, 1).reshape(blocks, rows, -1)
        out[:, :, lanes] = (total + got[...]).astype(BF16)


def middle_body(parts, out):
    units = parts.shape[2] // 3
    total = parts[0].astype(F32)
    for i in range(1, parts.shape[0]):
        total += parts[i].astype(F32)
    hid, gate_delta, up_delta = nonlinear(
        total[:, :units], total[:, units : 2 * units], total[:, 2 * units :]
    )
    row = jnp.concatenate([gate_delta, up_delta, hid], 1)
    out[...] = jnp.broadcast_to(row[None], out.shape)


def part_of(deltas, pair):
    lanes = pair.shape[0]
    rows = deltas[...].reshape(-1, deltas.shape[-1])[:, :lanes]
    return contract(rows, pair[...], 1, 0).astype(BF16)


def own_body(deltas, pair, out):
    out[...] = part_of(deltas, pair)


def other_body(where, deltas, pair, own, out):
    devices, tokens, _ = out.shape
    parts = (own[...], part_of(deltas, pair))
    for far in range(2):
        for k, offset in enumerate(OFFSETS):
            start = (far * len(OFFSETS) + k) * tokens
            for half, part in zip((where[0], 1 - where[0]), parts, strict=True):
                device = lax.rem(where[1] + devices + offset + FAR * (2 * half + far), devices)
                out[device] = part[start : start + tokens]


def rows_body(where, a, b, c, d, e, _, x_own, g_own, x_other, g_other):
    for kind, own, other in ((0, x_own, x_other), (1, g_own, g_other)):
        own[...] = half_rows(where[0], kind, (a, b, c), d, e)
        other[...] = half_rows(1 - where[0], kind, (a, b, c), d, e)


def swap_cores(value):
    return lax.ppermute(value, "core", [(0, 1), (1, 0)])


def shift(value, by):
    return lax.ppermute(value, "col", [((i + by) % 16, i) for i in range(16)])


def per_device(inputs, out_grad, gate_weight, up_weight, down_weight):
    tokens, width = inputs.shape
    units = gate_weight.shape[1]
    n = 16
    half = n * tokens // 2
    core, col = lax.axis_index("core"), lax.axis_index("col")
    where = jnp.stack([core, col]).astype(jnp.int32)
    pair = jnp.concatenate([gate_weight.T, up_weight.T], 0)

    both = jnp.stack([inputs, out_grad])
    group = jnp.stack([both, shift(both, FAR), shift(both, 2 * FAR), shift(both, -FAR)])
    after, before = shift(group, 1), shift(group, -1)
    low = shift(group[:2], 2)
    high = shift(jnp.concatenate([group[3:], group[:1]]), -2)
    held = (group, after, before, low, high)

    flops = 2 * half * units * width
    sds = jax.ShapeDtypeStruct
    sent = call(
        send_body,
        (sds((n, half // n, 2 * units), F32), sds((n, half // n, units), F32)),
        3 * flops,
        where,
        *held,
        pair,
        down_weight,
    )
    sent = [swap_cores(value) for value in sent]
    parts = call(
        keep_body, sds((n, half // n, 3 * units), BF16), 3 * flops, where, *held, pair, down_weight, *sent
    )
    parts = lax.all_to_all(parts, XY, 0, 0)
    row = call(middle_body, sds(parts.shape, BF16), 40 * half // n * units, parts)
    own = lax.all_to_all(row, XY, 0, 0)
    other = swap_cores(own)
    rows = sds((half, width), BF16)
    own_part = call(own_body, rows, 2 * flops, own, pair)
    pieces = call(
        other_body, sds((n, tokens, width), BF16), 2 * flops, where, other, pair, own_part
    )
    x_own, g_own, x_other, g_other = call(rows_body, (rows,) * 4, 0, where, *held, pieces)
    pieces = lax.all_to_all(pieces, "col", 0, 0)
    input_grad = jnp.sum(pieces.astype(F32), axis=0).astype(BF16)

    def grad(lanes, mine, others):
        total = contract(own.reshape(half, -1)[:, lanes], mine, 0, 0)
        return (total + contract(other.reshape(half, -1)[:, lanes], others, 0, 0)).astype(BF16)

    pair_grad = grad(slice(0, 2 * units), x_own, x_other)
    down_grad = grad(slice(2 * units, None), g_own, g_other)
    return (input_grad, pair_grad[:units].T, pair_grad[units:].T, down_grad)


def solution(mesh):
    grid = Mesh(mesh.devices.reshape(4, 4, 2, 16), ("x", "y", "core", "col"))
    row = ("x", "y", "core")
    return jax.shard_map(
        per_device,
        mesh=grid,
        in_specs=(P("col", row), P("col", row), P(row, "col"), P(row, "col"), P("col", row)),
        out_specs=(P("col", row), P(row, "col"), P(row, "col"), P("col", row)),
        check_vma=False,
    )
```

time: 166 us -> 163 us (0.982)
  blocking collectives: 85 us -> 49.1 us
  starting transfers between devices: 25.9 us -> 58.9 us
  local copies, waits for them, and re-layouts: 11.7 us -> 4.47 us
  waiting for transfers between devices: 28.2 us -> 33.9 us
  Pallas kernels: 5.78 us -> 8.03 us
  matrix products: 5.1 us -> 3.04 us
    all_to_all x2 -> x1, blocking collectives: 57.8 us -> 22.3 us  [per_device(): own = lax.all_to_all(row, XY, 0, 0)]
    ppermute x4 -> x7, starting transfers between devices: 13.8 us -> 41.2 us  [shift(): return lax.ppermute(value, 'col', [((i + by) % 16, i) for i in range(16)])]
    all_to_all x1, starting transfers between devices: 5.89 us -> 11.4 us  [per_device(): pieces = lax.all_to_all(pieces, 'col', 0, 0)]
    ppermute x4 -> x7, waiting for transfers between devices: 2.95 us -> 7.53 us  [shift(): return lax.ppermute(value, 'col', [((i + by) % 16, i) for i in range(16)])]
    ppermute x3, waiting for transfers between devices: 2.08 us -> 4.82 us  [swap_cores(): return lax.ppermute(value, 'core', [(0, 1), (1, 0)])]
    ppermute x1 -> x0, local copies, waits for them, and re-layouts: 2.46 us -> none  [swap_cores(): return lax.ppermute(value, 'core', [(0, 1), (1, 0)])]
    pallas_call x6, Pallas kernels: 5.78 us -> 8.03 us  [call(): pl.pallas_call(body, out_shape=outs, in_specs=[SMEM if a.dtype == jnp.int...]
    dot_general x4, matrix products: 5.1 us -> 3.04 us  [contract(): lax.dot_general(left, right, (((left_dim,), (right_dim,)), ((), ())), pre...]
  transfers between devices with their start and end apart: 8 -> 11, of which waited for: 4 -> 6; matrix products, arithmetic and copies ran while one was open for 7% -> 4% of each run, Pallas kernels for 1% -> 1%
where the time goes in v4:
time: 163 us; the launch traced here: 162 us
  starting transfers between devices  58.9 us (36%)
  blocking collectives  49.1 us (30%)
  waiting for transfers between devices  33.9 us (21%)
  Pallas kernels  8.03 us (5%)
  local copies, waits for them, and re-layouts  4.47 us (3%)
  other arithmetic  3.73 us (2%)
  matrix products  3.04 us (2%)
    ppermute x7, starting transfers between devices, shift(): return lax.ppermute(value, 'col', [((i + by) % 16, i) for i in range(16)])  41.2 us
    all_to_all x1, blocking collectives, per_device(): parts = lax.all_to_all(parts, XY, 0, 0)  26.8 us
    all_to_all x1, blocking collectives, per_device(): own = lax.all_to_all(row, XY, 0, 0)  22.3 us
    all_to_all x1, waiting for transfers between devices, per_device(): pieces = lax.all_to_all(pieces, 'col', 0, 0)  21.6 us
    all_to_all x1, starting transfers between devices, per_device(): pieces = lax.all_to_all(pieces, 'col', 0, 0)  11.4 us
    pallas_call x6, Pallas kernels, call(): pl.pallas_call(body, out_shape=outs, in_specs=[SMEM if a.dtype == jnp.int...  8.03 us
    ppermute x7, waiting for transfers between devices, shift(): return lax.ppermute(value, 'col', [((i + by) % 16, i) for i in range(16)])  7.53 us
    ppermute x3, starting transfers between devices, swap_cores(): return lax.ppermute(value, 'core', [(0, 1), (1, 0)])  6.24 us
  transfers between devices with their start and end apart: 11, of which 6 were waited for; matrix products, arithmetic and copies ran while one was open for 4% of the time, Pallas kernels for 1%

profile of v4, /device:TPU:32, one launch (start us, length us, event | category | flops | bytes accessed | tf_op | source)
XLA Modules:
  0.0 162.0 jit_solution(7804764457807135622)
XLA Ops:
  0.6 0.9 fusion.6
  1.5 11.8 %collective-permute-start = (bf16[2,32,512]{2,1,0:T(8,128)(2,1)S(1)}, bf16[2,32,512]{2,1,0:T(8,128)(2,1)S(1)}, u32[]{:S(2)}, u32[]{:S(2)}) collective-permute-start(bf16[2,32,512]{2,1,0:T(8,128)(2,1)S(1)} %get-tuple-element.21), channel_id=1, source_target_pairs={{4,0},{5,1},{6,2},{7,3},{8,4},{9,5},{10,6},{11,7},{12,8},{13,9},{1... | collective-permute-start | bytes 196616 | tf_op jit(solution)/shard_map/ppermute | solution.py:113
  13.3 1.9 %collective-permute-start.2 = (bf16[2,32,512]{2,1,0:T(8,128)(2,1)S(1)}, bf16[2,32,512]{2,1,0:T(8,128)(2,1)S(1)}, u32[]{:S(2)}, u32[]{:S(2)}) collective-permute-start(bf16[2,32,512]{2,1,0:T(8,128)(2,1)S(1)} %get-tuple-element.21), channel_id=1, source_target_pairs={{12,0},{13,1},{14,2},{15,3},{0,4},{1,5},{2,6},{3,7},{4,8},{5,9},{6... | collective-permute-start | bytes 196616 | tf_op jit(solution)/shard_map/ppermute | solution.py:113
  15.3 10.8 %collective-permute-start.1 = (bf16[2,32,512]{2,1,0:T(8,128)(2,1)S(1)}, bf16[2,32,512]{2,1,0:T(8,128)(2,1)S(1)}, u32[]{:S(2)}, u32[]{:S(2)}) collective-permute-start(bf16[2,32,512]{2,1,0:T(8,128)(2,1)S(1)} %get-tuple-element.21), channel_id=1, source_target_pairs={{8,0},{9,1},{10,2},{11,3},{12,4},{13,5},{14,6},{15,7},{0,8},{1,9},... | collective-permute-start | bytes 196616 | tf_op jit(solution)/shard_map/ppermute | solution.py:113
  26.1 0.7 pad_maximum_fusion.3
  26.8 3.6 %collective-permute-done.1 = bf16[2,32,512]{2,1,0:T(8,128)(2,1)S(1)} collective-permute-done((bf16[2,32,512]{2,1,0:T(8,128)(2,1)S(1)}, bf16[2,32,512]{2,1,0:T(8,128)(2,1)S(1)}, u32[]{:S(2)}, u32[]{:S(2)}) %collective-permute-start.1) | collective-permute-done | bytes 65568 | tf_op jit(solution)/shard_map/ppermute | solution.py:113
  30.5 5.3 %collective-permute-start.4 = (bf16[4,2,32,512]{3,2,1,0:T(8,128)(2,1)S(1)}, bf16[4,2,32,512]{3,2,1,0:T(8,128)(2,1)S(1)}, u32[]{:S(2)}, u32[]{:S(2)}) collective-permute-start(bf16[4,2,32,512]{3,2,1,0:T(8,128)(2,1)S(1)} %pad_maximum_fusion.1.a), channel_id=1, source_target_pairs={{15,0},{0,1},{1,2},{2,3},{3,4},{4,5},{5,6},{6,7},{7,8},{8,9},{9,10... | collective-permute-start | bytes 786440 | tf_op jit(solution)/shard_map/ppermute | solution.py:113
  35.8 1.9 %collective-permute-start.3 = (bf16[4,2,32,512]{3,2,1,0:T(8,128)(2,1)S(1)}, bf16[4,2,32,512]{3,2,1,0:T(8,128)(2,1)S(1)}, u32[]{:S(2)}, u32[]{:S(2)}) collective-permute-start(bf16[4,2,32,512]{3,2,1,0:T(8,128)(2,1)S(1)} %pad_maximum_fusion.1.a), channel_id=1, source_target_pairs={{1,0},{2,1},{3,2},{4,3},{5,4},{6,5},{7,6},{8,7},{9,8},{10,9},{11,1... | collective-permute-start | bytes 786440 | tf_op jit(solution)/shard_map/ppermute | solution.py:113
  37.7 5.6 %collective-permute-start.6 = (bf16[2,2,32,512]{3,2,1,0:T(8,128)(2,1)}, bf16[2,2,32,512]{3,2,1,0:T(8,128)(2,1)S(1)}, u32[]{:S(2)}, u32[]{:S(2)}) collective-permute-start(bf16[2,2,32,512]{3,2,1,0:T(8,128)(2,1)} %get-tuple-element.18), channel_id=1, source_target_pairs={{14,0},{15,1},{0,2},{1,3},{2,4},{3,5},{4,6},{5,7},{6,8},{7,9},{8,1... | collective-permute-start | bytes 393224 | tf_op jit(solution)/shard_map/ppermute | solution.py:113
  43.3 3.8 %collective-permute-start.5 = (bf16[2,2,32,512]{3,2,1,0:T(8,128)(2,1)}, bf16[2,2,32,512]{3,2,1,0:T(8,128)(2,1)}, u32[]{:S(2)}, u32[]{:S(2)}) collective-permute-start(bf16[2,2,32,512]{3,2,1,0:T(8,128)(2,1)} %get-tuple-element.19), channel_id=1, source_target_pairs={{2,0},{3,1},{4,2},{5,3},{6,4},{7,5},{8,6},{9,7},{10,8},{11,9},{12,... | collective-permute-start | bytes 393224 | tf_op jit(solution)/shard_map/ppermute | solution.py:113
  47.2 1.3 pad_maximum_fusion.pair
  48.6 2.8 %collective-permute-done.6.e = bf16[2,2,32,512]{3,2,1,0:T(8,128)(2,1)S(1)} collective-permute-done((bf16[2,2,32,512]{3,2,1,0:T(8,128)(2,1)}, bf16[2,2,32,512]{3,2,1,0:T(8,128)(2,1)S(1)}, u32[]{:S(2)}, u32[]{:S(2)}) %collective-permute-start.6) | collective-permute-done | bytes 131104 | tf_op jit(solution)/shard_map/ppermute | solution.py:113
  51.5 1.1 collective-permute-done.5.d
  52.6 1.9 %shard_map.84 = (f32[16,16,1664]{2,1,0:T(8,128)S(1)}, f32[16,16,832]{2,1,0:T(8,128)S(1)}) custom-call(s32[2]{0:T(128)S(1)} %pad_add_fusion.where, bf16[4,2,32,512]{3,2,1,0:T(8,128)(2,1)S(1)} %pad_maximum_fusion.1.a, bf16[4,2,32,512]{3,2,1,0:T(8,128)(2,1)S(1)} %collective-permute-done.3.b, bf16[4,2,32,512]{3,2,1,0:T(8,128)(2,1)S(1)} %collective-permute-done.4.c, ...), custom_call_target="tpu_custom_call" | custom-call | flops 654311424 | bytes 6160392 | tf_op jit(solution)/shard_map/pallas_call | solution.py:33
  54.5 1.9 %collective-permute-start.7 = (f32[16,16,1664]{2,1,0:T(8,128)S(1)}, f32[16,16,1664]{2,1,0:T(8,128)S(1)}, u32[]{:S(2)}, u32[]{:S(2)}) collective-permute-start(f32[16,16,1664]{2,1,0:T(8,128)S(1)} %get-tuple-element.10), channel_id=1, source_target_pairs={{0,16},{16,0},{1,17},{17,1},{2,18},{18,2},{3,19},{19,3},{4,20},{20... | collective-permute-start | bytes 5111816 | tf_op jit(solution)/shard_map/ppermute | solution.py:109
  56.4 2.4 %collective-permute-start.8 = (f32[16,16,832]{2,1,0:T(8,128)S(1)}, f32[16,16,832]{2,1,0:T(8,128)S(1)}, u32[]{:S(2)}, u32[]{:S(2)}) collective-permute-start(f32[16,16,832]{2,1,0:T(8,128)S(1)} %get-tuple-element.11), channel_id=1, source_target_pairs={{0,16},{16,0},{1,17},{17,1},{2,18},{18,2},{3,19},{19,3},{4,20},{20... | collective-permute-start | bytes 2555912 | tf_op jit(solution)/shard_map/ppermute | solution.py:109
  58.9 2.5 %collective-permute-done.8.got_down = f32[16,16,832]{2,1,0:T(8,128)S(1)} collective-permute-done((f32[16,16,832]{2,1,0:T(8,128)S(1)}, f32[16,16,832]{2,1,0:T(8,128)S(1)}, u32[]{:S(2)}, u32[]{:S(2)}) %collective-permute-start.8) | collective-permute-done | bytes 852000 | tf_op jit(solution)/shard_map/ppermute | solution.py:109
  61.3 1.9 %shard_map.85 = bf16[16,16,2496]{2,1,0:T(8,128)(2,1)S(1)} custom-call(s32[2]{0:T(128)S(1)} %pad_add_fusion.where, bf16[4,2,32,512]{3,2,1,0:T(8,128)(2,1)S(1)} %pad_maximum_fusion.1.a, bf16[4,2,32,512]{3,2,1,0:T(8,128)(2,1)S(1)} %collective-permute-done.3.b, bf16[4,2,32,512]{3,2,1,0:T(8,128)(2,1)S(1)} %collective-permute-done.4.c, ...), custom_call_target="tpu_custom_call" | custom-call | flops 654311424 | bytes 7438344 | tf_op jit(solution)/shard_map/pallas_call | solution.py:33
  63.2 26.8 %all_to_all.15.parts = bf16[16,16,2496]{2,1,0:T(8,128)(2,1)S(1)} all-to-all(bf16[16,16,2496]{2,1,0:T(8,128)(2,1)S(1)} %shard_map.85), channel_id=1, replica_groups=mesh['x'=4,'y'=4,'core'=2,'col'=16] {'x','y'}, dimensions={0} | all-to-all | bytes 2555904 | tf_op jit(solution)/shard_map/all_to_all | solution.py:147
  90.3 22.3 %all_to_all.16.deltas = bf16[16,16,2496]{2,1,0:T(8,128)(2,1)S(1)} all-to-all(bf16[16,16,2496]{2,1,0:T(8,128)(2,1)S(1)} %shard_map.86), channel_id=1, replica_groups=mesh['x'=4,'y'=4,'core'=2,'col'=16] {'x','y'}, dimensions={0} | all-to-all | bytes 2555904 | tf_op jit(solution)/shard_map/all_to_all | solution.py:149
  112.6 1.9 %collective-permute-start.9 = (bf16[16,16,2496]{2,1,0:T(8,128)(2,1)S(1)}, bf16[16,16,2496]{2,1,0:T(8,128)(2,1)S(1)}, u32[]{:S(2)}, u32[]{:S(2)}) collective-permute-start(bf16[16,16,2496]{2,1,0:T(8,128)(2,1)S(1)} %all_to_all.16.deltas), channel_id=1, source_target_pairs={{0,16},{16,0},{1,17},{17,1},{2,18},{18,2},{3,19},{19,3},{4,20},{20... | collective-permute-start | bytes 3833864 | tf_op jit(solution)/shard_map/ppermute | solution.py:109
  115.2 2.4 %collective-permute-done.9.deltas = bf16[16,16,2496]{2,1,0:T(8,128)(2,1)S(1)} collective-permute-done((bf16[16,16,2496]{2,1,0:T(8,128)(2,1)S(1)}, bf16[16,16,2496]{2,1,0:T(8,128)(2,1)S(1)}, u32[]{:S(2)}, u32[]{:S(2)}) %collective-permute-start.9) | collective-permute-done | bytes 1277984 | tf_op jit(solution)/shard_map/ppermute | solution.py:109
  117.5 2.0 %shard_map.88._ = bf16[16,32,512]{2,1,0:T(8,128)(2,1)} custom-call(s32[2]{0:T(128)S(1)} %pad_add_fusion.where, bf16[16,16,2496]{2,1,0:T(8,128)(2,1)S(1)} %collective-permute-done.9.deltas, bf16[1664,512]{1,0:T(8,128)(2,1)S(1)} %pad_maximum_fusion.pair, bf16[256,512]{1,0:T(8,128)(2,1)S(1)} %shard_map.87.own), custom_call_target="tpu_custom_call" | custom-call | flops 436207616 | bytes 3768328 | tf_op jit(solution)/shard_map/pallas_call | solution.py:33
  119.5 1.1 copy-done
  120.6 11.4 %all-to-all-start.2 = ((bf16[16,32,512]{2,1,0:T(8,128)(2,1)}), bf16[16,32,512]{2,1,0:T(8,128)(2,1)S(1)}, u32[]{:S(2)}, u32[]{:S(2)}) async-start(bf16[16,32,512]{2,1,0:T(8,128)(2,1)} %shard_map.88._), calls=%async_computation.2 | async-start | bytes 1048576 | tf_op jit(solution)/shard_map/all_to_all | solution.py:157
  132.0 0.9 copy-done.4
  132.9 0.9 copy-done.6
  133.8 1.3 shard_map.89
  137.1 1.3 slice_bitcast_fusion
  138.4 1.3 add_convert_fusion.1
  139.7 21.6 %all-to-all-done.2 = bf16[16,32,512]{2,1,0:T(8,128)(2,1)S(1)} async-done(((bf16[16,32,512]{2,1,0:T(8,128)(2,1)}), bf16[16,32,512]{2,1,0:T(8,128)(2,1)S(1)}, u32[]{:S(2)}, u32[]{:S(2)}) %all-to-all-start.2) | async-done | bytes 524320 | tf_op jit(solution)/shard_map/all_to_all | solution.py:157
  161.3 0.7 reduce_sum.12
  (25 shorter events, 3.0 us)
Async XLA Ops:
  0.6 46.5 %copy-start.7 = (bf16[512,832]{0,1:T(8,128)(2,1)S(1)}, bf16[512,832]{0,1:T(8,128)(2,1)}, u32[]{:S(2)}) copy-start(bf16[512,832]{0,1:T(8,128)(2,1)} %param.8) | copy-start | bytes 2555908
  1.5 24.6 %collective-permute-start = (bf16[2,32,512]{2,1,0:T(8,128)(2,1)S(1)}, bf16[2,32,512]{2,1,0:T(8,128)(2,1)S(1)}, u32[]{:S(2)}, u32[]{:S(2)}) collective-permute-start(bf16[2,32,512]{2,1,0:T(8,128)(2,1)S(1)} %get-tuple-element.21), channel_id=1, source_target_pairs={{4,0},{5,1},{6,2},{7,3},{8,4},{9,5},{10,6},{11,7},{12,8},{13,9},{1... | collective-permute-start | bytes 196616 | tf_op jit(solution)/shard_map/ppermute | solution.py:113
  13.3 12.8 %collective-permute-start.2 = (bf16[2,32,512]{2,1,0:T(8,128)(2,1)S(1)}, bf16[2,32,512]{2,1,0:T(8,128)(2,1)S(1)}, u32[]{:S(2)}, u32[]{:S(2)}) collective-permute-start(bf16[2,32,512]{2,1,0:T(8,128)(2,1)S(1)} %get-tuple-element.21), channel_id=1, source_target_pairs={{12,0},{13,1},{14,2},{15,3},{0,4},{1,5},{2,6},{3,7},{4,8},{5,9},{6... | collective-permute-start | bytes 196616 | tf_op jit(solution)/shard_map/ppermute | solution.py:113
  15.3 15.2 %collective-permute-start.1 = (bf16[2,32,512]{2,1,0:T(8,128)(2,1)S(1)}, bf16[2,32,512]{2,1,0:T(8,128)(2,1)S(1)}, u32[]{:S(2)}, u32[]{:S(2)}) collective-permute-start(bf16[2,32,512]{2,1,0:T(8,128)(2,1)S(1)} %get-tuple-element.21), channel_id=1, source_target_pairs={{8,0},{9,1},{10,2},{11,3},{12,4},{13,5},{14,6},{15,7},{0,8},{1,9},... | collective-permute-start | bytes 196616 | tf_op jit(solution)/shard_map/ppermute | solution.py:113
  30.5 22.0 %collective-permute-start.4 = (bf16[4,2,32,512]{3,2,1,0:T(8,128)(2,1)S(1)}, bf16[4,2,32,512]{3,2,1,0:T(8,128)(2,1)S(1)}, u32[]{:S(2)}, u32[]{:S(2)}) collective-permute-start(bf16[4,2,32,512]{3,2,1,0:T(8,128)(2,1)S(1)} %pad_maximum_fusion.1.a), channel_id=1, source_target_pairs={{15,0},{0,1},{1,2},{2,3},{3,4},{4,5},{5,6},{6,7},{7,8},{8,9},{9,10... | collective-permute-start | bytes 786440 | tf_op jit(solution)/shard_map/ppermute | solution.py:113
  35.8 16.8 %collective-permute-start.3 = (bf16[4,2,32,512]{3,2,1,0:T(8,128)(2,1)S(1)}, bf16[4,2,32,512]{3,2,1,0:T(8,128)(2,1)S(1)}, u32[]{:S(2)}, u32[]{:S(2)}) collective-permute-start(bf16[4,2,32,512]{3,2,1,0:T(8,128)(2,1)S(1)} %pad_maximum_fusion.1.a), channel_id=1, source_target_pairs={{1,0},{2,1},{3,2},{4,3},{5,4},{6,5},{7,6},{8,7},{9,8},{10,9},{11,1... | collective-permute-start | bytes 786440 | tf_op jit(solution)/shard_map/ppermute | solution.py:113
  37.7 13.7 %collective-permute-start.6 = (bf16[2,2,32,512]{3,2,1,0:T(8,128)(2,1)}, bf16[2,2,32,512]{3,2,1,0:T(8,128)(2,1)S(1)}, u32[]{:S(2)}, u32[]{:S(2)}) collective-permute-start(bf16[2,2,32,512]{3,2,1,0:T(8,128)(2,1)} %get-tuple-element.18), channel_id=1, source_target_pairs={{14,0},{15,1},{0,2},{1,3},{2,4},{3,5},{4,6},{5,7},{6,8},{7,9},{8,1... | collective-permute-start | bytes 393224 | tf_op jit(solution)/shard_map/ppermute | solution.py:113
  43.3 9.2 %collective-permute-start.5 = (bf16[2,2,32,512]{3,2,1,0:T(8,128)(2,1)}, bf16[2,2,32,512]{3,2,1,0:T(8,128)(2,1)}, u32[]{:S(2)}, u32[]{:S(2)}) collective-permute-start(bf16[2,2,32,512]{3,2,1,0:T(8,128)(2,1)} %get-tuple-element.19), channel_id=1, source_target_pairs={{2,0},{3,1},{4,2},{5,3},{6,4},{7,5},{8,6},{9,7},{10,8},{11,9},{12,... | collective-permute-start | bytes 393224 | tf_op jit(solution)/shard_map/ppermute | solution.py:113
  47.2 5.4 %copy-start.2 = (bf16[832,512]{1,0:T(8,128)(2,1)S(1)}, bf16[832,512]{1,0:T(8,128)(2,1)}, u32[]{:S(2)}) copy-start(bf16[832,512]{1,0:T(8,128)(2,1)} %down.3) | copy-start | bytes 2555908
  51.5 9.9 %copy-start.5 = (bf16[2,2,32,512]{3,2,1,0:T(8,128)(2,1)}, bf16[2,2,32,512]{3,2,1,0:T(8,128)(2,1)S(1)}, u32[]{:S(2)}) copy-start(bf16[2,2,32,512]{3,2,1,0:T(8,128)(2,1)S(1)} %collective-permute-done.6.e) | copy-start | bytes 393220
  52.5 8.8 %copy-start.3 = (bf16[4,2,32,512]{3,2,1,0:T(8,128)(2,1)}, bf16[4,2,32,512]{3,2,1,0:T(8,128)(2,1)S(1)}, u32[]{:S(2)}) copy-start(bf16[4,2,32,512]{3,2,1,0:T(8,128)(2,1)S(1)} %collective-permute-done.3.b) | copy-start | bytes 786436
  54.5 6.8 %collective-permute-start.7 = (f32[16,16,1664]{2,1,0:T(8,128)S(1)}, f32[16,16,1664]{2,1,0:T(8,128)S(1)}, u32[]{:S(2)}, u32[]{:S(2)}) collective-permute-start(f32[16,16,1664]{2,1,0:T(8,128)S(1)} %get-tuple-element.10), channel_id=1, source_target_pairs={{0,16},{16,0},{1,17},{17,1},{2,18},{18,2},{3,19},{19,3},{4,20},{20... | collective-permute-start | bytes 5111816 | tf_op jit(solution)/shard_map/ppermute | solution.py:109
  56.4 4.9 %collective-permute-start.8 = (f32[16,16,832]{2,1,0:T(8,128)S(1)}, f32[16,16,832]{2,1,0:T(8,128)S(1)}, u32[]{:S(2)}, u32[]{:S(2)}) collective-permute-start(f32[16,16,832]{2,1,0:T(8,128)S(1)} %get-tuple-element.11), channel_id=1, source_target_pairs={{0,16},{16,0},{1,17},{17,1},{2,18},{18,2},{3,19},{19,3},{4,20},{20... | collective-permute-start | bytes 2555912 | tf_op jit(solution)/shard_map/ppermute | solution.py:109
  112.6 4.9 %collective-permute-start.9 = (bf16[16,16,2496]{2,1,0:T(8,128)(2,1)S(1)}, bf16[16,16,2496]{2,1,0:T(8,128)(2,1)S(1)}, u32[]{:S(2)}, u32[]{:S(2)}) collective-permute-start(bf16[16,16,2496]{2,1,0:T(8,128)(2,1)S(1)} %all_to_all.16.deltas), channel_id=1, source_target_pairs={{0,16},{16,0},{1,17},{17,1},{2,18},{18,2},{3,19},{19,3},{4,20},{20... | collective-permute-start | bytes 3833864 | tf_op jit(solution)/shard_map/ppermute | solution.py:109
  119.5 1.1 copy-start
  120.6 40.7 %all-to-all-start.2 = ((bf16[16,32,512]{2,1,0:T(8,128)(2,1)}), bf16[16,32,512]{2,1,0:T(8,128)(2,1)S(1)}, u32[]{:S(2)}, u32[]{:S(2)}) async-start(bf16[16,32,512]{2,1,0:T(8,128)(2,1)} %shard_map.88._), calls=%async_computation.2 | async-start | bytes 1048576 | tf_op jit(solution)/shard_map/all_to_all | solution.py:157
  132.0 0.9 copy-start.4
  132.9 0.9 copy-start.6
  133.8 1.5 copy-start.1

commit v5 on v4

--- a/solution.py
+++ b/solution.py
@@ -35,7 +35,7 @@
         out_shape=outs,
         in_specs=[SMEM if a.dtype == jnp.int32 else VMEM for a in args],
         out_specs=jax.tree.map(lambda _: VMEM, outs),
-        compiler_params=pltpu.CompilerParams(vmem_limit_bytes=20 * 2**20),
+        compiler_params=pltpu.CompilerParams(vmem_limit_bytes=32 * 2**20),
         cost_estimate=pl.CostEstimate(flops=flops, bytes_accessed=moved, transcendentals=0),
     )(*args)
 
@@ -99,10 +99,23 @@
                 out[device] = part[start : start + tokens]
 
 
-def rows_body(where, a, b, c, d, e, _, x_own, g_own, x_other, g_other):
-    for kind, own, other in ((0, x_own, x_other), (1, g_own, g_other)):
-        own[...] = half_rows(where[0], kind, (a, b, c), d, e)
-        other[...] = half_rows(1 - where[0], kind, (a, b, c), d, e)
+def grads_body(where, a, b, c, d, e, own, other, pieces, input_out, gate_out, up_out, down_out):
+    total = pieces[0].astype(F32)
+    for i in range(1, pieces.shape[0]):
+        total += pieces[i].astype(F32)
+    input_out[...] = total.astype(BF16)
+    units = gate_out.shape[0]
+    deltas = [ref[...].reshape(-1, ref.shape[-1]) for ref in (own, other)]
+
+    def total_of(kind, lanes):
+        halves = (where[0], 1 - where[0])
+        rows = jnp.concatenate([half_rows(h, kind, (a, b, c), d, e) for h in halves], 0)
+        return contract(jnp.concatenate([m[:, lanes] for m in deltas], 0), rows, 0, 0).astype(BF16)
+
+    pair = total_of(0, slice(0, 2 * units))
+    gate_out[...] = pair[:units]
+    up_out[...] = pair[units:]
+    down_out[...] = total_of(1, slice(2 * units, 3 * units))
 
 
 def swap_cores(value):
@@ -148,22 +161,23 @@
     row = call(middle_body, sds(parts.shape, BF16), 40 * half // n * units, parts)
     own = lax.all_to_all(row, XY, 0, 0)
     other = swap_cores(own)
-    rows = sds((half, width), BF16)
-    own_part = call(own_body, rows, 2 * flops, own, pair)
+    own_part = call(own_body, sds((half, width), BF16), 2 * flops, own, pair)
     pieces = call(
         other_body, sds((n, tokens, width), BF16), 2 * flops, where, other, pair, own_part
     )
-    x_own, g_own, x_other, g_other = call(rows_body, (rows,) * 4, 0, where, *held, pieces)
     pieces = lax.all_to_all(pieces, "col", 0, 0)
-    input_grad = jnp.sum(pieces.astype(F32), axis=0).astype(BF16)
-
-    def grad(lanes, mine, others):
-        total = contract(own.reshape(half, -1)[:, lanes], mine, 0, 0)
-        return (total + contract(other.reshape(half, -1)[:, lanes], others, 0, 0)).astype(BF16)
-
-    pair_grad = grad(slice(0, 2 * units), x_own, x_other)
-    down_grad = grad(slice(2 * units, None), g_own, g_other)
-    return (input_grad, pair_grad[:units].T, pair_grad[units:].T, down_grad)
+    grad = sds((units, width), BF16)
+    input_grad, gate_grad, up_grad, down_grad = call(
+        grads_body,
+        (sds((tokens, width), BF16), grad, grad, grad),
+        6 * flops,
+        where,
+        *held,
+        own,
+        other,
+        pieces,
+    )
+    return (input_grad, gate_grad.T, up_grad.T, down_grad)
 
 
 def solution(mesh):

time: 163 us -> 163 us (level)
  blocking collectives: 49.1 us -> 89.6 us
  waiting for transfers between devices: 33.9 us -> 12.4 us
  starting transfers between devices: 58.9 us -> 47.5 us
  local copies, waits for them, and re-layouts: 4.47 us -> 0.01 us
  matrix products: 3.04 us -> 0 us
    all_to_all x0 -> x1, blocking collectives: none -> 40.5 us  [per_device(): pieces = lax.all_to_all(pieces, 'col', 0, 0)]
    all_to_all x1 -> x0, waiting for transfers between devices: 21.6 us -> none  [per_device(): pieces = lax.all_to_all(pieces, 'col', 0, 0)]
    all_to_all x1 -> x0, starting transfers between devices: 11.4 us -> none  [per_device(): pieces = lax.all_to_all(pieces, 'col', 0, 0)]
    unnamed x16 -> x4, local copies, waits for them, and re-layouts: 3.18 us -> 0.01 us
    dot_general x4 -> x0, matrix products: 3.04 us -> none  [contract(): lax.dot_general(left, right, (((left_dim,), (right_dim,)), ((), ())), pre...]
  transfers between devices with their start and end apart: 11 -> 10, of which waited for: 6 -> 5; matrix products, arithmetic and copies ran while one was open for 4% -> 1% of each run, Pallas kernels for 1% -> 0%
where the time goes in v5:
time: 163 us; the launch traced here: 162 us
  blocking collectives  89.6 us (55%)
  starting transfers between devices  47.5 us (29%)
  waiting for transfers between devices  12.4 us (8%)
  Pallas kernels  9.22 us (6%)
  other arithmetic  3.03 us (2%)
    ppermute x7, starting transfers between devices, shift(): return lax.ppermute(value, 'col', [((i + by) % 16, i) for i in range(16)])  41.2 us
    all_to_all x1, blocking collectives, per_device(): pieces = lax.all_to_all(pieces, 'col', 0, 0)  40.5 us
    all_to_all x1, blocking collectives, per_device(): parts = lax.all_to_all(parts, XY, 0, 0)  26.8 us
    all_to_all x1, blocking collectives, per_device(): own = lax.all_to_all(row, XY, 0, 0)  22.3 us
    pallas_call x6, Pallas kernels, call(): pl.pallas_call(body, out_shape=outs, in_specs=[SMEM if a.dtype == jnp.int...  9.22 us
    ppermute x7, waiting for transfers between devices, shift(): return lax.ppermute(value, 'col', [((i + by) % 16, i) for i in range(16)])  7.53 us
    ppermute x3, starting transfers between devices, swap_cores(): return lax.ppermute(value, 'core', [(0, 1), (1, 0)])  6.24 us
    ppermute x3, waiting for transfers between devices, swap_cores(): return lax.ppermute(value, 'core', [(0, 1), (1, 0)])  4.82 us
  transfers between devices with their start and end apart: 10, of which 5 were waited for; matrix products, arithmetic and copies ran while one was open for 1% of the time, Pallas kernels for 0%

profile of v5, /device:TPU:32, one launch (start us, length us, event | category | flops | bytes accessed | tf_op | source)
XLA Modules:
  0.0 162.5 jit_solution(6551133798249092928)
XLA Ops:
  0.6 0.9 fusion
  1.5 11.8 %collective-permute-start = (bf16[2,32,512]{2,1,0:T(8,128)(2,1)S(1)}, bf16[2,32,512]{2,1,0:T(8,128)(2,1)S(1)}, u32[]{:S(2)}, u32[]{:S(2)}) collective-permute-start(bf16[2,32,512]{2,1,0:T(8,128)(2,1)S(1)} %get-tuple-element.19), channel_id=1, source_target_pairs={{4,0},{5,1},{6,2},{7,3},{8,4},{9,5},{10,6},{11,7},{12,8},{13,9},{1... | collective-permute-start | bytes 196616 | tf_op jit(solution)/shard_map/ppermute | solution.py:126
  13.3 1.9 %collective-permute-start.2 = (bf16[2,32,512]{2,1,0:T(8,128)(2,1)S(1)}, bf16[2,32,512]{2,1,0:T(8,128)(2,1)S(1)}, u32[]{:S(2)}, u32[]{:S(2)}) collective-permute-start(bf16[2,32,512]{2,1,0:T(8,128)(2,1)S(1)} %get-tuple-element.19), channel_id=1, source_target_pairs={{12,0},{13,1},{14,2},{15,3},{0,4},{1,5},{2,6},{3,7},{4,8},{5,9},{6... | collective-permute-start | bytes 196616 | tf_op jit(solution)/shard_map/ppermute | solution.py:126
  15.3 10.8 %collective-permute-start.1 = (bf16[2,32,512]{2,1,0:T(8,128)(2,1)S(1)}, bf16[2,32,512]{2,1,0:T(8,128)(2,1)S(1)}, u32[]{:S(2)}, u32[]{:S(2)}) collective-permute-start(bf16[2,32,512]{2,1,0:T(8,128)(2,1)S(1)} %get-tuple-element.19), channel_id=1, source_target_pairs={{8,0},{9,1},{10,2},{11,3},{12,4},{13,5},{14,6},{15,7},{0,8},{1,9},... | collective-permute-start | bytes 196616 | tf_op jit(solution)/shard_map/ppermute | solution.py:126
  26.1 0.0 collective-permute-done.2
  26.1 0.7 pad_maximum_fusion.3
  26.8 3.6 %collective-permute-done.1 = bf16[2,32,512]{2,1,0:T(8,128)(2,1)S(1)} collective-permute-done((bf16[2,32,512]{2,1,0:T(8,128)(2,1)S(1)}, bf16[2,32,512]{2,1,0:T(8,128)(2,1)S(1)}, u32[]{:S(2)}, u32[]{:S(2)}) %collective-permute-start.1) | collective-permute-done | bytes 65568 | tf_op jit(solution)/shard_map/ppermute | solution.py:126
  30.5 5.3 %collective-permute-start.4 = (bf16[4,2,32,512]{3,2,1,0:T(8,128)(2,1)S(1)}, bf16[4,2,32,512]{3,2,1,0:T(8,128)(2,1)S(1)}, u32[]{:S(2)}, u32[]{:S(2)}) collective-permute-start(bf16[4,2,32,512]{3,2,1,0:T(8,128)(2,1)S(1)} %pad_maximum_fusion.1.a), channel_id=1, source_target_pairs={{15,0},{0,1},{1,2},{2,3},{3,4},{4,5},{5,6},{6,7},{7,8},{8,9},{9,10... | collective-permute-start | bytes 786440 | tf_op jit(solution)/shard_map/ppermute | solution.py:126
  35.8 1.9 %collective-permute-start.3 = (bf16[4,2,32,512]{3,2,1,0:T(8,128)(2,1)S(1)}, bf16[4,2,32,512]{3,2,1,0:T(8,128)(2,1)S(1)}, u32[]{:S(2)}, u32[]{:S(2)}) collective-permute-start(bf16[4,2,32,512]{3,2,1,0:T(8,128)(2,1)S(1)} %pad_maximum_fusion.1.a), channel_id=1, source_target_pairs={{1,0},{2,1},{3,2},{4,3},{5,4},{6,5},{7,6},{8,7},{9,8},{10,9},{11,1... | collective-permute-start | bytes 786440 | tf_op jit(solution)/shard_map/ppermute | solution.py:126
  37.7 5.6 %collective-permute-start.6 = (bf16[2,2,32,512]{3,2,1,0:T(8,128)(2,1)}, bf16[2,2,32,512]{3,2,1,0:T(8,128)(2,1)S(1)}, u32[]{:S(2)}, u32[]{:S(2)}) collective-permute-start(bf16[2,2,32,512]{3,2,1,0:T(8,128)(2,1)} %get-tuple-element.16), channel_id=1, source_target_pairs={{14,0},{15,1},{0,2},{1,3},{2,4},{3,5},{4,6},{5,7},{6,8},{7,9},{8,1... | collective-permute-start | bytes 393224 | tf_op jit(solution)/shard_map/ppermute | solution.py:126
  43.3 3.8 %collective-permute-start.5 = (bf16[2,2,32,512]{3,2,1,0:T(8,128)(2,1)}, bf16[2,2,32,512]{3,2,1,0:T(8,128)(2,1)}, u32[]{:S(2)}, u32[]{:S(2)}) collective-permute-start(bf16[2,2,32,512]{3,2,1,0:T(8,128)(2,1)} %get-tuple-element.17), channel_id=1, source_target_pairs={{2,0},{3,1},{4,2},{5,3},{6,4},{7,5},{8,6},{9,7},{10,8},{11,9},{12,... | collective-permute-start | bytes 393224 | tf_op jit(solution)/shard_map/ppermute | solution.py:126
  47.2 0.0 copy-start
  47.2 1.3 pad_maximum_fusion.pair
  48.5 0.1 pad_add_fusion.where
  48.6 2.8 %collective-permute-done.6.e = bf16[2,2,32,512]{3,2,1,0:T(8,128)(2,1)S(1)} collective-permute-done((bf16[2,2,32,512]{3,2,1,0:T(8,128)(2,1)}, bf16[2,2,32,512]{3,2,1,0:T(8,128)(2,1)S(1)}, u32[]{:S(2)}, u32[]{:S(2)}) %collective-permute-start.6) | collective-permute-done | bytes 131104 | tf_op jit(solution)/shard_map/ppermute | solution.py:126
  51.5 1.1 collective-permute-done.5.d
  52.5 0.0 collective-permute-done.4.c
  52.5 1.9 %shard_map.84 = (f32[16,16,1664]{2,1,0:T(8,128)S(1)}, f32[16,16,832]{2,1,0:T(8,128)S(1)}) custom-call(s32[2]{0:T(128)S(1)} %pad_add_fusion.where, bf16[4,2,32,512]{3,2,1,0:T(8,128)(2,1)S(1)} %pad_maximum_fusion.1.a, bf16[4,2,32,512]{3,2,1,0:T(8,128)(2,1)S(1)} %collective-permute-done.3.b, bf16[4,2,32,512]{3,2,1,0:T(8,128)(2,1)S(1)} %collective-permute-done.4.c, ...), custom_call_target="tpu_custom_call" | custom-call | flops 654311424 | bytes 6160392 | tf_op jit(solution)/shard_map/pallas_call | solution.py:33
  54.4 1.9 %collective-permute-start.7 = (f32[16,16,1664]{2,1,0:T(8,128)S(1)}, f32[16,16,1664]{2,1,0:T(8,128)S(1)}, u32[]{:S(2)}, u32[]{:S(2)}) collective-permute-start(f32[16,16,1664]{2,1,0:T(8,128)S(1)} %get-tuple-element.10), channel_id=1, source_target_pairs={{0,16},{16,0},{1,17},{17,1},{2,18},{18,2},{3,19},{19,3},{4,20},{20... | collective-permute-start | bytes 5111816 | tf_op jit(solution)/shard_map/ppermute | solution.py:122
  56.3 2.4 %collective-permute-start.8 = (f32[16,16,832]{2,1,0:T(8,128)S(1)}, f32[16,16,832]{2,1,0:T(8,128)S(1)}, u32[]{:S(2)}, u32[]{:S(2)}) collective-permute-start(f32[16,16,832]{2,1,0:T(8,128)S(1)} %get-tuple-element.11), channel_id=1, source_target_pairs={{0,16},{16,0},{1,17},{17,1},{2,18},{18,2},{3,19},{19,3},{4,20},{20... | collective-permute-start | bytes 2555912 | tf_op jit(solution)/shard_map/ppermute | solution.py:122
  58.8 2.5 %collective-permute-done.8.got_down = f32[16,16,832]{2,1,0:T(8,128)S(1)} collective-permute-done((f32[16,16,832]{2,1,0:T(8,128)S(1)}, f32[16,16,832]{2,1,0:T(8,128)S(1)}, u32[]{:S(2)}, u32[]{:S(2)}) %collective-permute-start.8) | collective-permute-done | bytes 852000 | tf_op jit(solution)/shard_map/ppermute | solution.py:122
  61.2 0.0 collective-permute-done.7.got_pair
  61.2 1.9 %shard_map.85 = bf16[16,16,2496]{2,1,0:T(8,128)(2,1)S(1)} custom-call(s32[2]{0:T(128)S(1)} %pad_add_fusion.where, bf16[4,2,32,512]{3,2,1,0:T(8,128)(2,1)S(1)} %pad_maximum_fusion.1.a, bf16[4,2,32,512]{3,2,1,0:T(8,128)(2,1)S(1)} %collective-permute-done.3.b, bf16[4,2,32,512]{3,2,1,0:T(8,128)(2,1)S(1)} %collective-permute-done.4.c, ...), custom_call_target="tpu_custom_call" | custom-call | flops 654311424 | bytes 7438344 | tf_op jit(solution)/shard_map/pallas_call | solution.py:33
  63.1 26.8 %all_to_all.15.parts = bf16[16,16,2496]{2,1,0:T(8,128)(2,1)S(1)} all-to-all(bf16[16,16,2496]{2,1,0:T(8,128)(2,1)S(1)} %shard_map.85), channel_id=1, replica_groups=mesh['x'=4,'y'=4,'core'=2,'col'=16] {'x','y'}, dimensions={0} | all-to-all | bytes 2555904 | tf_op jit(solution)/shard_map/all_to_all | solution.py:160
  89.9 0.3 shard_map.86
  90.2 22.3 %all_to_all.16.deltas.own = bf16[16,16,2496]{2,1,0:T(8,128)(2,1)S(1)} all-to-all(bf16[16,16,2496]{2,1,0:T(8,128)(2,1)S(1)} %shard_map.86), channel_id=1, replica_groups=mesh['x'=4,'y'=4,'core'=2,'col'=16] {'x','y'}, dimensions={0} | all-to-all | bytes 2555904 | tf_op jit(solution)/shard_map/all_to_all | solution.py:162
  112.5 1.9 %collective-permute-start.9 = (bf16[16,16,2496]{2,1,0:T(8,128)(2,1)S(1)}, bf16[16,16,2496]{2,1,0:T(8,128)(2,1)S(1)}, u32[]{:S(2)}, u32[]{:S(2)}) collective-permute-start(bf16[16,16,2496]{2,1,0:T(8,128)(2,1)S(1)} %all_to_all.16.deltas.own), channel_id=1, source_target_pairs={{0,16},{16,0},{1,17},{17,1},{2,18},{18,2},{3,19},{19,3},{4,20},{20... | collective-permute-start | bytes 3833864 | tf_op jit(solution)/shard_map/ppermute | solution.py:122
  114.4 0.6 shard_map.87.own
  115.1 2.4 %collective-permute-done.9.deltas.other = bf16[16,16,2496]{2,1,0:T(8,128)(2,1)S(1)} collective-permute-done((bf16[16,16,2496]{2,1,0:T(8,128)(2,1)S(1)}, bf16[16,16,2496]{2,1,0:T(8,128)(2,1)S(1)}, u32[]{:S(2)}, u32[]{:S(2)}) %collective-permute-start.9) | collective-permute-done | bytes 1277984 | tf_op jit(solution)/shard_map/ppermute | solution.py:122
  117.4 1.2 shard_map.88
  118.6 40.5 %all_to_all.17.pieces = bf16[16,32,512]{2,1,0:T(8,128)(2,1)S(1)} all-to-all(bf16[16,32,512]{2,1,0:T(8,128)(2,1)S(1)} %shard_map.88), channel_id=1, replica_groups=mesh['x'=4,'y'=4,'core'=2,'col'=16] {'col'}, dimensions={0} | all-to-all | bytes 1048576 | tf_op jit(solution)/shard_map/all_to_all | solution.py:168
  159.1 3.4 %shard_map.89 = (bf16[32,512]{1,0:T(8,128)(2,1)}, bf16[832,512]{1,0:T(8,128)(2,1)}, bf16[832,512]{1,0:T(8,128)(2,1)}, bf16[832,512]{1,0:T(8,128)(2,1)}) custom-call(s32[2]{0:T(128)S(1)} %pad_add_fusion.where, bf16[4,2,32,512]{3,2,1,0:T(8,128)(2,1)S(1)} %pad_maximum_fusion.1.a, bf16[4,2,32,512]{3,2,1,0:T(8,128)(2,1)S(1)} %collective-permute-done.3.b, ...), custom_call_target="tpu_custom_call" | custom-call | flops 1308622848 | bytes 6717448 | tf_op jit(solution)/shard_map/pallas_call | solution.py:33
  (6 shorter events, 0.0 us)
Async XLA Ops:
  0.6 46.5 %copy-start.1 = (bf16[512,832]{0,1:T(8,128)(2,1)S(1)}, bf16[512,832]{0,1:T(8,128)(2,1)}, u32[]{:S(2)}) copy-start(bf16[512,832]{0,1:T(8,128)(2,1)} %param.8) | copy-start | bytes 2555908
  1.5 24.6 %collective-permute-start = (bf16[2,32,512]{2,1,0:T(8,128)(2,1)S(1)}, bf16[2,32,512]{2,1,0:T(8,128)(2,1)S(1)}, u32[]{:S(2)}, u32[]{:S(2)}) collective-permute-start(bf16[2,32,512]{2,1,0:T(8,128)(2,1)S(1)} %get-tuple-element.19), channel_id=1, source_target_pairs={{4,0},{5,1},{6,2},{7,3},{8,4},{9,5},{10,6},{11,7},{12,8},{13,9},{1... | collective-permute-start | bytes 196616 | tf_op jit(solution)/shard_map/ppermute | solution.py:126
  13.3 12.8 %collective-permute-start.2 = (bf16[2,32,512]{2,1,0:T(8,128)(2,1)S(1)}, bf16[2,32,512]{2,1,0:T(8,128)(2,1)S(1)}, u32[]{:S(2)}, u32[]{:S(2)}) collective-permute-start(bf16[2,32,512]{2,1,0:T(8,128)(2,1)S(1)} %get-tuple-element.19), channel_id=1, source_target_pairs={{12,0},{13,1},{14,2},{15,3},{0,4},{1,5},{2,6},{3,7},{4,8},{5,9},{6... | collective-permute-start | bytes 196616 | tf_op jit(solution)/shard_map/ppermute | solution.py:126
  15.3 15.2 %collective-permute-start.1 = (bf16[2,32,512]{2,1,0:T(8,128)(2,1)S(1)}, bf16[2,32,512]{2,1,0:T(8,128)(2,1)S(1)}, u32[]{:S(2)}, u32[]{:S(2)}) collective-permute-start(bf16[2,32,512]{2,1,0:T(8,128)(2,1)S(1)} %get-tuple-element.19), channel_id=1, source_target_pairs={{8,0},{9,1},{10,2},{11,3},{12,4},{13,5},{14,6},{15,7},{0,8},{1,9},... | collective-permute-start | bytes 196616 | tf_op jit(solution)/shard_map/ppermute | solution.py:126
  30.5 22.0 %collective-permute-start.4 = (bf16[4,2,32,512]{3,2,1,0:T(8,128)(2,1)S(1)}, bf16[4,2,32,512]{3,2,1,0:T(8,128)(2,1)S(1)}, u32[]{:S(2)}, u32[]{:S(2)}) collective-permute-start(bf16[4,2,32,512]{3,2,1,0:T(8,128)(2,1)S(1)} %pad_maximum_fusion.1.a), channel_id=1, source_target_pairs={{15,0},{0,1},{1,2},{2,3},{3,4},{4,5},{5,6},{6,7},{7,8},{8,9},{9,10... | collective-permute-start | bytes 786440 | tf_op jit(solution)/shard_map/ppermute | solution.py:126
  35.8 16.8 %collective-permute-start.3 = (bf16[4,2,32,512]{3,2,1,0:T(8,128)(2,1)S(1)}, bf16[4,2,32,512]{3,2,1,0:T(8,128)(2,1)S(1)}, u32[]{:S(2)}, u32[]{:S(2)}) collective-permute-start(bf16[4,2,32,512]{3,2,1,0:T(8,128)(2,1)S(1)} %pad_maximum_fusion.1.a), channel_id=1, source_target_pairs={{1,0},{2,1},{3,2},{4,3},{5,4},{6,5},{7,6},{8,7},{9,8},{10,9},{11,1... | collective-permute-start | bytes 786440 | tf_op jit(solution)/shard_map/ppermute | solution.py:126
  37.7 13.7 %collective-permute-start.6 = (bf16[2,2,32,512]{3,2,1,0:T(8,128)(2,1)}, bf16[2,2,32,512]{3,2,1,0:T(8,128)(2,1)S(1)}, u32[]{:S(2)}, u32[]{:S(2)}) collective-permute-start(bf16[2,2,32,512]{3,2,1,0:T(8,128)(2,1)} %get-tuple-element.16), channel_id=1, source_target_pairs={{14,0},{15,1},{0,2},{1,3},{2,4},{3,5},{4,6},{5,7},{6,8},{7,9},{8,1... | collective-permute-start | bytes 393224 | tf_op jit(solution)/shard_map/ppermute | solution.py:126
  43.3 9.2 %collective-permute-start.5 = (bf16[2,2,32,512]{3,2,1,0:T(8,128)(2,1)}, bf16[2,2,32,512]{3,2,1,0:T(8,128)(2,1)}, u32[]{:S(2)}, u32[]{:S(2)}) collective-permute-start(bf16[2,2,32,512]{3,2,1,0:T(8,128)(2,1)} %get-tuple-element.17), channel_id=1, source_target_pairs={{2,0},{3,1},{4,2},{5,3},{6,4},{7,5},{8,6},{9,7},{10,8},{11,9},{12,... | collective-permute-start | bytes 393224 | tf_op jit(solution)/shard_map/ppermute | solution.py:126
  47.2 5.4 %copy-start = (bf16[832,512]{1,0:T(8,128)(2,1)S(1)}, bf16[832,512]{1,0:T(8,128)(2,1)}, u32[]{:S(2)}) copy-start(bf16[832,512]{1,0:T(8,128)(2,1)} %down.3) | copy-start | bytes 2555908
  54.4 6.8 %collective-permute-start.7 = (f32[16,16,1664]{2,1,0:T(8,128)S(1)}, f32[16,16,1664]{2,1,0:T(8,128)S(1)}, u32[]{:S(2)}, u32[]{:S(2)}) collective-permute-start(f32[16,16,1664]{2,1,0:T(8,128)S(1)} %get-tuple-element.10), channel_id=1, source_target_pairs={{0,16},{16,0},{1,17},{17,1},{2,18},{18,2},{3,19},{19,3},{4,20},{20... | collective-permute-start | bytes 5111816 | tf_op jit(solution)/shard_map/ppermute | solution.py:122
  56.3 4.9 %collective-permute-start.8 = (f32[16,16,832]{2,1,0:T(8,128)S(1)}, f32[16,16,832]{2,1,0:T(8,128)S(1)}, u32[]{:S(2)}, u32[]{:S(2)}) collective-permute-start(f32[16,16,832]{2,1,0:T(8,128)S(1)} %get-tuple-element.11), channel_id=1, source_target_pairs={{0,16},{16,0},{1,17},{17,1},{2,18},{18,2},{3,19},{19,3},{4,20},{20... | collective-permute-start | bytes 2555912 | tf_op jit(solution)/shard_map/ppermute | solution.py:122
  112.5 4.9 %collective-permute-start.9 = (bf16[16,16,2496]{2,1,0:T(8,128)(2,1)S(1)}, bf16[16,16,2496]{2,1,0:T(8,128)(2,1)S(1)}, u32[]{:S(2)}, u32[]{:S(2)}) collective-permute-start(bf16[16,16,2496]{2,1,0:T(8,128)(2,1)S(1)} %all_to_all.16.deltas.own), channel_id=1, source_target_pairs={{0,16},{16,0},{1,17},{17,1},{2,18},{18,2},{3,19},{19,3},{4,20},{20... | collective-permute-start | bytes 3833864 | tf_op jit(solution)/shard_map/ppermute | solution.py:122

commit v6 on v5

--- a/solution.py
+++ b/solution.py
@@ -66,7 +66,7 @@
         out[:, :, lanes] = (total + got[...]).astype(BF16)
 
 
-def middle_body(parts, out):
+def middle_body(parts, deltas, hidden):
     units = parts.shape[2] // 3
     total = parts[0].astype(F32)
     for i in range(1, parts.shape[0]):
@@ -74,8 +74,11 @@
     hid, gate_delta, up_delta = nonlinear(
         total[:, :units], total[:, units : 2 * units], total[:, 2 * units :]
     )
-    row = jnp.concatenate([gate_delta, up_delta, hid], 1)
-    out[...] = jnp.broadcast_to(row[None], out.shape)
+    hidden[:, :units] = hid.astype(hidden.dtype)
+    if parts.shape[2] // 3 > units:
+        hidden[:, units:] = jnp.zeros_like(hidden[:, units:])
+    row = jnp.concatenate([gate_delta, up_delta], 1)
+    deltas[...] = jnp.broadcast_to(row[None], deltas.shape)
 
 
 def part_of(deltas, pair):
@@ -99,11 +102,7 @@
                 out[device] = part[start : start + tokens]
 
 
-def grads_body(where, a, b, c, d, e, own, other, pieces, input_out, gate_out, up_out, down_out):
-    total = pieces[0].astype(F32)
-    for i in range(1, pieces.shape[0]):
-        total += pieces[i].astype(F32)
-    input_out[...] = total.astype(BF16)
+def grads_body(where, a, b, c, d, e, own, other, gate_out, up_out):
     units = gate_out.shape[0]
     deltas = [ref[...].reshape(-1, ref.shape[-1]) for ref in (own, other)]
 
@@ -115,7 +114,16 @@
     pair = total_of(0, slice(0, 2 * units))
     gate_out[...] = pair[:units]
     up_out[...] = pair[units:]
-    down_out[...] = total_of(1, slice(2 * units, 3 * units))
+
+
+def down_body(where, a, b, c, d, e, hidden, out):
+    units = out.shape[0]
+    total = jnp.zeros(out.shape, F32)
+    for half in range(2):
+        rows = half_rows(half, 1, (a, b, c), d, e)
+        left = hidden[:, half, :, :units].astype(BF16).reshape(rows.shape[0], units)
+        total += contract(left, rows, 0, 0)
+    out[...] = total.astype(BF16)
 
 
 def swap_cores(value):
@@ -158,7 +166,13 @@
         keep_body, sds((n, half // n, 3 * units), BF16), 3 * flops, where, *held, pair, down_weight, *sent
     )
     parts = lax.all_to_all(parts, XY, 0, 0)
-    row = call(middle_body, sds(parts.shape, BF16), 40 * half // n * units, parts)
+    row, hidden = call(
+        middle_body,
+        (sds((n, half // n, 2 * units), BF16), sds((half // n, 1024), F32)),
+        40 * half // n * units,
+        parts,
+    )
+    hidden = lax.all_gather(hidden, ("x", "y", "core"), axis=0)
     own = lax.all_to_all(row, XY, 0, 0)
     other = swap_cores(own)
     own_part = call(own_body, sds((half, width), BF16), 2 * flops, own, pair)
@@ -167,16 +181,18 @@
     )
     pieces = lax.all_to_all(pieces, "col", 0, 0)
     grad = sds((units, width), BF16)
-    input_grad, gate_grad, up_grad, down_grad = call(
+    input_grad = jnp.sum(pieces.astype(F32), axis=0).astype(BF16)
+    gate_grad, up_grad = call(
         grads_body,
-        (sds((tokens, width), BF16), grad, grad, grad),
+        (grad, grad),
         6 * flops,
         where,
         *held,
         own,
         other,
-        pieces,
-    )
+    )
+    hidden = hidden.reshape(n, 2, half // n, -1)
+    down_grad = call(down_body, grad, 2 * flops, where, *held, hidden)
     return (input_grad, gate_grad.T, up_grad.T, down_grad)
 
 

time: 163 us -> 176 us (1.080)
  blocking collectives: 89.6 us -> 44.4 us
  waiting for transfers between devices: 12.4 us -> 36.9 us
  between operations: 0.81 us -> 14.2 us
  starting transfers between devices: 47.5 us -> 58.9 us
  local copies, waits for them, and re-layouts: 0.01 us -> 5.34 us
  Pallas kernels: 9.22 us -> 11.8 us
    all_to_all x1 -> x0, blocking collectives: 40.5 us -> none  [per_device(): pieces = lax.all_to_all(pieces, 'col', 0, 0)]
    all_to_all x0 -> x1, waiting for transfers between devices: none -> 25.2 us  [per_device(): pieces = lax.all_to_all(pieces, 'col', 0, 0)]
    all_to_all x0 -> x1, starting transfers between devices: none -> 11.4 us  [per_device(): pieces = lax.all_to_all(pieces, 'col', 0, 0)]
    unnamed x4 -> x14, local copies, waits for them, and re-layouts: 0.01 us -> 5.34 us
    all_to_all x1, blocking collectives: 22.3 us -> 17.6 us  [per_device(): own = lax.all_to_all(row, XY, 0, 0)]
    pallas_call x6 -> x7, Pallas kernels: 9.22 us -> 11.8 us  [call(): pl.pallas_call(body, out_shape=outs, in_specs=[SMEM if a.dtype == jnp.int...]
  transfers between devices with their start and end apart: 10 -> 12, of which waited for: 5 -> 6; matrix products, arithmetic and copies ran while one was open for 1% -> 2% of each run, Pallas kernels for 0% -> 3%
where the time goes in v6:
time: 176 us; the launch traced here: 175 us
  starting transfers between devices  58.9 us (33%)
  blocking collectives  44.4 us (25%)
  waiting for transfers between devices  36.9 us (21%)
  between operations  14.2 us (8%)
  Pallas kernels  11.8 us (7%)
  local copies, waits for them, and re-layouts  5.34 us (3%)
  other arithmetic  3.73 us (2%)
    ppermute x7, starting transfers between devices, shift(): return lax.ppermute(value, 'col', [((i + by) % 16, i) for i in range(16)])  41.2 us
    all_to_all x1, blocking collectives, per_device(): parts = lax.all_to_all(parts, XY, 0, 0)  26.8 us
    all_to_all x1, waiting for transfers between devices, per_device(): pieces = lax.all_to_all(pieces, 'col', 0, 0)  25.2 us
    all_to_all x1, blocking collectives, per_device(): own = lax.all_to_all(row, XY, 0, 0)  17.6 us
    pallas_call x7, Pallas kernels, call(): pl.pallas_call(body, out_shape=outs, in_specs=[SMEM if a.dtype == jnp.int...  11.8 us
    all_to_all x1, starting transfers between devices, per_device(): pieces = lax.all_to_all(pieces, 'col', 0, 0)  11.4 us
    ppermute x7, waiting for transfers between devices, shift(): return lax.ppermute(value, 'col', [((i + by) % 16, i) for i in range(16)])  7.53 us
    ppermute x3, starting transfers between devices, swap_cores(): return lax.ppermute(value, 'core', [(0, 1), (1, 0)])  6.24 us
  transfers between devices with their start and end apart: 12, of which 6 were waited for; matrix products, arithmetic and copies ran while one was open for 2% of the time, Pallas kernels for 3%

profile of v6, /device:TPU:32, one launch (start us, length us, event | category | flops | bytes accessed | tf_op | source)
XLA Modules:
  0.0 175.2 jit_solution(10897327900827508371)
XLA Ops:
  7.2 0.9 fusion
  8.1 11.8 %collective-permute-start = (bf16[2,32,512]{2,1,0:T(8,128)(2,1)S(1)}, bf16[2,32,512]{2,1,0:T(8,128)(2,1)S(1)}, u32[]{:S(2)}, u32[]{:S(2)}) collective-permute-start(bf16[2,32,512]{2,1,0:T(8,128)(2,1)S(1)} %get-tuple-element.19), channel_id=1, source_target_pairs={{4,0},{5,1},{6,2},{7,3},{8,4},{9,5},{10,6},{11,7},{12,8},{13,9},{1... | collective-permute-start | bytes 196616 | tf_op jit(solution)/shard_map/ppermute | solution.py:134
  19.9 1.9 %collective-permute-start.2 = (bf16[2,32,512]{2,1,0:T(8,128)(2,1)S(1)}, bf16[2,32,512]{2,1,0:T(8,128)(2,1)S(1)}, u32[]{:S(2)}, u32[]{:S(2)}) collective-permute-start(bf16[2,32,512]{2,1,0:T(8,128)(2,1)S(1)} %get-tuple-element.19), channel_id=1, source_target_pairs={{12,0},{13,1},{14,2},{15,3},{0,4},{1,5},{2,6},{3,7},{4,8},{5,9},{6... | collective-permute-start | bytes 196616 | tf_op jit(solution)/shard_map/ppermute | solution.py:134
  21.9 10.8 %collective-permute-start.1 = (bf16[2,32,512]{2,1,0:T(8,128)(2,1)S(1)}, bf16[2,32,512]{2,1,0:T(8,128)(2,1)S(1)}, u32[]{:S(2)}, u32[]{:S(2)}) collective-permute-start(bf16[2,32,512]{2,1,0:T(8,128)(2,1)S(1)} %get-tuple-element.19), channel_id=1, source_target_pairs={{8,0},{9,1},{10,2},{11,3},{12,4},{13,5},{14,6},{15,7},{0,8},{1,9},... | collective-permute-start | bytes 196616 | tf_op jit(solution)/shard_map/ppermute | solution.py:134
  33.4 3.6 %collective-permute-done.1 = bf16[2,32,512]{2,1,0:T(8,128)(2,1)S(1)} collective-permute-done((bf16[2,32,512]{2,1,0:T(8,128)(2,1)S(1)}, bf16[2,32,512]{2,1,0:T(8,128)(2,1)S(1)}, u32[]{:S(2)}, u32[]{:S(2)}) %collective-permute-start.1) | collective-permute-done | bytes 65568 | tf_op jit(solution)/shard_map/ppermute | solution.py:134
  37.1 5.3 %collective-permute-start.4 = (bf16[4,2,32,512]{3,2,1,0:T(8,128)(2,1)S(1)}, bf16[4,2,32,512]{3,2,1,0:T(8,128)(2,1)S(1)}, u32[]{:S(2)}, u32[]{:S(2)}) collective-permute-start(bf16[4,2,32,512]{3,2,1,0:T(8,128)(2,1)S(1)} %pad_maximum_fusion.1.a), channel_id=1, source_target_pairs={{15,0},{0,1},{1,2},{2,3},{3,4},{4,5},{5,6},{6,7},{7,8},{8,9},{9,10... | collective-permute-start | bytes 786440 | tf_op jit(solution)/shard_map/ppermute | solution.py:134
  42.4 1.9 %collective-permute-start.3 = (bf16[4,2,32,512]{3,2,1,0:T(8,128)(2,1)S(1)}, bf16[4,2,32,512]{3,2,1,0:T(8,128)(2,1)S(1)}, u32[]{:S(2)}, u32[]{:S(2)}) collective-permute-start(bf16[4,2,32,512]{3,2,1,0:T(8,128)(2,1)S(1)} %pad_maximum_fusion.1.a), channel_id=1, source_target_pairs={{1,0},{2,1},{3,2},{4,3},{5,4},{6,5},{7,6},{8,7},{9,8},{10,9},{11,1... | collective-permute-start | bytes 786440 | tf_op jit(solution)/shard_map/ppermute | solution.py:134
  44.3 5.6 %collective-permute-start.6 = (bf16[2,2,32,512]{3,2,1,0:T(8,128)(2,1)}, bf16[2,2,32,512]{3,2,1,0:T(8,128)(2,1)S(1)}, u32[]{:S(2)}, u32[]{:S(2)}) collective-permute-start(bf16[2,2,32,512]{3,2,1,0:T(8,128)(2,1)} %get-tuple-element.16), channel_id=1, source_target_pairs={{14,0},{15,1},{0,2},{1,3},{2,4},{3,5},{4,6},{5,7},{6,8},{7,9},{8,1... | collective-permute-start | bytes 393224 | tf_op jit(solution)/shard_map/ppermute | solution.py:134
  49.9 3.8 %collective-permute-start.5 = (bf16[2,2,32,512]{3,2,1,0:T(8,128)(2,1)}, bf16[2,2,32,512]{3,2,1,0:T(8,128)(2,1)}, u32[]{:S(2)}, u32[]{:S(2)}) collective-permute-start(bf16[2,2,32,512]{3,2,1,0:T(8,128)(2,1)} %get-tuple-element.17), channel_id=1, source_target_pairs={{2,0},{3,1},{4,2},{5,3},{6,4},{7,5},{8,6},{9,7},{10,8},{11,9},{12,... | collective-permute-start | bytes 393224 | tf_op jit(solution)/shard_map/ppermute | solution.py:134
  53.8 1.3 pad_maximum_fusion.pair
  55.2 2.8 %collective-permute-done.6.e = bf16[2,2,32,512]{3,2,1,0:T(8,128)(2,1)S(1)} collective-permute-done((bf16[2,2,32,512]{3,2,1,0:T(8,128)(2,1)}, bf16[2,2,32,512]{3,2,1,0:T(8,128)(2,1)S(1)}, u32[]{:S(2)}, u32[]{:S(2)}) %collective-permute-start.6) | collective-permute-done | bytes 131104 | tf_op jit(solution)/shard_map/ppermute | solution.py:134
  58.0 1.1 collective-permute-done.5.d
  59.1 1.9 %shard_map.84 = (f32[16,16,1664]{2,1,0:T(8,128)S(1)}, f32[16,16,832]{2,1,0:T(8,128)S(1)}) custom-call(s32[2]{0:T(128)S(1)} %pad_add_fusion.where, bf16[4,2,32,512]{3,2,1,0:T(8,128)(2,1)S(1)} %pad_maximum_fusion.1.a, bf16[4,2,32,512]{3,2,1,0:T(8,128)(2,1)S(1)} %collective-permute-done.3.b, bf16[4,2,32,512]{3,2,1,0:T(8,128)(2,1)S(1)} %collective-permute-done.4.c, ...), custom_call_target="tpu_custom_call" | custom-call | flops 654311424 | bytes 6160392 | tf_op jit(solution)/shard_map/pallas_call | solution.py:33
  61.0 1.9 %collective-permute-start.7 = (f32[16,16,1664]{2,1,0:T(8,128)S(1)}, f32[16,16,1664]{2,1,0:T(8,128)S(1)}, u32[]{:S(2)}, u32[]{:S(2)}) collective-permute-start(f32[16,16,1664]{2,1,0:T(8,128)S(1)} %get-tuple-element.10), channel_id=1, source_target_pairs={{0,16},{16,0},{1,17},{17,1},{2,18},{18,2},{3,19},{19,3},{4,20},{20... | collective-permute-start | bytes 5111816 | tf_op jit(solution)/shard_map/ppermute | solution.py:130
  62.9 2.4 %collective-permute-start.8 = (f32[16,16,832]{2,1,0:T(8,128)S(1)}, f32[16,16,832]{2,1,0:T(8,128)S(1)}, u32[]{:S(2)}, u32[]{:S(2)}) collective-permute-start(f32[16,16,832]{2,1,0:T(8,128)S(1)} %get-tuple-element.11), channel_id=1, source_target_pairs={{0,16},{16,0},{1,17},{17,1},{2,18},{18,2},{3,19},{19,3},{4,20},{20... | collective-permute-start | bytes 2555912 | tf_op jit(solution)/shard_map/ppermute | solution.py:130
  65.3 2.5 %collective-permute-done.8.got_down = f32[16,16,832]{2,1,0:T(8,128)S(1)} collective-permute-done((f32[16,16,832]{2,1,0:T(8,128)S(1)}, f32[16,16,832]{2,1,0:T(8,128)S(1)}, u32[]{:S(2)}, u32[]{:S(2)}) %collective-permute-start.8) | collective-permute-done | bytes 852000 | tf_op jit(solution)/shard_map/ppermute | solution.py:130
  67.8 1.9 %shard_map.85 = bf16[16,16,2496]{2,1,0:T(8,128)(2,1)S(1)} custom-call(s32[2]{0:T(128)S(1)} %pad_add_fusion.where, bf16[4,2,32,512]{3,2,1,0:T(8,128)(2,1)S(1)} %pad_maximum_fusion.1.a, bf16[4,2,32,512]{3,2,1,0:T(8,128)(2,1)S(1)} %collective-permute-done.3.b, bf16[4,2,32,512]{3,2,1,0:T(8,128)(2,1)S(1)} %collective-permute-done.4.c, ...), custom_call_target="tpu_custom_call" | custom-call | flops 654311424 | bytes 7438344 | tf_op jit(solution)/shard_map/pallas_call | solution.py:33
  69.7 26.8 %all_to_all.15.parts = bf16[16,16,2496]{2,1,0:T(8,128)(2,1)S(1)} all-to-all(bf16[16,16,2496]{2,1,0:T(8,128)(2,1)S(1)} %shard_map.85), channel_id=1, replica_groups=mesh['x'=4,'y'=4,'core'=2,'col'=16] {'x','y'}, dimensions={0} | all-to-all | bytes 2555904 | tf_op jit(solution)/shard_map/all_to_all | solution.py:168
  96.5 0.8 shard_map.86
  97.3 0.9 copy-done.5
  98.2 17.6 %all_to_all.16.deltas.own = bf16[16,16,1664]{2,1,0:T(8,128)(2,1)S(1)} all-to-all(bf16[16,16,1664]{2,1,0:T(8,128)(2,1)} %copy-done.5), channel_id=1, replica_groups=mesh['x'=4,'y'=4,'core'=2,'col'=16] {'x','y'}, dimensions={0} | all-to-all | bytes 1703936 | tf_op jit(solution)/shard_map/all_to_all | solution.py:176
  115.8 1.9 %collective-permute-start.9 = (bf16[16,16,1664]{2,1,0:T(8,128)(2,1)S(1)}, bf16[16,16,1664]{2,1,0:T(8,128)(2,1)S(1)}, u32[]{:S(2)}, u32[]{:S(2)}) collective-permute-start(bf16[16,16,1664]{2,1,0:T(8,128)(2,1)S(1)} %all_to_all.16.deltas.own), channel_id=1, source_target_pairs={{0,16},{16,0},{1,17},{17,1},{2,18},{18,2},{3,19},{19,3},{4,20},{20... | collective-permute-start | bytes 2555912 | tf_op jit(solution)/shard_map/ppermute | solution.py:130
  118.4 1.7 collective-permute-done.9.deltas.other
  120.1 1.2 shard_map.88
  121.2 0.8 copy-done.2
  122.0 0.9 copy-done.3
  122.9 11.4 %all-to-all-start.2 = ((bf16[16,32,512]{2,1,0:T(8,128)(2,1)}), bf16[16,32,512]{2,1,0:T(8,128)(2,1)S(1)}, u32[]{:S(2)}, u32[]{:S(2)}) async-start(bf16[16,32,512]{2,1,0:T(8,128)(2,1)} %copy-done.2), calls=%async_computation.2 | async-start | bytes 1048576 | tf_op jit(solution)/shard_map/all_to_all | solution.py:182
  134.3 1.1 copy-done.4
  135.5 3.0 %shard_map.89 = (bf16[832,512]{1,0:T(8,128)(2,1)}, bf16[832,512]{1,0:T(8,128)(2,1)}) custom-call(s32[2]{0:T(128)S(1)} %pad_add_fusion.where, bf16[4,2,32,512]{3,2,1,0:T(8,128)(2,1)S(1)} %pad_maximum_fusion.1.a, bf16[4,2,32,512]{3,2,1,0:T(8,128)(2,1)S(1)} %collective-permute-done.3.b, bf16[4,2,32,512]{3,2,1,0:T(8,128)(2,1)S(1)} %collective-permute-done.4.c, ...), custom_call_target="tpu_custom_call" | custom-call | flops 1308622848 | bytes 4456456 | tf_op jit(solution)/shard_map/pallas_call | solution.py:33
  138.4 25.2 %all-to-all-done.2 = bf16[16,32,512]{2,1,0:T(8,128)(2,1)S(1)} async-done(((bf16[16,32,512]{2,1,0:T(8,128)(2,1)}), bf16[16,32,512]{2,1,0:T(8,128)(2,1)S(1)}, u32[]{:S(2)}, u32[]{:S(2)}) %all-to-all-start.2) | async-done | bytes 524320 | tf_op jit(solution)/shard_map/all_to_all | solution.py:182
  164.3 1.6 copy-done.1
  165.9 2.5 %shard_map.90 = bf16[832,512]{1,0:T(8,128)(2,1)} custom-call(s32[2]{0:T(128)S(1)} %pad_add_fusion.where, bf16[4,2,32,512]{3,2,1,0:T(8,128)(2,1)S(1)} %pad_maximum_fusion.1.a, bf16[4,2,32,512]{3,2,1,0:T(8,128)(2,1)S(1)} %collective-permute-done.3.b, bf16[4,2,32,512]{3,2,1,0:T(8,128)(2,1)S(1)} %collective-permute-done.4.c, ...), custom_call_target="tpu_custom_call" | custom-call | flops 436207616 | bytes 3997704 | tf_op jit(solution)/shard_map/pallas_call | solution.py:33
  (22 shorter events, 2.2 us)
Async XLA Ops:
  7.2 157.1 %all-gather.3.cloned.1.call-start = ((), (), s32[]{:S(2)}) async-start(), calls=%async_computation.3 | async-start | bytes 2162688 | tf_op jit(solution)/shard_map/all_gather | solution.py:175
  7.2 46.5 %copy-start.6 = (bf16[512,832]{0,1:T(8,128)(2,1)S(1)}, bf16[512,832]{0,1:T(8,128)(2,1)}, u32[]{:S(2)}) copy-start(bf16[512,832]{0,1:T(8,128)(2,1)} %param.8) | copy-start | bytes 2555908
  8.1 24.6 %collective-permute-start = (bf16[2,32,512]{2,1,0:T(8,128)(2,1)S(1)}, bf16[2,32,512]{2,1,0:T(8,128)(2,1)S(1)}, u32[]{:S(2)}, u32[]{:S(2)}) collective-permute-start(bf16[2,32,512]{2,1,0:T(8,128)(2,1)S(1)} %get-tuple-element.19), channel_id=1, source_target_pairs={{4,0},{5,1},{6,2},{7,3},{8,4},{9,5},{10,6},{11,7},{12,8},{13,9},{1... | collective-permute-start | bytes 196616 | tf_op jit(solution)/shard_map/ppermute | solution.py:134
  19.9 12.8 %collective-permute-start.2 = (bf16[2,32,512]{2,1,0:T(8,128)(2,1)S(1)}, bf16[2,32,512]{2,1,0:T(8,128)(2,1)S(1)}, u32[]{:S(2)}, u32[]{:S(2)}) collective-permute-start(bf16[2,32,512]{2,1,0:T(8,128)(2,1)S(1)} %get-tuple-element.19), channel_id=1, source_target_pairs={{12,0},{13,1},{14,2},{15,3},{0,4},{1,5},{2,6},{3,7},{4,8},{5,9},{6... | collective-permute-start | bytes 196616 | tf_op jit(solution)/shard_map/ppermute | solution.py:134
  21.9 15.2 %collective-permute-start.1 = (bf16[2,32,512]{2,1,0:T(8,128)(2,1)S(1)}, bf16[2,32,512]{2,1,0:T(8,128)(2,1)S(1)}, u32[]{:S(2)}, u32[]{:S(2)}) collective-permute-start(bf16[2,32,512]{2,1,0:T(8,128)(2,1)S(1)} %get-tuple-element.19), channel_id=1, source_target_pairs={{8,0},{9,1},{10,2},{11,3},{12,4},{13,5},{14,6},{15,7},{0,8},{1,9},... | collective-permute-start | bytes 196616 | tf_op jit(solution)/shard_map/ppermute | solution.py:134
  37.1 22.0 %collective-permute-start.4 = (bf16[4,2,32,512]{3,2,1,0:T(8,128)(2,1)S(1)}, bf16[4,2,32,512]{3,2,1,0:T(8,128)(2,1)S(1)}, u32[]{:S(2)}, u32[]{:S(2)}) collective-permute-start(bf16[4,2,32,512]{3,2,1,0:T(8,128)(2,1)S(1)} %pad_maximum_fusion.1.a), channel_id=1, source_target_pairs={{15,0},{0,1},{1,2},{2,3},{3,4},{4,5},{5,6},{6,7},{7,8},{8,9},{9,10... | collective-permute-start | bytes 786440 | tf_op jit(solution)/shard_map/ppermute | solution.py:134
  42.4 16.8 %collective-permute-start.3 = (bf16[4,2,32,512]{3,2,1,0:T(8,128)(2,1)S(1)}, bf16[4,2,32,512]{3,2,1,0:T(8,128)(2,1)S(1)}, u32[]{:S(2)}, u32[]{:S(2)}) collective-permute-start(bf16[4,2,32,512]{3,2,1,0:T(8,128)(2,1)S(1)} %pad_maximum_fusion.1.a), channel_id=1, source_target_pairs={{1,0},{2,1},{3,2},{4,3},{5,4},{6,5},{7,6},{8,7},{9,8},{10,9},{11,1... | collective-permute-start | bytes 786440 | tf_op jit(solution)/shard_map/ppermute | solution.py:134
  44.3 13.7 %collective-permute-start.6 = (bf16[2,2,32,512]{3,2,1,0:T(8,128)(2,1)}, bf16[2,2,32,512]{3,2,1,0:T(8,128)(2,1)S(1)}, u32[]{:S(2)}, u32[]{:S(2)}) collective-permute-start(bf16[2,2,32,512]{3,2,1,0:T(8,128)(2,1)} %get-tuple-element.16), channel_id=1, source_target_pairs={{14,0},{15,1},{0,2},{1,3},{2,4},{3,5},{4,6},{5,7},{6,8},{7,9},{8,1... | collective-permute-start | bytes 393224 | tf_op jit(solution)/shard_map/ppermute | solution.py:134
  49.9 9.2 %collective-permute-start.5 = (bf16[2,2,32,512]{3,2,1,0:T(8,128)(2,1)}, bf16[2,2,32,512]{3,2,1,0:T(8,128)(2,1)}, u32[]{:S(2)}, u32[]{:S(2)}) collective-permute-start(bf16[2,2,32,512]{3,2,1,0:T(8,128)(2,1)} %get-tuple-element.17), channel_id=1, source_target_pairs={{2,0},{3,1},{4,2},{5,3},{6,4},{7,5},{8,6},{9,7},{10,8},{11,9},{12,... | collective-permute-start | bytes 393224 | tf_op jit(solution)/shard_map/ppermute | solution.py:134
  53.8 5.4 %copy-start = (bf16[832,512]{1,0:T(8,128)(2,1)S(1)}, bf16[832,512]{1,0:T(8,128)(2,1)}, u32[]{:S(2)}) copy-start(bf16[832,512]{1,0:T(8,128)(2,1)} %down.3) | copy-start | bytes 2555908
  61.0 6.8 %collective-permute-start.7 = (f32[16,16,1664]{2,1,0:T(8,128)S(1)}, f32[16,16,1664]{2,1,0:T(8,128)S(1)}, u32[]{:S(2)}, u32[]{:S(2)}) collective-permute-start(f32[16,16,1664]{2,1,0:T(8,128)S(1)} %get-tuple-element.10), channel_id=1, source_target_pairs={{0,16},{16,0},{1,17},{17,1},{2,18},{18,2},{3,19},{19,3},{4,20},{20... | collective-permute-start | bytes 5111816 | tf_op jit(solution)/shard_map/ppermute | solution.py:130
  62.9 4.9 %collective-permute-start.8 = (f32[16,16,832]{2,1,0:T(8,128)S(1)}, f32[16,16,832]{2,1,0:T(8,128)S(1)}, u32[]{:S(2)}, u32[]{:S(2)}) collective-permute-start(f32[16,16,832]{2,1,0:T(8,128)S(1)} %get-tuple-element.11), channel_id=1, source_target_pairs={{0,16},{16,0},{1,17},{17,1},{2,18},{18,2},{3,19},{19,3},{4,20},{20... | collective-permute-start | bytes 2555912 | tf_op jit(solution)/shard_map/ppermute | solution.py:130
  97.3 0.9 copy-start.5
  115.8 4.3 %collective-permute-start.9 = (bf16[16,16,1664]{2,1,0:T(8,128)(2,1)S(1)}, bf16[16,16,1664]{2,1,0:T(8,128)(2,1)S(1)}, u32[]{:S(2)}, u32[]{:S(2)}) collective-permute-start(bf16[16,16,1664]{2,1,0:T(8,128)(2,1)S(1)} %all_to_all.16.deltas.own), channel_id=1, source_target_pairs={{0,16},{16,0},{1,17},{17,1},{2,18},{18,2},{3,19},{19,3},{4,20},{20... | collective-permute-start | bytes 2555912 | tf_op jit(solution)/shard_map/ppermute | solution.py:130
  121.2 0.8 copy-start.2
  122.0 0.9 copy-start.3
  122.9 40.7 %all-to-all-start.2 = ((bf16[16,32,512]{2,1,0:T(8,128)(2,1)}), bf16[16,32,512]{2,1,0:T(8,128)(2,1)S(1)}, u32[]{:S(2)}, u32[]{:S(2)}) async-start(bf16[16,32,512]{2,1,0:T(8,128)(2,1)} %copy-done.2), calls=%async_computation.2 | async-start | bytes 1048576 | tf_op jit(solution)/shard_map/all_to_all | solution.py:182
  134.3 1.2 copy-start.4
  164.3 1.6 copy-start.1
Sparse Core Ops, SparseCore 0:
  98.3 56.0 all-gather.2

commit v7 on v5

--- a/solution.py
+++ b/solution.py
@@ -10,6 +10,7 @@
 FAR = 4
 OFFSETS = (0, 1, -1, 2)
 VMEM = pl.BlockSpec(memory_space=pltpu.VMEM)
+ANY = pl.BlockSpec(memory_space=pl.ANY)
 SMEM = pl.BlockSpec(memory_space=pltpu.SMEM)
 
 
@@ -28,16 +29,16 @@
     )
 
 
-def call(body, outs, flops, *args):
+def call(body, outs, flops, *args, after=()):
     moved = sum(a.size * a.dtype.itemsize for a in (*args, *jax.tree.leaves(outs)))
     return pl.pallas_call(
         body,
         out_shape=outs,
-        in_specs=[SMEM if a.dtype == jnp.int32 else VMEM for a in args],
+        in_specs=[SMEM if a.dtype == jnp.int32 else VMEM for a in args] + [ANY] * len(after),
         out_specs=jax.tree.map(lambda _: VMEM, outs),
         compiler_params=pltpu.CompilerParams(vmem_limit_bytes=32 * 2**20),
         cost_estimate=pl.CostEstimate(flops=flops, bytes_accessed=moved, transcendentals=0),
-    )(*args)
+    )(*args, *after)
 
 
 def half_rows(which, kind, near, second_low, second_high):
@@ -81,29 +82,34 @@
 def part_of(deltas, pair):
     lanes = pair.shape[0]
     rows = deltas[...].reshape(-1, deltas.shape[-1])[:, :lanes]
-    return contract(rows, pair[...], 1, 0).astype(BF16)
+    return contract(rows, pair[...], 1, 0)
 
 
 def own_body(deltas, pair, out):
     out[...] = part_of(deltas, pair)
 
 
-def other_body(where, deltas, pair, own, out):
-    devices, tokens, _ = out.shape
+def other_body(where, deltas, pair, own, keep, send):
+    slots, tokens, _ = keep.shape
     parts = (own[...], part_of(deltas, pair))
     for far in range(2):
         for k, offset in enumerate(OFFSETS):
             start = (far * len(OFFSETS) + k) * tokens
             for half, part in zip((where[0], 1 - where[0]), parts, strict=True):
-                device = lax.rem(where[1] + devices + offset + FAR * (2 * half + far), devices)
-                out[device] = part[start : start + tokens]
-
-
-def grads_body(where, a, b, c, d, e, own, other, pieces, input_out, gate_out, up_out, down_out):
-    total = pieces[0].astype(F32)
-    for i in range(1, pieces.shape[0]):
-        total += pieces[i].astype(F32)
-    input_out[...] = total.astype(BF16)
+                device = where[1] + 2 * slots + offset + FAR * (2 * half + far)
+                slot = lax.div(lax.rem(device, 2 * slots), 2)
+                rows = part[start : start + tokens]
+                if offset % 2:
+                    send[slot] = rows.astype(BF16)
+                else:
+                    keep[slot] = rows
+
+
+def add_body(keep, got, _, out):
+    out[...] = (keep[...] + got[...].astype(F32)).astype(BF16)
+
+
+def grads_body(where, a, b, c, d, e, own, other, gate_out, up_out, down_out):
     units = gate_out.shape[0]
     deltas = [ref[...].reshape(-1, ref.shape[-1]) for ref in (own, other)]
 
@@ -161,22 +167,26 @@
     row = call(middle_body, sds(parts.shape, BF16), 40 * half // n * units, parts)
     own = lax.all_to_all(row, XY, 0, 0)
     other = swap_cores(own)
-    own_part = call(own_body, sds((half, width), BF16), 2 * flops, own, pair)
-    pieces = call(
-        other_body, sds((n, tokens, width), BF16), 2 * flops, where, other, pair, own_part
-    )
-    pieces = lax.all_to_all(pieces, "col", 0, 0)
+    own_part = call(own_body, sds((half, width), F32), 2 * flops, own, pair)
+    slots = (n // 2, tokens, width)
+    keep, send = call(
+        other_body, (sds(slots, F32), sds(slots, BF16)), 2 * flops, where, other, pair, own_part
+    )
+    got = lax.ppermute(send, "col", [(i, i ^ 1) for i in range(n)])
     grad = sds((units, width), BF16)
-    input_grad, gate_grad, up_grad, down_grad = call(
+    gate_grad, up_grad, down_grad = call(
         grads_body,
-        (sds((tokens, width), BF16), grad, grad, grad),
+        (grad, grad, grad),
         6 * flops,
         where,
         *held,
         own,
         other,
-        pieces,
-    )
+    )
+    pieces = call(add_body, sds(slots, BF16), 0, keep, got, after=(down_grad,))
+    parity = [list(range(i, n, 2)) for i in range(2)]
+    pieces = lax.all_to_all(pieces, "col", 0, 0, axis_index_groups=parity)
+    input_grad = jnp.sum(pieces.astype(F32), axis=0).astype(BF16)
     return (input_grad, gate_grad.T, up_grad.T, down_grad)
 
 

time: 163 us -> 162 us (level)
  the two profiles are of different devices: /device:TPU:32 before, /device:TPU:8 now
where the time goes in v7:
time: 162 us; the launch traced here: 161 us
  blocking collectives  76.8 us (47%)
  starting transfers between devices  51.9 us (32%)
  waiting for transfers between devices  17.3 us (11%)
  Pallas kernels  9.4 us (6%)
  other arithmetic  3.69 us (2%)
    ppermute x7, starting transfers between devices, shift(): return lax.ppermute(value, 'col', [((i + by) % 16, i) for i in range(16)])  43.7 us
    all_to_all x1, blocking collectives, per_device(): pieces = lax.all_to_all(pieces, 'col', 0, 0, axis_index_groups=parity)  28.8 us
    all_to_all x1, blocking collectives, per_device(): parts = lax.all_to_all(parts, XY, 0, 0)  25.7 us
    all_to_all x1, blocking collectives, per_device(): own = lax.all_to_all(row, XY, 0, 0)  22.3 us
    pallas_call x7, Pallas kernels, call(): pl.pallas_call(body, out_shape=outs, in_specs=[SMEM if a.dtype == jnp.int...  9.4 us
    ppermute x7, waiting for transfers between devices, shift(): return lax.ppermute(value, 'col', [((i + by) % 16, i) for i in range(16)])  7.63 us
    ppermute x3, starting transfers between devices, swap_cores(): return lax.ppermute(value, 'core', [(0, 1), (1, 0)])  6.24 us
    ppermute x3, waiting for transfers between devices, swap_cores(): return lax.ppermute(value, 'core', [(0, 1), (1, 0)])  4.82 us
  transfers between devices with their start and end apart: 11, of which 6 were waited for; matrix products, arithmetic and copies ran while one was open for 1% of the time, Pallas kernels for 3%

profile of v7, /device:TPU:8, one launch (start us, length us, event | category | flops | bytes accessed | tf_op | source)
XLA Modules:
  0.0 161.0 jit_solution(14654004374586915798)
XLA Ops:
  0.6 0.9 fusion
  1.5 12.7 %collective-permute-start = (bf16[2,32,512]{2,1,0:T(8,128)(2,1)S(1)}, bf16[2,32,512]{2,1,0:T(8,128)(2,1)S(1)}, u32[]{:S(2)}, u32[]{:S(2)}) collective-permute-start(bf16[2,32,512]{2,1,0:T(8,128)(2,1)S(1)} %get-tuple-element.21), channel_id=1, source_target_pairs={{4,0},{5,1},{6,2},{7,3},{8,4},{9,5},{10,6},{11,7},{12,8},{13,9},{1... | collective-permute-start | bytes 196616 | tf_op jit(solution)/shard_map/ppermute | solution.py:132
  14.2 1.9 %collective-permute-start.2 = (bf16[2,32,512]{2,1,0:T(8,128)(2,1)S(1)}, bf16[2,32,512]{2,1,0:T(8,128)(2,1)S(1)}, u32[]{:S(2)}, u32[]{:S(2)}) collective-permute-start(bf16[2,32,512]{2,1,0:T(8,128)(2,1)S(1)} %get-tuple-element.21), channel_id=1, source_target_pairs={{12,0},{13,1},{14,2},{15,3},{0,4},{1,5},{2,6},{3,7},{4,8},{5,9},{6... | collective-permute-start | bytes 196616 | tf_op jit(solution)/shard_map/ppermute | solution.py:132
  16.2 10.8 %collective-permute-start.1 = (bf16[2,32,512]{2,1,0:T(8,128)(2,1)S(1)}, bf16[2,32,512]{2,1,0:T(8,128)(2,1)S(1)}, u32[]{:S(2)}, u32[]{:S(2)}) collective-permute-start(bf16[2,32,512]{2,1,0:T(8,128)(2,1)S(1)} %get-tuple-element.21), channel_id=1, source_target_pairs={{8,0},{9,1},{10,2},{11,3},{12,4},{13,5},{14,6},{15,7},{0,8},{1,9},... | collective-permute-start | bytes 196616 | tf_op jit(solution)/shard_map/ppermute | solution.py:132
  27.0 0.7 pad_maximum_fusion.3
  27.7 3.7 %collective-permute-done.1 = bf16[2,32,512]{2,1,0:T(8,128)(2,1)S(1)} collective-permute-done((bf16[2,32,512]{2,1,0:T(8,128)(2,1)S(1)}, bf16[2,32,512]{2,1,0:T(8,128)(2,1)S(1)}, u32[]{:S(2)}, u32[]{:S(2)}) %collective-permute-start.1) | collective-permute-done | bytes 65568 | tf_op jit(solution)/shard_map/ppermute | solution.py:132
  31.5 2.8 %collective-permute-start.4 = (bf16[4,2,32,512]{3,2,1,0:T(8,128)(2,1)S(1)}, bf16[4,2,32,512]{3,2,1,0:T(8,128)(2,1)S(1)}, u32[]{:S(2)}, u32[]{:S(2)}) collective-permute-start(bf16[4,2,32,512]{3,2,1,0:T(8,128)(2,1)S(1)} %pad_maximum_fusion.1.a), channel_id=1, source_target_pairs={{15,0},{0,1},{1,2},{2,3},{3,4},{4,5},{5,6},{6,7},{7,8},{8,9},{9,10... | collective-permute-start | bytes 786440 | tf_op jit(solution)/shard_map/ppermute | solution.py:132
  34.3 7.4 %collective-permute-start.3 = (bf16[4,2,32,512]{3,2,1,0:T(8,128)(2,1)S(1)}, bf16[4,2,32,512]{3,2,1,0:T(8,128)(2,1)S(1)}, u32[]{:S(2)}, u32[]{:S(2)}) collective-permute-start(bf16[4,2,32,512]{3,2,1,0:T(8,128)(2,1)S(1)} %pad_maximum_fusion.1.a), channel_id=1, source_target_pairs={{1,0},{2,1},{3,2},{4,3},{5,4},{6,5},{7,6},{8,7},{9,8},{10,9},{11,1... | collective-permute-start | bytes 786440 | tf_op jit(solution)/shard_map/ppermute | solution.py:132
  41.8 1.9 %collective-permute-start.6 = (bf16[2,2,32,512]{3,2,1,0:T(8,128)(2,1)}, bf16[2,2,32,512]{3,2,1,0:T(8,128)(2,1)S(1)}, u32[]{:S(2)}, u32[]{:S(2)}) collective-permute-start(bf16[2,2,32,512]{3,2,1,0:T(8,128)(2,1)} %get-tuple-element.18), channel_id=1, source_target_pairs={{14,0},{15,1},{0,2},{1,3},{2,4},{3,5},{4,6},{5,7},{6,8},{7,9},{8,1... | collective-permute-start | bytes 393224 | tf_op jit(solution)/shard_map/ppermute | solution.py:132
  43.7 6.0 %collective-permute-start.5 = (bf16[2,2,32,512]{3,2,1,0:T(8,128)(2,1)}, bf16[2,2,32,512]{3,2,1,0:T(8,128)(2,1)}, u32[]{:S(2)}, u32[]{:S(2)}) collective-permute-start(bf16[2,2,32,512]{3,2,1,0:T(8,128)(2,1)} %get-tuple-element.19), channel_id=1, source_target_pairs={{2,0},{3,1},{4,2},{5,3},{6,4},{7,5},{8,6},{9,7},{10,8},{11,9},{12,... | collective-permute-start | bytes 393224 | tf_op jit(solution)/shard_map/ppermute | solution.py:132
  49.8 1.3 pad_maximum_fusion.pair
  51.1 0.1 pad_add_fusion.where
  51.2 2.7 %collective-permute-done.6.e = bf16[2,2,32,512]{3,2,1,0:T(8,128)(2,1)S(1)} collective-permute-done((bf16[2,2,32,512]{3,2,1,0:T(8,128)(2,1)}, bf16[2,2,32,512]{3,2,1,0:T(8,128)(2,1)S(1)}, u32[]{:S(2)}, u32[]{:S(2)}) %collective-permute-start.6) | collective-permute-done | bytes 131104 | tf_op jit(solution)/shard_map/ppermute | solution.py:132
  53.9 1.2 collective-permute-done.5.d
  55.1 1.9 %shard_map.84 = (f32[16,16,1664]{2,1,0:T(8,128)S(1)}, f32[16,16,832]{2,1,0:T(8,128)S(1)}) custom-call(s32[2]{0:T(128)S(1)} %pad_add_fusion.where, bf16[4,2,32,512]{3,2,1,0:T(8,128)(2,1)S(1)} %pad_maximum_fusion.1.a, bf16[4,2,32,512]{3,2,1,0:T(8,128)(2,1)S(1)} %collective-permute-done.3.b, bf16[4,2,32,512]{3,2,1,0:T(8,128)(2,1)S(1)} %collective-permute-done.4.c, ...), custom_call_target="tpu_custom_call" | custom-call | flops 654311424 | bytes 6160392 | tf_op jit(solution)/shard_map/pallas_call | solution.py:34
  57.0 1.9 %collective-permute-start.7 = (f32[16,16,1664]{2,1,0:T(8,128)S(1)}, f32[16,16,1664]{2,1,0:T(8,128)S(1)}, u32[]{:S(2)}, u32[]{:S(2)}) collective-permute-start(f32[16,16,1664]{2,1,0:T(8,128)S(1)} %get-tuple-element.11), channel_id=1, source_target_pairs={{0,16},{16,0},{1,17},{17,1},{2,18},{18,2},{3,19},{19,3},{4,20},{20... | collective-permute-start | bytes 5111816 | tf_op jit(solution)/shard_map/ppermute | solution.py:128
  58.9 2.4 %collective-permute-start.8 = (f32[16,16,832]{2,1,0:T(8,128)S(1)}, f32[16,16,832]{2,1,0:T(8,128)S(1)}, u32[]{:S(2)}, u32[]{:S(2)}) collective-permute-start(f32[16,16,832]{2,1,0:T(8,128)S(1)} %get-tuple-element.12), channel_id=1, source_target_pairs={{0,16},{16,0},{1,17},{17,1},{2,18},{18,2},{3,19},{19,3},{4,20},{20... | collective-permute-start | bytes 2555912 | tf_op jit(solution)/shard_map/ppermute | solution.py:128
  61.3 2.5 %collective-permute-done.8.got_down = f32[16,16,832]{2,1,0:T(8,128)S(1)} collective-permute-done((f32[16,16,832]{2,1,0:T(8,128)S(1)}, f32[16,16,832]{2,1,0:T(8,128)S(1)}, u32[]{:S(2)}, u32[]{:S(2)}) %collective-permute-start.8) | collective-permute-done | bytes 852000 | tf_op jit(solution)/shard_map/ppermute | solution.py:128
  63.8 1.9 %shard_map.85 = bf16[16,16,2496]{2,1,0:T(8,128)(2,1)S(1)} custom-call(s32[2]{0:T(128)S(1)} %pad_add_fusion.where, bf16[4,2,32,512]{3,2,1,0:T(8,128)(2,1)S(1)} %pad_maximum_fusion.1.a, bf16[4,2,32,512]{3,2,1,0:T(8,128)(2,1)S(1)} %collective-permute-done.3.b, bf16[4,2,32,512]{3,2,1,0:T(8,128)(2,1)S(1)} %collective-permute-done.4.c, ...), custom_call_target="tpu_custom_call" | custom-call | flops 654311424 | bytes 7438344 | tf_op jit(solution)/shard_map/pallas_call | solution.py:34
  65.7 25.7 %all_to_all.15.parts = bf16[16,16,2496]{2,1,0:T(8,128)(2,1)S(1)} all-to-all(bf16[16,16,2496]{2,1,0:T(8,128)(2,1)S(1)} %shard_map.85), channel_id=1, replica_groups=mesh['x'=4,'y'=4,'core'=2,'col'=16] {'x','y'}, dimensions={0} | all-to-all | bytes 2555904 | tf_op jit(solution)/shard_map/all_to_all | solution.py:166
  91.4 0.3 shard_map.86
  91.7 22.3 %all_to_all.16.deltas.own = bf16[16,16,2496]{2,1,0:T(8,128)(2,1)S(1)} all-to-all(bf16[16,16,2496]{2,1,0:T(8,128)(2,1)S(1)} %shard_map.86), channel_id=1, replica_groups=mesh['x'=4,'y'=4,'core'=2,'col'=16] {'x','y'}, dimensions={0} | all-to-all | bytes 2555904 | tf_op jit(solution)/shard_map/all_to_all | solution.py:168
  114.0 1.9 %collective-permute-start.9 = (bf16[16,16,2496]{2,1,0:T(8,128)(2,1)S(1)}, bf16[16,16,2496]{2,1,0:T(8,128)(2,1)S(1)}, u32[]{:S(2)}, u32[]{:S(2)}) collective-permute-start(bf16[16,16,2496]{2,1,0:T(8,128)(2,1)S(1)} %all_to_all.16.deltas.own), channel_id=1, source_target_pairs={{0,16},{16,0},{1,17},{17,1},{2,18},{18,2},{3,19},{19,3},{4,20},{20... | collective-permute-start | bytes 3833864 | tf_op jit(solution)/shard_map/ppermute | solution.py:128
  115.9 0.6 shard_map.87.own
  116.6 2.4 %collective-permute-done.9.deltas.other = bf16[16,16,2496]{2,1,0:T(8,128)(2,1)S(1)} collective-permute-done((bf16[16,16,2496]{2,1,0:T(8,128)(2,1)S(1)}, bf16[16,16,2496]{2,1,0:T(8,128)(2,1)S(1)}, u32[]{:S(2)}, u32[]{:S(2)}) %collective-permute-start.9) | collective-permute-done | bytes 1277984 | tf_op jit(solution)/shard_map/ppermute | solution.py:128
  118.9 1.2 shard_map.88
  120.1 1.9 %collective-permute-start.10 = (bf16[8,32,512]{2,1,0:T(8,128)(2,1)S(1)}, bf16[8,32,512]{2,1,0:T(8,128)(2,1)S(1)}, u32[]{:S(2)}, u32[]{:S(2)}) collective-permute-start(bf16[8,32,512]{2,1,0:T(8,128)(2,1)S(1)} %get-tuple-element.14), channel_id=1, source_target_pairs={{0,1},{1,0},{2,3},{3,2},{4,5},{5,4},{6,7},{7,6},{8,9},{9,8},{10,11... | collective-permute-start | bytes 786440 | tf_op jit(solution)/shard_map/ppermute | solution.py:175
  122.0 3.5 %shard_map.89 = (bf16[832,512]{1,0:T(8,128)(2,1)}, bf16[832,512]{1,0:T(8,128)(2,1)}, bf16[832,512]{1,0:T(8,128)(2,1)}) custom-call(s32[2]{0:T(128)S(1)} %pad_add_fusion.where, bf16[4,2,32,512]{3,2,1,0:T(8,128)(2,1)S(1)} %pad_maximum_fusion.1.a, bf16[4,2,32,512]{3,2,1,0:T(8,128)(2,1)S(1)} %collective-permute-done.3.b, ...), custom_call_target="tpu_custom_call" | custom-call | flops 1308622848 | bytes 6160392 | tf_op jit(solution)/shard_map/pallas_call | solution.py:34
  125.5 4.8 %collective-permute-done.10.got = bf16[8,32,512]{2,1,0:T(8,128)(2,1)S(1)} collective-permute-done((bf16[8,32,512]{2,1,0:T(8,128)(2,1)S(1)}, bf16[8,32,512]{2,1,0:T(8,128)(2,1)S(1)}, u32[]{:S(2)}, u32[]{:S(2)}) %collective-permute-start.10) | collective-permute-done | bytes 262176 | tf_op jit(solution)/shard_map/ppermute | solution.py:175
  130.3 1.2 copy-done.1
  131.6 28.8 %all_to_all.17 = bf16[8,32,512]{2,1,0:T(8,128)(2,1)S(1)} all-to-all(bf16[8,32,512]{2,1,0:T(8,128)(2,1)S(1)} %shard_map.90), channel_id=1, replica_groups={{0,2,4,6,8,10,12,14},{1,3,5,7,9,11,13,15},{16,18,20,22,24,26,28,30},{17..., dimensions={0} | all-to-all | bytes 524288 | tf_op jit(solution)/shard_map/all_to_all | solution.py:188
  160.3 0.7 reduce_sum.12
  (12 shorter events, 0.1 us)
Async XLA Ops:
  0.6 49.1 %copy-start.2 = (bf16[512,832]{0,1:T(8,128)(2,1)S(1)}, bf16[512,832]{0,1:T(8,128)(2,1)}, u32[]{:S(2)}) copy-start(bf16[512,832]{0,1:T(8,128)(2,1)} %param.8) | copy-start | bytes 2555908
  1.5 25.5 %collective-permute-start = (bf16[2,32,512]{2,1,0:T(8,128)(2,1)S(1)}, bf16[2,32,512]{2,1,0:T(8,128)(2,1)S(1)}, u32[]{:S(2)}, u32[]{:S(2)}) collective-permute-start(bf16[2,32,512]{2,1,0:T(8,128)(2,1)S(1)} %get-tuple-element.21), channel_id=1, source_target_pairs={{4,0},{5,1},{6,2},{7,3},{8,4},{9,5},{10,6},{11,7},{12,8},{13,9},{1... | collective-permute-start | bytes 196616 | tf_op jit(solution)/shard_map/ppermute | solution.py:132
  14.2 12.8 %collective-permute-start.2 = (bf16[2,32,512]{2,1,0:T(8,128)(2,1)S(1)}, bf16[2,32,512]{2,1,0:T(8,128)(2,1)S(1)}, u32[]{:S(2)}, u32[]{:S(2)}) collective-permute-start(bf16[2,32,512]{2,1,0:T(8,128)(2,1)S(1)} %get-tuple-element.21), channel_id=1, source_target_pairs={{12,0},{13,1},{14,2},{15,3},{0,4},{1,5},{2,6},{3,7},{4,8},{5,9},{6... | collective-permute-start | bytes 196616 | tf_op jit(solution)/shard_map/ppermute | solution.py:132
  16.2 15.3 %collective-permute-start.1 = (bf16[2,32,512]{2,1,0:T(8,128)(2,1)S(1)}, bf16[2,32,512]{2,1,0:T(8,128)(2,1)S(1)}, u32[]{:S(2)}, u32[]{:S(2)}) collective-permute-start(bf16[2,32,512]{2,1,0:T(8,128)(2,1)S(1)} %get-tuple-element.21), channel_id=1, source_target_pairs={{8,0},{9,1},{10,2},{11,3},{12,4},{13,5},{14,6},{15,7},{0,8},{1,9},... | collective-permute-start | bytes 196616 | tf_op jit(solution)/shard_map/ppermute | solution.py:132
  31.5 23.7 %collective-permute-start.4 = (bf16[4,2,32,512]{3,2,1,0:T(8,128)(2,1)S(1)}, bf16[4,2,32,512]{3,2,1,0:T(8,128)(2,1)S(1)}, u32[]{:S(2)}, u32[]{:S(2)}) collective-permute-start(bf16[4,2,32,512]{3,2,1,0:T(8,128)(2,1)S(1)} %pad_maximum_fusion.1.a), channel_id=1, source_target_pairs={{15,0},{0,1},{1,2},{2,3},{3,4},{4,5},{5,6},{6,7},{7,8},{8,9},{9,10... | collective-permute-start | bytes 786440 | tf_op jit(solution)/shard_map/ppermute | solution.py:132
  34.3 20.8 %collective-permute-start.3 = (bf16[4,2,32,512]{3,2,1,0:T(8,128)(2,1)S(1)}, bf16[4,2,32,512]{3,2,1,0:T(8,128)(2,1)S(1)}, u32[]{:S(2)}, u32[]{:S(2)}) collective-permute-start(bf16[4,2,32,512]{3,2,1,0:T(8,128)(2,1)S(1)} %pad_maximum_fusion.1.a), channel_id=1, source_target_pairs={{1,0},{2,1},{3,2},{4,3},{5,4},{6,5},{7,6},{8,7},{9,8},{10,9},{11,1... | collective-permute-start | bytes 786440 | tf_op jit(solution)/shard_map/ppermute | solution.py:132
  41.8 12.1 %collective-permute-start.6 = (bf16[2,2,32,512]{3,2,1,0:T(8,128)(2,1)}, bf16[2,2,32,512]{3,2,1,0:T(8,128)(2,1)S(1)}, u32[]{:S(2)}, u32[]{:S(2)}) collective-permute-start(bf16[2,2,32,512]{3,2,1,0:T(8,128)(2,1)} %get-tuple-element.18), channel_id=1, source_target_pairs={{14,0},{15,1},{0,2},{1,3},{2,4},{3,5},{4,6},{5,7},{6,8},{7,9},{8,1... | collective-permute-start | bytes 393224 | tf_op jit(solution)/shard_map/ppermute | solution.py:132
  43.7 11.4 %collective-permute-start.5 = (bf16[2,2,32,512]{3,2,1,0:T(8,128)(2,1)}, bf16[2,2,32,512]{3,2,1,0:T(8,128)(2,1)}, u32[]{:S(2)}, u32[]{:S(2)}) collective-permute-start(bf16[2,2,32,512]{3,2,1,0:T(8,128)(2,1)} %get-tuple-element.19), channel_id=1, source_target_pairs={{2,0},{3,1},{4,2},{5,3},{6,4},{7,5},{8,6},{9,7},{10,8},{11,9},{12,... | collective-permute-start | bytes 393224 | tf_op jit(solution)/shard_map/ppermute | solution.py:132
  49.7 5.4 %copy-start = (bf16[832,512]{1,0:T(8,128)(2,1)S(1)}, bf16[832,512]{1,0:T(8,128)(2,1)}, u32[]{:S(2)}) copy-start(bf16[832,512]{1,0:T(8,128)(2,1)} %down.3) | copy-start | bytes 2555908
  57.0 6.8 %collective-permute-start.7 = (f32[16,16,1664]{2,1,0:T(8,128)S(1)}, f32[16,16,1664]{2,1,0:T(8,128)S(1)}, u32[]{:S(2)}, u32[]{:S(2)}) collective-permute-start(f32[16,16,1664]{2,1,0:T(8,128)S(1)} %get-tuple-element.11), channel_id=1, source_target_pairs={{0,16},{16,0},{1,17},{17,1},{2,18},{18,2},{3,19},{19,3},{4,20},{20... | collective-permute-start | bytes 5111816 | tf_op jit(solution)/shard_map/ppermute | solution.py:128
  58.9 4.9 %collective-permute-start.8 = (f32[16,16,832]{2,1,0:T(8,128)S(1)}, f32[16,16,832]{2,1,0:T(8,128)S(1)}, u32[]{:S(2)}, u32[]{:S(2)}) collective-permute-start(f32[16,16,832]{2,1,0:T(8,128)S(1)} %get-tuple-element.12), channel_id=1, source_target_pairs={{0,16},{16,0},{1,17},{17,1},{2,18},{18,2},{3,19},{19,3},{4,20},{20... | collective-permute-start | bytes 2555912 | tf_op jit(solution)/shard_map/ppermute | solution.py:128
  114.0 4.9 %collective-permute-start.9 = (bf16[16,16,2496]{2,1,0:T(8,128)(2,1)S(1)}, bf16[16,16,2496]{2,1,0:T(8,128)(2,1)S(1)}, u32[]{:S(2)}, u32[]{:S(2)}) collective-permute-start(bf16[16,16,2496]{2,1,0:T(8,128)(2,1)S(1)} %all_to_all.16.deltas.own), channel_id=1, source_target_pairs={{0,16},{16,0},{1,17},{17,1},{2,18},{18,2},{3,19},{19,3},{4,20},{20... | collective-permute-start | bytes 3833864 | tf_op jit(solution)/shard_map/ppermute | solution.py:128
  120.1 10.2 %collective-permute-start.10 = (bf16[8,32,512]{2,1,0:T(8,128)(2,1)S(1)}, bf16[8,32,512]{2,1,0:T(8,128)(2,1)S(1)}, u32[]{:S(2)}, u32[]{:S(2)}) collective-permute-start(bf16[8,32,512]{2,1,0:T(8,128)(2,1)S(1)} %get-tuple-element.14), channel_id=1, source_target_pairs={{0,1},{1,0},{2,3},{3,2},{4,5},{5,4},{6,7},{7,6},{8,9},{9,8},{10,11... | collective-permute-start | bytes 786440 | tf_op jit(solution)/shard_map/ppermute | solution.py:175
  130.3 1.2 copy-start.1

commit v8 on v7

--- a/solution.py
+++ b/solution.py
@@ -7,8 +7,6 @@
 
 BF16, F32 = jnp.bfloat16, jnp.float32
 XY = ("x", "y")
-FAR = 4
-OFFSETS = (0, 1, -1, 2)
 VMEM = pl.BlockSpec(memory_space=pltpu.VMEM)
 ANY = pl.BlockSpec(memory_space=pl.ANY)
 SMEM = pl.BlockSpec(memory_space=pltpu.SMEM)
@@ -41,28 +39,27 @@
     )(*args, *after)
 
 
-def half_rows(which, kind, near, second_low, second_high):
-    rows = []
-    for far in range(2):
-        rows += [ref[2 * which + far, kind] for ref in near]
-        rows.append(jnp.where(which == 0, second_low[far, kind], second_high[far, kind]))
-    return jnp.concatenate(rows, 0)
+def half_rows(which, kind, even, low, high):
+    count, tokens, width = low.shape[0], *low.shape[2:]
+    first = even[pl.ds(which * count, count), kind]
+    second = jnp.where(which == 0, low[:, kind], high[:, kind])
+    return jnp.concatenate([first, second], 0).reshape(2 * count * tokens, width)
 
 
-def send_body(where, a, b, c, d, e, pair, down, pair_out, down_out):
+def send_body(where, a, b, c, pair, down, pair_out, down_out):
     for kind, weight, out in ((0, pair, pair_out), (1, down, down_out)):
-        rows = half_rows(1 - where[0], kind, (a, b, c), d, e)
+        rows = half_rows(1 - where[0], kind, a, b, c)
         out[...] = contract(rows, weight[...], 1, 1).reshape(out.shape)
 
 
-def keep_body(where, a, b, c, d, e, pair, down, got_pair, got_down, out):
+def keep_body(where, a, b, c, pair, down, got_pair, got_down, out):
     blocks, rows, _ = out.shape
     wide = pair.shape[0]
     for kind, weight, got, lanes in (
         (0, pair, got_pair, slice(0, wide)),
         (1, down, got_down, slice(wide, None)),
     ):
-        mine = half_rows(where[0], kind, (a, b, c), d, e)
+        mine = half_rows(where[0], kind, a, b, c)
         total = contract(mine, weight[...], 1, 1).reshape(blocks, rows, -1)
         out[:, :, lanes] = (total + got[...]).astype(BF16)
 
@@ -90,32 +87,26 @@
 
 
 def other_body(where, deltas, pair, own, keep, send):
-    slots, tokens, _ = keep.shape
+    count, tokens = keep.shape[0] // 2, keep.shape[1]
     parts = (own[...], part_of(deltas, pair))
-    for far in range(2):
-        for k, offset in enumerate(OFFSETS):
-            start = (far * len(OFFSETS) + k) * tokens
-            for half, part in zip((where[0], 1 - where[0]), parts, strict=True):
-                device = where[1] + 2 * slots + offset + FAR * (2 * half + far)
-                slot = lax.div(lax.rem(device, 2 * slots), 2)
-                rows = part[start : start + tokens]
-                if offset % 2:
-                    send[slot] = rows.astype(BF16)
-                else:
-                    keep[slot] = rows
+    for half, part in zip((where[0], 1 - where[0]), parts, strict=True):
+        rows = part.reshape(2 * count, tokens, -1)
+        keep[pl.ds(half * count, count)] = rows[:count]
+        send[pl.ds(half * count, count)] = rows[count:].astype(BF16)
 
 
 def add_body(keep, got, _, out):
     out[...] = (keep[...] + got[...].astype(F32)).astype(BF16)
 
 
-def grads_body(where, a, b, c, d, e, own, other, gate_out, up_out, down_out):
+def grads_body(where, a, b, c, own, other, gate_out, up_out, down_out, done):
+    done[...] = jnp.zeros_like(done)
     units = gate_out.shape[0]
     deltas = [ref[...].reshape(-1, ref.shape[-1]) for ref in (own, other)]
 
     def total_of(kind, lanes):
         halves = (where[0], 1 - where[0])
-        rows = jnp.concatenate([half_rows(h, kind, (a, b, c), d, e) for h in halves], 0)
+        rows = jnp.concatenate([half_rows(h, kind, a, b, c) for h in halves], 0)
         return contract(jnp.concatenate([m[:, lanes] for m in deltas], 0), rows, 0, 0).astype(BF16)
 
     pair = total_of(0, slice(0, 2 * units))
@@ -137,16 +128,14 @@
     units = gate_weight.shape[1]
     n = 16
     half = n * tokens // 2
-    core, col = lax.axis_index("core"), lax.axis_index("col")
-    where = jnp.stack([core, col]).astype(jnp.int32)
+    where = lax.axis_index("core").astype(jnp.int32).reshape(1)
     pair = jnp.concatenate([gate_weight.T, up_weight.T], 0)
 
+    parity = [list(range(i, n, 2)) for i in range(2)]
     both = jnp.stack([inputs, out_grad])
-    group = jnp.stack([both, shift(both, FAR), shift(both, 2 * FAR), shift(both, -FAR)])
-    after, before = shift(group, 1), shift(group, -1)
-    low = shift(group[:2], 2)
-    high = shift(jnp.concatenate([group[3:], group[:1]]), -2)
-    held = (group, after, before, low, high)
+    even = lax.all_gather(both, "col", axis=0, axis_index_groups=parity)
+    low, high = shift(even[: n // 4], 1), shift(even[n // 4 :], -1)
+    held = (even, low, high)
 
     flops = 2 * half * units * width
     sds = jax.ShapeDtypeStruct
@@ -174,17 +163,16 @@
     )
     got = lax.ppermute(send, "col", [(i, i ^ 1) for i in range(n)])
     grad = sds((units, width), BF16)
-    gate_grad, up_grad, down_grad = call(
+    gate_grad, up_grad, down_grad, done = call(
         grads_body,
-        (grad, grad, grad),
+        (grad, grad, grad, sds((8, 128), F32)),
         6 * flops,
         where,
         *held,
         own,
         other,
     )
-    pieces = call(add_body, sds(slots, BF16), 0, keep, got, after=(down_grad,))
-    parity = [list(range(i, n, 2)) for i in range(2)]
+    pieces = call(add_body, sds(slots, BF16), 0, keep, got, after=(done,))
     pieces = lax.all_to_all(pieces, "col", 0, 0, axis_index_groups=parity)
     input_grad = jnp.sum(pieces.astype(F32), axis=0).astype(BF16)
     return (input_grad, gate_grad.T, up_grad.T, down_grad)

time: 162 us -> 154 us (0.951)
  starting transfers between devices: 51.9 us -> 14.1 us
  blocking collectives: 76.8 us -> 113 us
  Pallas kernels: 9.4 us -> 6.01 us
  other arithmetic: 3.69 us -> 1.67 us
    ppermute x7 -> x2, starting transfers between devices: 43.7 us -> 5.91 us  [shift(): return lax.ppermute(value, 'col', [((i + by) % 16, i) for i in range(16)])]
    all_gather x0 -> x1, blocking collectives: none -> 37.2 us  [per_device(): even = lax.all_gather(both, 'col', axis=0, axis_index_groups=parity)]
    pallas_call x7, Pallas kernels: 9.4 us -> 6.01 us  [call(): pl.pallas_call(body, out_shape=outs, in_specs=[SMEM if a.dtype == jnp.int...]
    ppermute x7 -> x2, waiting for transfers between devices: 7.63 us -> 7.39 us  [shift(): return lax.ppermute(value, 'col', [((i + by) % 16, i) for i in range(16)])]
  transfers between devices with their start and end apart: 11 -> 6, of which waited for: 6 -> 5; matrix products, arithmetic and copies ran while one was open for 1% -> 0% of each run, Pallas kernels for 3% -> 2%
where the time goes in v8:
time: 154 us; the launch traced here: 153 us
  blocking collectives  113 us (73%)
  waiting for transfers between devices  18.1 us (12%)
  starting transfers between devices  14.1 us (9%)
  Pallas kernels  6.01 us (4%)
  other arithmetic  1.67 us (1%)
    all_gather x1, blocking collectives, per_device(): even = lax.all_gather(both, 'col', axis=0, axis_index_groups=parity)  37.2 us
    all_to_all x1, blocking collectives, per_device(): pieces = lax.all_to_all(pieces, 'col', 0, 0, axis_index_groups=parity)  27.6 us
    all_to_all x1, blocking collectives, per_device(): parts = lax.all_to_all(parts, XY, 0, 0)  25.7 us
    all_to_all x1, blocking collectives, per_device(): own = lax.all_to_all(row, XY, 0, 0)  22.3 us
    ppermute x2, waiting for transfers between devices, shift(): return lax.ppermute(value, 'col', [((i + by) % 16, i) for i in range(16)])  7.39 us
    ppermute x3, starting transfers between devices, swap_cores(): return lax.ppermute(value, 'core', [(0, 1), (1, 0)])  6.24 us
    pallas_call x7, Pallas kernels, call(): pl.pallas_call(body, out_shape=outs, in_specs=[SMEM if a.dtype == jnp.int...  6.01 us
    ppermute x2, starting transfers between devices, shift(): return lax.ppermute(value, 'col', [((i + by) % 16, i) for i in range(16)])  5.91 us
  transfers between devices with their start and end apart: 6, of which 5 were waited for; matrix products, arithmetic and copies ran while one was open for 0% of the time, Pallas kernels for 2%

profile of v8, /device:TPU:8, one launch (start us, length us, event | category | flops | bytes accessed | tf_op | source)
XLA Modules:
  0.0 153.4 jit_solution(16009661207229634898)
XLA Ops:
  0.6 0.0 copy-start.1
  0.6 0.0 copy-start.2
  0.7 0.9 pad_maximum_fusion.1
  1.6 37.2 %all-gather = bf16[16,32,512]{2,1,0:T(8,128)(2,1)S(1)} all-gather(bf16[2,32,512]{2,1,0:T(8,128)(2,1)S(1)} %pad_maximum_fusion.1), channel_id=2, replica_groups={{0,2,4,6,8,10,12,14},{1,3,5,7,9,11,13,15},{16,18,20,22,24,26,28,30},{17..., dimensions={0}, use_global_device_ids=true | all-gather | bytes 589824 | tf_op jit(solution)/shard_map/all_gather | solution.py:136
  38.8 4.0 %collective-permute-start = (bf16[4,2,32,512]{3,2,1,0:T(8,128)(2,1)S(1)}, bf16[4,2,32,512]{3,2,1,0:T(8,128)(2,1)S(1)}, u32[]{:S(2)}, u32[]{:S(2)}) collective-permute-start(bf16[4,2,32,512]{3,2,1,0:T(8,128)(2,1)S(1)} %bitcast.16), channel_id=1, source_target_pairs={{1,0},{2,1},{3,2},{4,3},{5,4},{6,5},{7,6},{8,7},{9,8},{10,9},{11,1... | collective-permute-start | bytes 786440 | tf_op jit(solution)/shard_map/ppermute | solution.py:123
  42.8 1.9 %collective-permute-start.1 = (bf16[4,2,32,512]{3,2,1,0:T(8,128)(2,1)S(1)}, bf16[4,2,32,512]{3,2,1,0:T(8,128)(2,1)S(1)}, u32[]{:S(2)}, u32[]{:S(2)}) collective-permute-start(bf16[4,2,32,512]{3,2,1,0:T(8,128)(2,1)S(1)} %bitcast.15), channel_id=1, source_target_pairs={{15,0},{0,1},{1,2},{2,3},{3,4},{4,5},{5,6},{6,7},{7,8},{8,9},{9,10... | collective-permute-start | bytes 786440 | tf_op jit(solution)/shard_map/ppermute | solution.py:123
  44.7 0.0 copy-done.1
  44.7 0.0 copy-done.2
  44.8 0.0 copy-start
  44.8 0.1 pad_maximum_fusion.pair
  44.9 2.2 %collective-permute-done.b = bf16[4,2,32,512]{3,2,1,0:T(8,128)(2,1)S(1)} collective-permute-done((bf16[4,2,32,512]{3,2,1,0:T(8,128)(2,1)S(1)}, bf16[4,2,32,512]{3,2,1,0:T(8,128)(2,1)S(1)}, u32[]{:S(2)}, u32[]{:S(2)}) %collective-permute-start) | collective-permute-done | bytes 262176 | tf_op jit(solution)/shard_map/ppermute | solution.py:123
  47.1 5.2 %collective-permute-done.1.c = bf16[4,2,32,512]{3,2,1,0:T(8,128)(2,1)S(1)} collective-permute-done((bf16[4,2,32,512]{3,2,1,0:T(8,128)(2,1)S(1)}, bf16[4,2,32,512]{3,2,1,0:T(8,128)(2,1)S(1)}, u32[]{:S(2)}, u32[]{:S(2)}) %collective-permute-start.1) | collective-permute-done | bytes 262176 | tf_op jit(solution)/shard_map/ppermute | solution.py:123
  52.3 0.0 copy-done
  52.3 1.0 shard_map.84
  53.2 1.9 %collective-permute-start.2 = (f32[16,16,1664]{2,1,0:T(8,128)S(1)}, f32[16,16,1664]{2,1,0:T(8,128)S(1)}, u32[]{:S(2)}, u32[]{:S(2)}) collective-permute-start(f32[16,16,1664]{2,1,0:T(8,128)S(1)} %get-tuple-element.12), channel_id=1, source_target_pairs={{0,16},{16,0},{1,17},{17,1},{2,18},{18,2},{3,19},{19,3},{4,20},{20... | collective-permute-start | bytes 5111816 | tf_op jit(solution)/shard_map/ppermute | solution.py:119
  55.2 2.4 %collective-permute-start.3 = (f32[16,16,832]{2,1,0:T(8,128)S(1)}, f32[16,16,832]{2,1,0:T(8,128)S(1)}, u32[]{:S(2)}, u32[]{:S(2)}) collective-permute-start(f32[16,16,832]{2,1,0:T(8,128)S(1)} %get-tuple-element.13), channel_id=1, source_target_pairs={{0,16},{16,0},{1,17},{17,1},{2,18},{18,2},{3,19},{19,3},{4,20},{20... | collective-permute-start | bytes 2555912 | tf_op jit(solution)/shard_map/ppermute | solution.py:119
  57.6 2.5 %collective-permute-done.3.got_down = f32[16,16,832]{2,1,0:T(8,128)S(1)} collective-permute-done((f32[16,16,832]{2,1,0:T(8,128)S(1)}, f32[16,16,832]{2,1,0:T(8,128)S(1)}, u32[]{:S(2)}, u32[]{:S(2)}) %collective-permute-start.3) | collective-permute-done | bytes 852000 | tf_op jit(solution)/shard_map/ppermute | solution.py:119
  60.1 0.0 collective-permute-done.2.got_pair
  60.1 1.0 shard_map.85
  61.0 25.7 %all_to_all.15.parts = bf16[16,16,2496]{2,1,0:T(8,128)(2,1)S(1)} all-to-all(bf16[16,16,2496]{2,1,0:T(8,128)(2,1)S(1)} %shard_map.85), channel_id=1, replica_groups=mesh['x'=4,'y'=4,'core'=2,'col'=16] {'x','y'}, dimensions={0} | all-to-all | bytes 2555904 | tf_op jit(solution)/shard_map/all_to_all | solution.py:155
  86.7 0.3 shard_map.86
  87.0 22.3 %all_to_all.16.deltas.own = bf16[16,16,2496]{2,1,0:T(8,128)(2,1)S(1)} all-to-all(bf16[16,16,2496]{2,1,0:T(8,128)(2,1)S(1)} %shard_map.86), channel_id=1, replica_groups=mesh['x'=4,'y'=4,'core'=2,'col'=16] {'x','y'}, dimensions={0} | all-to-all | bytes 2555904 | tf_op jit(solution)/shard_map/all_to_all | solution.py:157
  109.4 1.9 %collective-permute-start.4 = (bf16[16,16,2496]{2,1,0:T(8,128)(2,1)S(1)}, bf16[16,16,2496]{2,1,0:T(8,128)(2,1)S(1)}, u32[]{:S(2)}, u32[]{:S(2)}) collective-permute-start(bf16[16,16,2496]{2,1,0:T(8,128)(2,1)S(1)} %all_to_all.16.deltas.own), channel_id=1, source_target_pairs={{0,16},{16,0},{1,17},{17,1},{2,18},{18,2},{3,19},{19,3},{4,20},{20... | collective-permute-start | bytes 3833864 | tf_op jit(solution)/shard_map/ppermute | solution.py:119
  111.3 0.6 shard_map.87.own
  111.9 2.4 %collective-permute-done.4.deltas.other = bf16[16,16,2496]{2,1,0:T(8,128)(2,1)S(1)} collective-permute-done((bf16[16,16,2496]{2,1,0:T(8,128)(2,1)S(1)}, bf16[16,16,2496]{2,1,0:T(8,128)(2,1)S(1)}, u32[]{:S(2)}, u32[]{:S(2)}) %collective-permute-start.4) | collective-permute-done | bytes 1277984 | tf_op jit(solution)/shard_map/ppermute | solution.py:119
  114.3 0.6 shard_map.88
  114.9 1.9 %collective-permute-start.5 = (bf16[8,32,512]{2,1,0:T(8,128)(2,1)S(1)}, bf16[8,32,512]{2,1,0:T(8,128)(2,1)S(1)}, u32[]{:S(2)}, u32[]{:S(2)}) collective-permute-start(bf16[8,32,512]{2,1,0:T(8,128)(2,1)S(1)} %get-tuple-element.15), channel_id=1, source_target_pairs={{0,1},{1,0},{2,3},{3,2},{4,5},{5,4},{6,7},{7,6},{8,9},{9,8},{10,11... | collective-permute-start | bytes 786440 | tf_op jit(solution)/shard_map/ppermute | solution.py:164
  116.8 2.5 %shard_map.89 = (bf16[832,512]{1,0:T(8,128)(2,1)}, bf16[832,512]{1,0:T(8,128)(2,1)}, bf16[832,512]{1,0:T(8,128)(2,1)}, f32[8,128]{1,0:T(8,128)S(1)}) custom-call(s32[1]{0:T(128)} %bitcast.where, bf16[8,2,32,512]{3,2,1,0:T(8,128)(2,1)S(1)} %bitcast.12, bf16[4,2,32,512]{3,2,1,0:T(8,128)(2,1)S(1)} %collective-permute-done.b, ...), custom_call_target="tpu_custom_call" | custom-call | flops 1308622848 | bytes 6164484 | tf_op jit(solution)/shard_map/pallas_call | solution.py:32
  119.3 5.8 %collective-permute-done.5.got = bf16[8,32,512]{2,1,0:T(8,128)(2,1)S(1)} collective-permute-done((bf16[8,32,512]{2,1,0:T(8,128)(2,1)S(1)}, bf16[8,32,512]{2,1,0:T(8,128)(2,1)S(1)}, u32[]{:S(2)}, u32[]{:S(2)}) %collective-permute-start.5) | collective-permute-done | bytes 262176 | tf_op jit(solution)/shard_map/ppermute | solution.py:164
  125.2 27.6 %all_to_all.17 = bf16[8,32,512]{2,1,0:T(8,128)(2,1)S(1)} all-to-all(bf16[8,32,512]{2,1,0:T(8,128)(2,1)S(1)} %shard_map.90), channel_id=1, replica_groups={{0,2,4,6,8,10,12,14},{1,3,5,7,9,11,13,15},{16,18,20,22,24,26,28,30},{17..., dimensions={0} | all-to-all | bytes 524288 | tf_op jit(solution)/shard_map/all_to_all | solution.py:176
  152.8 0.7 reduce_sum.12
  (2 shorter events, 0.1 us)
Async XLA Ops:
  0.6 44.1 %copy-start.1 = (bf16[512,832]{0,1:T(8,128)(2,1)S(1)}, bf16[512,832]{0,1:T(8,128)(2,1)}, u32[]{:S(2)}) copy-start(bf16[512,832]{0,1:T(8,128)(2,1)} %param.8) | copy-start | bytes 2555908
  0.6 44.1 %copy-start.2 = (bf16[512,832]{0,1:T(8,128)(2,1)S(1)}, bf16[512,832]{0,1:T(8,128)(2,1)}, u32[]{:S(2)}) copy-start(bf16[512,832]{0,1:T(8,128)(2,1)} %param.7) | copy-start | bytes 2555908
  38.8 8.3 %collective-permute-start = (bf16[4,2,32,512]{3,2,1,0:T(8,128)(2,1)S(1)}, bf16[4,2,32,512]{3,2,1,0:T(8,128)(2,1)S(1)}, u32[]{:S(2)}, u32[]{:S(2)}) collective-permute-start(bf16[4,2,32,512]{3,2,1,0:T(8,128)(2,1)S(1)} %bitcast.16), channel_id=1, source_target_pairs={{1,0},{2,1},{3,2},{4,3},{5,4},{6,5},{7,6},{8,7},{9,8},{10,9},{11,1... | collective-permute-start | bytes 786440 | tf_op jit(solution)/shard_map/ppermute | solution.py:123
  42.8 9.5 %collective-permute-start.1 = (bf16[4,2,32,512]{3,2,1,0:T(8,128)(2,1)S(1)}, bf16[4,2,32,512]{3,2,1,0:T(8,128)(2,1)S(1)}, u32[]{:S(2)}, u32[]{:S(2)}) collective-permute-start(bf16[4,2,32,512]{3,2,1,0:T(8,128)(2,1)S(1)} %bitcast.15), channel_id=1, source_target_pairs={{15,0},{0,1},{1,2},{2,3},{3,4},{4,5},{5,6},{6,7},{7,8},{8,9},{9,10... | collective-permute-start | bytes 786440 | tf_op jit(solution)/shard_map/ppermute | solution.py:123
  44.8 7.5 %copy-start = (bf16[832,512]{1,0:T(8,128)(2,1)S(1)}, bf16[832,512]{1,0:T(8,128)(2,1)}, u32[]{:S(2)}) copy-start(bf16[832,512]{1,0:T(8,128)(2,1)} %down.3) | copy-start | bytes 2555908
  53.2 6.8 %collective-permute-start.2 = (f32[16,16,1664]{2,1,0:T(8,128)S(1)}, f32[16,16,1664]{2,1,0:T(8,128)S(1)}, u32[]{:S(2)}, u32[]{:S(2)}) collective-permute-start(f32[16,16,1664]{2,1,0:T(8,128)S(1)} %get-tuple-element.12), channel_id=1, source_target_pairs={{0,16},{16,0},{1,17},{17,1},{2,18},{18,2},{3,19},{19,3},{4,20},{20... | collective-permute-start | bytes 5111816 | tf_op jit(solution)/shard_map/ppermute | solution.py:119
  55.2 4.9 %collective-permute-start.3 = (f32[16,16,832]{2,1,0:T(8,128)S(1)}, f32[16,16,832]{2,1,0:T(8,128)S(1)}, u32[]{:S(2)}, u32[]{:S(2)}) collective-permute-start(f32[16,16,832]{2,1,0:T(8,128)S(1)} %get-tuple-element.13), channel_id=1, source_target_pairs={{0,16},{16,0},{1,17},{17,1},{2,18},{18,2},{3,19},{19,3},{4,20},{20... | collective-permute-start | bytes 2555912 | tf_op jit(solution)/shard_map/ppermute | solution.py:119
  109.4 4.9 %collective-permute-start.4 = (bf16[16,16,2496]{2,1,0:T(8,128)(2,1)S(1)}, bf16[16,16,2496]{2,1,0:T(8,128)(2,1)S(1)}, u32[]{:S(2)}, u32[]{:S(2)}) collective-permute-start(bf16[16,16,2496]{2,1,0:T(8,128)(2,1)S(1)} %all_to_all.16.deltas.own), channel_id=1, source_target_pairs={{0,16},{16,0},{1,17},{17,1},{2,18},{18,2},{3,19},{19,3},{4,20},{20... | collective-permute-start | bytes 3833864 | tf_op jit(solution)/shard_map/ppermute | solution.py:119
  114.9 10.2 %collective-permute-start.5 = (bf16[8,32,512]{2,1,0:T(8,128)(2,1)S(1)}, bf16[8,32,512]{2,1,0:T(8,128)(2,1)S(1)}, u32[]{:S(2)}, u32[]{:S(2)}) collective-permute-start(bf16[8,32,512]{2,1,0:T(8,128)(2,1)S(1)} %get-tuple-element.15), channel_id=1, source_target_pairs={{0,1},{1,0},{2,3},{3,2},{4,5},{5,4},{6,7},{7,6},{8,9},{9,8},{10,11... | collective-permute-start | bytes 786440 | tf_op jit(solution)/shard_map/ppermute | solution.py:164

commit v9 on v8

--- a/solution.py
+++ b/solution.py
@@ -39,29 +39,50 @@
     )(*args, *after)
 
 
+def flat(value):
+    return value.reshape(-1, value.shape[-1])
+
+
+def first_rows(which, kind, even):
+    count = even.shape[0] // 2
+    return flat(even[pl.ds(which * count, count), kind])
+
+
+def second_rows(which, kind, low, high):
+    return flat(jnp.where(which == 0, low[:, kind], high[:, kind]))
+
+
+def send_body(rows, weights, out):
+    end = 0
+    for kind, weight in enumerate(weights):
+        lanes = slice(end, end + weight.shape[0])
+        end = lanes.stop
+        part = contract(rows(kind), weight[...], 1, 1)
+        out[:, :, lanes] = part.reshape(*out.shape[:2], -1)
+
+
+def send_first_body(where, even, pair, down, out):
+    send_body(lambda kind: first_rows(1 - where[0], kind, even), (pair, down), out)
+
+
+def send_second_body(where, low, high, pair, down, out):
+    send_body(lambda kind: second_rows(1 - where[0], kind, low, high), (pair, down), out)
+
+
 def half_rows(which, kind, even, low, high):
-    count, tokens, width = low.shape[0], *low.shape[2:]
-    first = even[pl.ds(which * count, count), kind]
-    second = jnp.where(which == 0, low[:, kind], high[:, kind])
-    return jnp.concatenate([first, second], 0).reshape(2 * count * tokens, width)
-
-
-def send_body(where, a, b, c, pair, down, pair_out, down_out):
-    for kind, weight, out in ((0, pair, pair_out), (1, down, down_out)):
-        rows = half_rows(1 - where[0], kind, a, b, c)
-        out[...] = contract(rows, weight[...], 1, 1).reshape(out.shape)
-
-
-def keep_body(where, a, b, c, pair, down, got_pair, got_down, out):
+    return jnp.concatenate(
+        [first_rows(which, kind, even), second_rows(which, kind, low, high)], 0
+    )
+
+
+def keep_body(where, even, low, high, pair, down, got_first, got_second, out):
     blocks, rows, _ = out.shape
-    wide = pair.shape[0]
-    for kind, weight, got, lanes in (
-        (0, pair, got_pair, slice(0, wide)),
-        (1, down, got_down, slice(wide, None)),
-    ):
-        mine = half_rows(where[0], kind, a, b, c)
+    wide, mid = pair.shape[0], blocks // 2
+    for kind, weight, lanes in ((0, pair, slice(0, wide)), (1, down, slice(wide, None))):
+        mine = half_rows(where[0], kind, even, low, high)
         total = contract(mine, weight[...], 1, 1).reshape(blocks, rows, -1)
-        out[:, :, lanes] = (total + got[...]).astype(BF16)
+        out[:mid, :, lanes] = (total[:mid] + got_first[:, :, lanes]).astype(BF16)
+        out[mid:, :, lanes] = (total[mid:] + got_second[:, :, lanes]).astype(BF16)
 
 
 def middle_body(parts, out):
@@ -86,17 +107,21 @@
     out[...] = part_of(deltas, pair)
 
 
-def other_body(where, deltas, pair, own, keep, send):
+def other_body(where, deltas, pair, own, keep, send_low, send_high):
     count, tokens = keep.shape[0] // 2, keep.shape[1]
-    parts = (own[...], part_of(deltas, pair))
-    for half, part in zip((where[0], 1 - where[0]), parts, strict=True):
-        rows = part.reshape(2 * count, tokens, -1)
-        keep[pl.ds(half * count, count)] = rows[:count]
-        send[pl.ds(half * count, count)] = rows[count:].astype(BF16)
-
-
-def add_body(keep, got, _, out):
-    out[...] = (keep[...] + got[...].astype(F32)).astype(BF16)
+    mine = own[...].reshape(2 * count, tokens, -1)
+    other = part_of(deltas, pair).reshape(2 * count, tokens, -1)
+    keep[pl.ds(where[0] * count, count)] = mine[:count]
+    keep[pl.ds((1 - where[0]) * count, count)] = other[:count]
+    mine, other = mine[count:].astype(BF16), other[count:].astype(BF16)
+    send_low[...] = jnp.where(where[0] == 0, mine, other)
+    send_high[...] = jnp.where(where[0] == 0, other, mine)
+
+
+def add_body(keep, got_low, got_high, _, out):
+    count = keep.shape[0] // 2
+    out[:count] = (keep[:count] + got_low[...].astype(F32)).astype(BF16)
+    out[count:] = (keep[count:] + got_high[...].astype(F32)).astype(BF16)
 
 
 def grads_body(where, a, b, c, own, other, gate_out, up_out, down_out, done):
@@ -139,29 +164,30 @@
 
     flops = 2 * half * units * width
     sds = jax.ShapeDtypeStruct
-    sent = call(
-        send_body,
-        (sds((n, half // n, 2 * units), F32), sds((n, half // n, units), F32)),
+    sent = sds((n // 2, half // n, 3 * units), F32)
+    weights = (pair, down_weight)
+    first = swap_cores(call(send_first_body, sent, 3 * flops // 2, where, even, *weights))
+    second = swap_cores(call(send_second_body, sent, 3 * flops // 2, where, low, high, *weights))
+    parts = call(
+        keep_body,
+        sds((n, half // n, 3 * units), BF16),
         3 * flops,
         where,
         *held,
-        pair,
-        down_weight,
-    )
-    sent = [swap_cores(value) for value in sent]
-    parts = call(
-        keep_body, sds((n, half // n, 3 * units), BF16), 3 * flops, where, *held, pair, down_weight, *sent
+        *weights,
+        first,
+        second,
     )
     parts = lax.all_to_all(parts, XY, 0, 0)
     row = call(middle_body, sds(parts.shape, BF16), 40 * half // n * units, parts)
     own = lax.all_to_all(row, XY, 0, 0)
     other = swap_cores(own)
     own_part = call(own_body, sds((half, width), F32), 2 * flops, own, pair)
-    slots = (n // 2, tokens, width)
-    keep, send = call(
-        other_body, (sds(slots, F32), sds(slots, BF16)), 2 * flops, where, other, pair, own_part
-    )
-    got = lax.ppermute(send, "col", [(i, i ^ 1) for i in range(n)])
+    slots, some = (n // 2, tokens, width), sds((n // 4, tokens, width), BF16)
+    keep, send_low, send_high = call(
+        other_body, (sds(slots, F32), some, some), 2 * flops, where, other, pair, own_part
+    )
+    got = (shift(send_low, 1), shift(send_high, -1))
     grad = sds((units, width), BF16)
     gate_grad, up_grad, down_grad, done = call(
         grads_body,
@@ -172,7 +198,7 @@
         own,
         other,
     )
-    pieces = call(add_body, sds(slots, BF16), 0, keep, got, after=(done,))
+    pieces = call(add_body, sds(slots, BF16), 0, keep, *got, after=(done,))
     pieces = lax.all_to_all(pieces, "col", 0, 0, axis_index_groups=parity)
     input_grad = jnp.sum(pieces.astype(F32), axis=0).astype(BF16)
     return (input_grad, gate_grad.T, up_grad.T, down_grad)

time: 154 us -> 152 us (0.987)
  waiting for transfers between devices: 18.1 us -> 11.2 us
  starting transfers between devices: 14.1 us -> 17.5 us
    ppermute x1 -> x0, waiting for transfers between devices: 5.85 us -> none  [per_device(): got = lax.ppermute(send, 'col', [(i, i ^ 1) for i in range(n)])]
    ppermute x2 -> x4, starting transfers between devices: 5.91 us -> 11.8 us  [shift(): return lax.ppermute(value, 'col', [((i + by) % 16, i) for i in range(16)])]
    ppermute x1 -> x0, starting transfers between devices: 1.92 us -> none  [per_device(): got = lax.ppermute(send, 'col', [(i, i ^ 1) for i in range(n)])]
    ppermute x2 -> x4, waiting for transfers between devices: 7.39 us -> 5.81 us  [shift(): return lax.ppermute(value, 'col', [((i + by) % 16, i) for i in range(16)])]
    pallas_call x7 -> x8, Pallas kernels: 6.01 us -> 6.96 us  [call(): pl.pallas_call(body, out_shape=outs, in_specs=[SMEM if a.dtype == jnp.int...]
  transfers between devices with their start and end apart: 6 -> 7, of which waited for: 5 -> 4; matrix products, arithmetic and copies ran while one was open for 0% -> 0% of each run, Pallas kernels for 2% -> 3%
where the time goes in v9:
time: 152 us
  blocking collectives  112 us (74%)
  starting transfers between devices  17.5 us (12%)
  waiting for transfers between devices  11.2 us (7%)
  Pallas kernels  6.96 us (5%)
  other arithmetic  1.67 us (1%)
    all_gather x1, blocking collectives, per_device(): even = lax.all_gather(both, 'col', axis=0, axis_index_groups=parity)  37.2 us
    all_to_all x1, blocking collectives, per_device(): pieces = lax.all_to_all(pieces, 'col', 0, 0, axis_index_groups=parity)  27.2 us
    all_to_all x1, blocking collectives, per_device(): parts = lax.all_to_all(parts, XY, 0, 0)  25.7 us
    all_to_all x1, blocking collectives, per_device(): own = lax.all_to_all(row, XY, 0, 0)  22.3 us
    ppermute x4, starting transfers between devices, shift(): return lax.ppermute(value, 'col', [((i + by) % 16, i) for i in range(16)])  11.8 us
    pallas_call x8, Pallas kernels, call(): pl.pallas_call(body, out_shape=outs, in_specs=[SMEM if a.dtype == jnp.int...  6.96 us
    ppermute x4, waiting for transfers between devices, shift(): return lax.ppermute(value, 'col', [((i + by) % 16, i) for i in range(16)])  5.81 us
    ppermute x3, starting transfers between devices, swap_cores(): return lax.ppermute(value, 'core', [(0, 1), (1, 0)])  5.75 us
  transfers between devices with their start and end apart: 7, of which 4 were waited for; matrix products, arithmetic and copies ran while one was open for 0% of the time, Pallas kernels for 3%

profile of v9, /device:TPU:8, one launch (start us, length us, event | category | flops | bytes accessed | tf_op | source)
XLA Modules:
  0.0 151.6 jit_solution(12210869865422952715)
XLA Ops:
  0.6 0.0 copy-start.1
  0.6 0.0 copy-start.2
  0.7 0.9 pad_maximum_fusion.1
  1.6 37.2 %all-gather = bf16[16,32,512]{2,1,0:T(8,128)(2,1)S(1)} all-gather(bf16[2,32,512]{2,1,0:T(8,128)(2,1)S(1)} %pad_maximum_fusion.1), channel_id=2, replica_groups={{0,2,4,6,8,10,12,14},{1,3,5,7,9,11,13,15},{16,18,20,22,24,26,28,30},{17..., dimensions={0}, use_global_device_ids=true | all-gather | bytes 589824 | tf_op jit(solution)/shard_map/all_gather | solution.py:161
  38.8 4.0 %collective-permute-start = (bf16[4,2,32,512]{3,2,1,0:T(8,128)(2,1)S(1)}, bf16[4,2,32,512]{3,2,1,0:T(8,128)(2,1)S(1)}, u32[]{:S(2)}, u32[]{:S(2)}) collective-permute-start(bf16[4,2,32,512]{3,2,1,0:T(8,128)(2,1)S(1)} %bitcast.16), channel_id=1, source_target_pairs={{1,0},{2,1},{3,2},{4,3},{5,4},{6,5},{7,6},{8,7},{9,8},{10,9},{11,1... | collective-permute-start | bytes 786440 | tf_op jit(solution)/shard_map/ppermute | solution.py:148
  42.8 1.9 %collective-permute-start.1 = (bf16[4,2,32,512]{3,2,1,0:T(8,128)(2,1)S(1)}, bf16[4,2,32,512]{3,2,1,0:T(8,128)(2,1)S(1)}, u32[]{:S(2)}, u32[]{:S(2)}) collective-permute-start(bf16[4,2,32,512]{3,2,1,0:T(8,128)(2,1)S(1)} %bitcast.15), channel_id=1, source_target_pairs={{15,0},{0,1},{1,2},{2,3},{3,4},{4,5},{5,6},{6,7},{7,8},{8,9},{9,10... | collective-permute-start | bytes 786440 | tf_op jit(solution)/shard_map/ppermute | solution.py:148
  44.8 0.0 copy-start
  44.8 0.1 pad_maximum_fusion.pair
  44.9 1.0 copy-done
  45.9 0.9 shard_map.84
  46.9 1.9 %collective-permute-start.2 = (f32[8,16,2496]{2,1,0:T(8,128)S(1)}, f32[8,16,2496]{2,1,0:T(8,128)S(1)}, u32[]{:S(2)}, u32[]{:S(2)}) collective-permute-start(f32[8,16,2496]{2,1,0:T(8,128)S(1)} %shard_map.84), channel_id=1, source_target_pairs={{0,16},{16,0},{1,17},{17,1},{2,18},{18,2},{3,19},{19,3},{4,20},{20... | collective-permute-start | bytes 3833864 | tf_op jit(solution)/shard_map/ppermute | solution.py:144
  48.8 0.0 collective-permute-done.low.b
  48.8 3.5 %collective-permute-done.1.high.c = bf16[4,2,32,512]{3,2,1,0:T(8,128)(2,1)S(1)} collective-permute-done((bf16[4,2,32,512]{3,2,1,0:T(8,128)(2,1)S(1)}, bf16[4,2,32,512]{3,2,1,0:T(8,128)(2,1)S(1)}, u32[]{:S(2)}, u32[]{:S(2)}) %collective-permute-start.1) | collective-permute-done | bytes 262176 | tf_op jit(solution)/shard_map/ppermute | solution.py:148
  52.3 0.9 shard_map.85
  53.2 1.9 %collective-permute-start.3 = (f32[8,16,2496]{2,1,0:T(8,128)S(1)}, f32[8,16,2496]{2,1,0:T(8,128)S(1)}, u32[]{:S(2)}, u32[]{:S(2)}) collective-permute-start(f32[8,16,2496]{2,1,0:T(8,128)S(1)} %shard_map.85), channel_id=1, source_target_pairs={{0,16},{16,0},{1,17},{17,1},{2,18},{18,2},{3,19},{19,3},{4,20},{20... | collective-permute-start | bytes 3833864 | tf_op jit(solution)/shard_map/ppermute | solution.py:144
  55.2 0.0 collective-permute-done.2.got_first
  55.2 3.0 %collective-permute-done.3.got_second = f32[8,16,2496]{2,1,0:T(8,128)S(1)} collective-permute-done((f32[8,16,2496]{2,1,0:T(8,128)S(1)}, f32[8,16,2496]{2,1,0:T(8,128)S(1)}, u32[]{:S(2)}, u32[]{:S(2)}) %collective-permute-start.3) | collective-permute-done | bytes 1277984 | tf_op jit(solution)/shard_map/ppermute | solution.py:144
  58.2 1.0 shard_map.86
  59.2 25.7 %all_to_all.15.parts = bf16[16,16,2496]{2,1,0:T(8,128)(2,1)S(1)} all-to-all(bf16[16,16,2496]{2,1,0:T(8,128)(2,1)S(1)} %shard_map.86), channel_id=1, replica_groups=mesh['x'=4,'y'=4,'core'=2,'col'=16] {'x','y'}, dimensions={0} | all-to-all | bytes 2555904 | tf_op jit(solution)/shard_map/all_to_all | solution.py:181
  84.9 0.3 shard_map.87
  85.2 22.3 %all_to_all.16.deltas.own = bf16[16,16,2496]{2,1,0:T(8,128)(2,1)S(1)} all-to-all(bf16[16,16,2496]{2,1,0:T(8,128)(2,1)S(1)} %shard_map.87), channel_id=1, replica_groups=mesh['x'=4,'y'=4,'core'=2,'col'=16] {'x','y'}, dimensions={0} | all-to-all | bytes 2555904 | tf_op jit(solution)/shard_map/all_to_all | solution.py:183
  107.5 1.9 %collective-permute-start.4 = (bf16[16,16,2496]{2,1,0:T(8,128)(2,1)S(1)}, bf16[16,16,2496]{2,1,0:T(8,128)(2,1)S(1)}, u32[]{:S(2)}, u32[]{:S(2)}) collective-permute-start(bf16[16,16,2496]{2,1,0:T(8,128)(2,1)S(1)} %all_to_all.16.deltas.own), channel_id=1, source_target_pairs={{0,16},{16,0},{1,17},{17,1},{2,18},{18,2},{3,19},{19,3},{4,20},{20... | collective-permute-start | bytes 3833864 | tf_op jit(solution)/shard_map/ppermute | solution.py:144
  109.4 0.6 shard_map.88.own
  110.0 2.4 %collective-permute-done.4.deltas.other = bf16[16,16,2496]{2,1,0:T(8,128)(2,1)S(1)} collective-permute-done((bf16[16,16,2496]{2,1,0:T(8,128)(2,1)S(1)}, bf16[16,16,2496]{2,1,0:T(8,128)(2,1)S(1)}, u32[]{:S(2)}, u32[]{:S(2)}) %collective-permute-start.4) | collective-permute-done | bytes 1277984 | tf_op jit(solution)/shard_map/ppermute | solution.py:144
  112.4 0.6 shard_map.89
  113.0 2.3 %collective-permute-start.5 = (bf16[4,32,512]{2,1,0:T(8,128)(2,1)S(1)}, bf16[4,32,512]{2,1,0:T(8,128)(2,1)S(1)}, u32[]{:S(2)}, u32[]{:S(2)}) collective-permute-start(bf16[4,32,512]{2,1,0:T(8,128)(2,1)S(1)} %get-tuple-element.12), channel_id=1, source_target_pairs={{1,0},{2,1},{3,2},{4,3},{5,4},{6,5},{7,6},{8,7},{9,8},{10,9},{11,1... | collective-permute-start | bytes 393224 | tf_op jit(solution)/shard_map/ppermute | solution.py:148
  115.3 3.6 %collective-permute-start.6 = (bf16[4,32,512]{2,1,0:T(8,128)(2,1)S(1)}, bf16[4,32,512]{2,1,0:T(8,128)(2,1)S(1)}, u32[]{:S(2)}, u32[]{:S(2)}) collective-permute-start(bf16[4,32,512]{2,1,0:T(8,128)(2,1)S(1)} %get-tuple-element.13), channel_id=1, source_target_pairs={{15,0},{0,1},{1,2},{2,3},{3,4},{4,5},{5,6},{6,7},{7,8},{8,9},{9,10... | collective-permute-start | bytes 393224 | tf_op jit(solution)/shard_map/ppermute | solution.py:148
  118.9 2.5 %shard_map.90 = (bf16[832,512]{1,0:T(8,128)(2,1)}, bf16[832,512]{1,0:T(8,128)(2,1)}, bf16[832,512]{1,0:T(8,128)(2,1)}, f32[8,128]{1,0:T(8,128)S(1)}) custom-call(s32[1]{0:T(128)} %bitcast.where, bf16[8,2,32,512]{3,2,1,0:T(8,128)(2,1)S(1)} %bitcast.12, bf16[4,2,32,512]{3,2,1,0:T(8,128)(2,1)S(1)} %collective-permute-done.low.b, ...), custom_call_target="tpu_custom_call" | custom-call | flops 1308622848 | bytes 6164484 | tf_op jit(solution)/shard_map/pallas_call | solution.py:32
  121.4 0.0 collective-permute-done.5.got_low
  121.4 2.3 %collective-permute-done.6.got_high = bf16[4,32,512]{2,1,0:T(8,128)(2,1)S(1)} collective-permute-done((bf16[4,32,512]{2,1,0:T(8,128)(2,1)S(1)}, bf16[4,32,512]{2,1,0:T(8,128)(2,1)S(1)}, u32[]{:S(2)}, u32[]{:S(2)}) %collective-permute-start.6) | collective-permute-done | bytes 131104 | tf_op jit(solution)/shard_map/ppermute | solution.py:148
  123.7 27.2 %all_to_all.17 = bf16[8,32,512]{2,1,0:T(8,128)(2,1)S(1)} all-to-all(bf16[8,32,512]{2,1,0:T(8,128)(2,1)S(1)} %shard_map.91), channel_id=1, replica_groups={{0,2,4,6,8,10,12,14},{1,3,5,7,9,11,13,15},{16,18,20,22,24,26,28,30},{17..., dimensions={0} | all-to-all | bytes 524288 | tf_op jit(solution)/shard_map/all_to_all | solution.py:202
  150.9 0.7 reduce_sum.12
  (4 shorter events, 0.1 us)
Async XLA Ops:
  0.6 44.1 %copy-start.1 = (bf16[512,832]{0,1:T(8,128)(2,1)S(1)}, bf16[512,832]{0,1:T(8,128)(2,1)}, u32[]{:S(2)}) copy-start(bf16[512,832]{0,1:T(8,128)(2,1)} %param.8) | copy-start | bytes 2555908
  0.6 44.1 %copy-start.2 = (bf16[512,832]{0,1:T(8,128)(2,1)S(1)}, bf16[512,832]{0,1:T(8,128)(2,1)}, u32[]{:S(2)}) copy-start(bf16[512,832]{0,1:T(8,128)(2,1)} %param.7) | copy-start | bytes 2555908
  38.8 10.0 %collective-permute-start = (bf16[4,2,32,512]{3,2,1,0:T(8,128)(2,1)S(1)}, bf16[4,2,32,512]{3,2,1,0:T(8,128)(2,1)S(1)}, u32[]{:S(2)}, u32[]{:S(2)}) collective-permute-start(bf16[4,2,32,512]{3,2,1,0:T(8,128)(2,1)S(1)} %bitcast.16), channel_id=1, source_target_pairs={{1,0},{2,1},{3,2},{4,3},{5,4},{6,5},{7,6},{8,7},{9,8},{10,9},{11,1... | collective-permute-start | bytes 786440 | tf_op jit(solution)/shard_map/ppermute | solution.py:148
  42.8 9.5 %collective-permute-start.1 = (bf16[4,2,32,512]{3,2,1,0:T(8,128)(2,1)S(1)}, bf16[4,2,32,512]{3,2,1,0:T(8,128)(2,1)S(1)}, u32[]{:S(2)}, u32[]{:S(2)}) collective-permute-start(bf16[4,2,32,512]{3,2,1,0:T(8,128)(2,1)S(1)} %bitcast.15), channel_id=1, source_target_pairs={{15,0},{0,1},{1,2},{2,3},{3,4},{4,5},{5,6},{6,7},{7,8},{8,9},{9,10... | collective-permute-start | bytes 786440 | tf_op jit(solution)/shard_map/ppermute | solution.py:148
  44.8 1.2 copy-start
  46.9 8.3 %collective-permute-start.2 = (f32[8,16,2496]{2,1,0:T(8,128)S(1)}, f32[8,16,2496]{2,1,0:T(8,128)S(1)}, u32[]{:S(2)}, u32[]{:S(2)}) collective-permute-start(f32[8,16,2496]{2,1,0:T(8,128)S(1)} %shard_map.84), channel_id=1, source_target_pairs={{0,16},{16,0},{1,17},{17,1},{2,18},{18,2},{3,19},{19,3},{4,20},{20... | collective-permute-start | bytes 3833864 | tf_op jit(solution)/shard_map/ppermute | solution.py:144
  53.2 4.9 %collective-permute-start.3 = (f32[8,16,2496]{2,1,0:T(8,128)S(1)}, f32[8,16,2496]{2,1,0:T(8,128)S(1)}, u32[]{:S(2)}, u32[]{:S(2)}) collective-permute-start(f32[8,16,2496]{2,1,0:T(8,128)S(1)} %shard_map.85), channel_id=1, source_target_pairs={{0,16},{16,0},{1,17},{17,1},{2,18},{18,2},{3,19},{19,3},{4,20},{20... | collective-permute-start | bytes 3833864 | tf_op jit(solution)/shard_map/ppermute | solution.py:144
  107.5 4.9 %collective-permute-start.4 = (bf16[16,16,2496]{2,1,0:T(8,128)(2,1)S(1)}, bf16[16,16,2496]{2,1,0:T(8,128)(2,1)S(1)}, u32[]{:S(2)}, u32[]{:S(2)}) collective-permute-start(bf16[16,16,2496]{2,1,0:T(8,128)(2,1)S(1)} %all_to_all.16.deltas.own), channel_id=1, source_target_pairs={{0,16},{16,0},{1,17},{17,1},{2,18},{18,2},{3,19},{19,3},{4,20},{20... | collective-permute-start | bytes 3833864 | tf_op jit(solution)/shard_map/ppermute | solution.py:144
  113.0 8.3 %collective-permute-start.5 = (bf16[4,32,512]{2,1,0:T(8,128)(2,1)S(1)}, bf16[4,32,512]{2,1,0:T(8,128)(2,1)S(1)}, u32[]{:S(2)}, u32[]{:S(2)}) collective-permute-start(bf16[4,32,512]{2,1,0:T(8,128)(2,1)S(1)} %get-tuple-element.12), channel_id=1, source_target_pairs={{1,0},{2,1},{3,2},{4,3},{5,4},{6,5},{7,6},{8,7},{9,8},{10,9},{11,1... | collective-permute-start | bytes 393224 | tf_op jit(solution)/shard_map/ppermute | solution.py:148
  115.3 8.4 %collective-permute-start.6 = (bf16[4,32,512]{2,1,0:T(8,128)(2,1)S(1)}, bf16[4,32,512]{2,1,0:T(8,128)(2,1)S(1)}, u32[]{:S(2)}, u32[]{:S(2)}) collective-permute-start(bf16[4,32,512]{2,1,0:T(8,128)(2,1)S(1)} %get-tuple-element.13), channel_id=1, source_target_pairs={{15,0},{0,1},{1,2},{2,3},{3,4},{4,5},{5,6},{6,7},{7,8},{8,9},{9,10... | collective-permute-start | bytes 393224 | tf_op jit(solution)/shard_map/ppermute | solution.py:148

commit v10 on v9

--- a/solution.py
+++ b/solution.py
@@ -103,25 +103,16 @@
     return contract(rows, pair[...], 1, 0)
 
 
-def own_body(deltas, pair, out):
-    out[...] = part_of(deltas, pair)
-
-
-def other_body(where, deltas, pair, own, keep, send_low, send_high):
-    count, tokens = keep.shape[0] // 2, keep.shape[1]
-    mine = own[...].reshape(2 * count, tokens, -1)
-    other = part_of(deltas, pair).reshape(2 * count, tokens, -1)
-    keep[pl.ds(where[0] * count, count)] = mine[:count]
-    keep[pl.ds((1 - where[0]) * count, count)] = other[:count]
-    mine, other = mine[count:].astype(BF16), other[count:].astype(BF16)
-    send_low[...] = jnp.where(where[0] == 0, mine, other)
-    send_high[...] = jnp.where(where[0] == 0, other, mine)
-
-
-def add_body(keep, got_low, got_high, _, out):
-    count = keep.shape[0] // 2
-    out[:count] = (keep[:count] + got_low[...].astype(F32)).astype(BF16)
-    out[count:] = (keep[count:] + got_high[...].astype(F32)).astype(BF16)
+def part_body(deltas, pair, keep, send):
+    part = part_of(deltas, pair).reshape(2 * keep.shape[0], *keep.shape[1:])
+    keep[...] = part[: keep.shape[0]]
+    send[...] = part[keep.shape[0] :].astype(BF16)
+
+
+def add_body(where, keep_own, got_own, keep_other, got_other, _, out):
+    count = keep_own.shape[0]
+    for half, keep, got in ((where[0], keep_own, got_own), (1 - where[0], keep_other, got_other)):
+        out[pl.ds(half * count, count)] = (keep[...] + got[...].astype(F32)).astype(BF16)
 
 
 def grads_body(where, a, b, c, own, other, gate_out, up_out, down_out, done):
@@ -144,8 +135,9 @@
     return lax.ppermute(value, "core", [(0, 1), (1, 0)])
 
 
-def shift(value, by):
-    return lax.ppermute(value, "col", [((i + by) % 16, i) for i in range(16)])
+def from_neighbour(value, by):
+    pairs = [(c * 16 + (i + by[c]) % 16, c * 16 + i) for c in range(2) for i in range(16)]
+    return lax.ppermute(value, ("core", "col"), pairs)
 
 
 def per_device(inputs, out_grad, gate_weight, up_weight, down_weight):
@@ -159,7 +151,8 @@
     parity = [list(range(i, n, 2)) for i in range(2)]
     both = jnp.stack([inputs, out_grad])
     even = lax.all_gather(both, "col", axis=0, axis_index_groups=parity)
-    low, high = shift(even[: n // 4], 1), shift(even[n // 4 :], -1)
+    low = from_neighbour(even[: n // 4], (1, 1))
+    high = from_neighbour(even[n // 4 :], (-1, -1))
     held = (even, low, high)
 
     flops = 2 * half * units * width
@@ -182,12 +175,12 @@
     row = call(middle_body, sds(parts.shape, BF16), 40 * half // n * units, parts)
     own = lax.all_to_all(row, XY, 0, 0)
     other = swap_cores(own)
-    own_part = call(own_body, sds((half, width), F32), 2 * flops, own, pair)
-    slots, some = (n // 2, tokens, width), sds((n // 4, tokens, width), BF16)
-    keep, send_low, send_high = call(
-        other_body, (sds(slots, F32), some, some), 2 * flops, where, other, pair, own_part
-    )
-    got = (shift(send_low, 1), shift(send_high, -1))
+    some = (n // 4, tokens, width)
+    outs = (sds(some, F32), sds(some, BF16))
+    keep_own, send_own = call(part_body, outs, 2 * flops, own, pair)
+    got_own = from_neighbour(send_own, (1, -1))
+    keep_other, send_other = call(part_body, outs, 2 * flops, other, pair)
+    got_other = from_neighbour(send_other, (-1, 1))
     grad = sds((units, width), BF16)
     gate_grad, up_grad, down_grad, done = call(
         grads_body,
@@ -198,7 +191,8 @@
         own,
         other,
     )
-    pieces = call(add_body, sds(slots, BF16), 0, keep, *got, after=(done,))
+    added = (keep_own, got_own, keep_other, got_other)
+    pieces = call(add_body, sds((n // 2, tokens, width), BF16), 0, where, *added, after=(done,))
     pieces = lax.all_to_all(pieces, "col", 0, 0, axis_index_groups=parity)
     input_grad = jnp.sum(pieces.astype(F32), axis=0).astype(BF16)
     return (input_grad, gate_grad.T, up_grad.T, down_grad)

time: 152 us -> 150 us (0.987)
  waiting for transfers between devices: 11.2 us -> 8.66 us
    ppermute x3, waiting for transfers between devices: 5.35 us -> 3.06 us  [swap_cores(): return lax.ppermute(value, 'core', [(0, 1), (1, 0)])]
  transfers between devices with their start and end apart: 7 -> 7, of which waited for: 4 -> 4; matrix products, arithmetic and copies ran while one was open for 0% -> 0% of each run, Pallas kernels for 3% -> 4%
where the time goes in v10:
time: 150 us
  blocking collectives  113 us (75%)
  starting transfers between devices  17.5 us (12%)
  waiting for transfers between devices  8.66 us (6%)
  Pallas kernels  6.95 us (5%)
  other arithmetic  1.67 us (1%)
    all_gather x1, blocking collectives, per_device(): even = lax.all_gather(both, 'col', axis=0, axis_index_groups=parity)  37.2 us
    all_to_all x1, blocking collectives, per_device(): pieces = lax.all_to_all(pieces, 'col', 0, 0, axis_index_groups=parity)  27.7 us
    all_to_all x1, blocking collectives, per_device(): parts = lax.all_to_all(parts, XY, 0, 0)  25.7 us
    all_to_all x1, blocking collectives, per_device(): own = lax.all_to_all(row, XY, 0, 0)  22.3 us
    ppermute x4, starting transfers between devices, from_neighbour(): return lax.ppermute(value, ('core', 'col'), pairs)  11.7 us
    pallas_call x8, Pallas kernels, call(): pl.pallas_call(body, out_shape=outs, in_specs=[SMEM if a.dtype == jnp.int...  6.95 us
    ppermute x3, starting transfers between devices, swap_cores(): return lax.ppermute(value, 'core', [(0, 1), (1, 0)])  5.75 us
    ppermute x4, waiting for transfers between devices, from_neighbour(): return lax.ppermute(value, ('core', 'col'), pairs)  5.61 us
  transfers between devices with their start and end apart: 7, of which 4 were waited for; matrix products, arithmetic and copies ran while one was open for 0% of the time, Pallas kernels for 4%

profile of v10, /device:TPU:8, one launch (start us, length us, event | category | flops | bytes accessed | tf_op | source)
XLA Modules:
  0.0 149.5 jit_solution(8593502632451745421)
XLA Ops:
  0.6 0.0 copy-start.1
  0.7 0.9 pad_maximum_fusion.1
  1.6 37.2 %all-gather = bf16[16,32,512]{2,1,0:T(8,128)(2,1)S(1)} all-gather(bf16[2,32,512]{2,1,0:T(8,128)(2,1)S(1)} %pad_maximum_fusion.1), channel_id=2, replica_groups={{0,2,4,6,8,10,12,14},{1,3,5,7,9,11,13,15},{16,18,20,22,24,26,28,30},{17..., dimensions={0}, use_global_device_ids=true | all-gather | bytes 589824 | tf_op jit(solution)/shard_map/all_gather | solution.py:153
  38.8 4.0 %collective-permute-start = (bf16[4,2,32,512]{3,2,1,0:T(8,128)(2,1)S(1)}, bf16[4,2,32,512]{3,2,1,0:T(8,128)(2,1)S(1)}, u32[]{:S(2)}, u32[]{:S(2)}) collective-permute-start(bf16[4,2,32,512]{3,2,1,0:T(8,128)(2,1)S(1)} %bitcast.16), channel_id=1, source_target_pairs={{1,0},{2,1},{3,2},{4,3},{5,4},{6,5},{7,6},{8,7},{9,8},{10,9},{11,1... | collective-permute-start | bytes 786440 | tf_op jit(solution)/shard_map/ppermute | solution.py:140
  42.8 1.9 %collective-permute-start.1 = (bf16[4,2,32,512]{3,2,1,0:T(8,128)(2,1)S(1)}, bf16[4,2,32,512]{3,2,1,0:T(8,128)(2,1)S(1)}, u32[]{:S(2)}, u32[]{:S(2)}) collective-permute-start(bf16[4,2,32,512]{3,2,1,0:T(8,128)(2,1)S(1)} %bitcast.15), channel_id=1, source_target_pairs={{15,0},{0,1},{1,2},{2,3},{3,4},{4,5},{5,6},{6,7},{7,8},{8,9},{9,10... | collective-permute-start | bytes 786440 | tf_op jit(solution)/shard_map/ppermute | solution.py:140
  44.8 0.0 copy-start
  44.8 0.1 pad_maximum_fusion.pair
  44.9 1.0 copy-done
  45.9 0.9 shard_map.84
  46.9 1.9 %collective-permute-start.2 = (f32[8,16,2496]{2,1,0:T(8,128)S(1)}, f32[8,16,2496]{2,1,0:T(8,128)S(1)}, u32[]{:S(2)}, u32[]{:S(2)}) collective-permute-start(f32[8,16,2496]{2,1,0:T(8,128)S(1)} %shard_map.84), channel_id=1, source_target_pairs={{0,16},{16,0},{1,17},{17,1},{2,18},{18,2},{3,19},{19,3},{4,20},{20... | collective-permute-start | bytes 3833864 | tf_op jit(solution)/shard_map/ppermute | solution.py:135
  48.8 0.0 collective-permute-done.low.b
  48.8 3.5 %collective-permute-done.1.high.c = bf16[4,2,32,512]{3,2,1,0:T(8,128)(2,1)S(1)} collective-permute-done((bf16[4,2,32,512]{3,2,1,0:T(8,128)(2,1)S(1)}, bf16[4,2,32,512]{3,2,1,0:T(8,128)(2,1)S(1)}, u32[]{:S(2)}, u32[]{:S(2)}) %collective-permute-start.1) | collective-permute-done | bytes 262176 | tf_op jit(solution)/shard_map/ppermute | solution.py:140
  52.3 0.9 shard_map.85
  53.2 1.9 %collective-permute-start.3 = (f32[8,16,2496]{2,1,0:T(8,128)S(1)}, f32[8,16,2496]{2,1,0:T(8,128)S(1)}, u32[]{:S(2)}, u32[]{:S(2)}) collective-permute-start(f32[8,16,2496]{2,1,0:T(8,128)S(1)} %shard_map.85), channel_id=1, source_target_pairs={{0,16},{16,0},{1,17},{17,1},{2,18},{18,2},{3,19},{19,3},{4,20},{20... | collective-permute-start | bytes 3833864 | tf_op jit(solution)/shard_map/ppermute | solution.py:135
  55.2 0.0 collective-permute-done.2.got_first
  55.2 3.0 %collective-permute-done.3.got_second = f32[8,16,2496]{2,1,0:T(8,128)S(1)} collective-permute-done((f32[8,16,2496]{2,1,0:T(8,128)S(1)}, f32[8,16,2496]{2,1,0:T(8,128)S(1)}, u32[]{:S(2)}, u32[]{:S(2)}) %collective-permute-start.3) | collective-permute-done | bytes 1277984 | tf_op jit(solution)/shard_map/ppermute | solution.py:135
  58.2 1.0 shard_map.86
  59.2 25.7 %all_to_all.15.parts = bf16[16,16,2496]{2,1,0:T(8,128)(2,1)S(1)} all-to-all(bf16[16,16,2496]{2,1,0:T(8,128)(2,1)S(1)} %shard_map.86), channel_id=1, replica_groups=mesh['x'=4,'y'=4,'core'=2,'col'=16] {'x','y'}, dimensions={0} | all-to-all | bytes 2555904 | tf_op jit(solution)/shard_map/all_to_all | solution.py:174
  84.9 0.3 shard_map.87
  85.2 22.3 %all_to_all.16.deltas.own = bf16[16,16,2496]{2,1,0:T(8,128)(2,1)S(1)} all-to-all(bf16[16,16,2496]{2,1,0:T(8,128)(2,1)S(1)} %shard_map.87), channel_id=1, replica_groups=mesh['x'=4,'y'=4,'core'=2,'col'=16] {'x','y'}, dimensions={0} | all-to-all | bytes 2555904 | tf_op jit(solution)/shard_map/all_to_all | solution.py:176
  107.5 1.9 %collective-permute-start.5 = (bf16[16,16,2496]{2,1,0:T(8,128)(2,1)S(1)}, bf16[16,16,2496]{2,1,0:T(8,128)(2,1)S(1)}, u32[]{:S(2)}, u32[]{:S(2)}) collective-permute-start(bf16[16,16,2496]{2,1,0:T(8,128)(2,1)S(1)} %all_to_all.16.deltas.own), channel_id=1, source_target_pairs={{0,16},{16,0},{1,17},{17,1},{2,18},{18,2},{3,19},{19,3},{4,20},{20... | collective-permute-start | bytes 3833864 | tf_op jit(solution)/shard_map/ppermute | solution.py:135
  109.4 0.6 shard_map.88
  110.0 2.3 %collective-permute-start.4 = (bf16[4,32,512]{2,1,0:T(8,128)(2,1)S(1)}, bf16[4,32,512]{2,1,0:T(8,128)(2,1)S(1)}, u32[]{:S(2)}, u32[]{:S(2)}) collective-permute-start(bf16[4,32,512]{2,1,0:T(8,128)(2,1)S(1)} %get-tuple-element.13), channel_id=1, source_target_pairs={{1,0},{2,1},{3,2},{4,3},{5,4},{6,5},{7,6},{8,7},{9,8},{10,9},{11,1... | collective-permute-start | bytes 393224 | tf_op jit(solution)/shard_map/ppermute | solution.py:140
  112.3 0.1 collective-permute-done.5.deltas.other
  112.4 0.6 shard_map.89
  113.0 3.5 %collective-permute-start.6 = (bf16[4,32,512]{2,1,0:T(8,128)(2,1)S(1)}, bf16[4,32,512]{2,1,0:T(8,128)(2,1)S(1)}, u32[]{:S(2)}, u32[]{:S(2)}) collective-permute-start(bf16[4,32,512]{2,1,0:T(8,128)(2,1)S(1)} %get-tuple-element.15), channel_id=1, source_target_pairs={{15,0},{0,1},{1,2},{2,3},{3,4},{4,5},{5,6},{6,7},{7,8},{8,9},{9,10... | collective-permute-start | bytes 393224 | tf_op jit(solution)/shard_map/ppermute | solution.py:140
  116.5 2.4 %shard_map.90 = (bf16[832,512]{1,0:T(8,128)(2,1)}, bf16[832,512]{1,0:T(8,128)(2,1)}, bf16[832,512]{1,0:T(8,128)(2,1)}, f32[8,128]{1,0:T(8,128)S(1)}) custom-call(s32[1]{0:T(128)} %bitcast.where, bf16[8,2,32,512]{3,2,1,0:T(8,128)(2,1)S(1)} %bitcast.12, bf16[4,2,32,512]{3,2,1,0:T(8,128)(2,1)S(1)} %collective-permute-done.low.b, ...), custom_call_target="tpu_custom_call" | custom-call | flops 1308622848 | bytes 6164484 | tf_op jit(solution)/shard_map/pallas_call | solution.py:32
  119.0 0.0 collective-permute-done.4.got_own
  119.0 2.1 %collective-permute-done.6.got_other = bf16[4,32,512]{2,1,0:T(8,128)(2,1)S(1)} collective-permute-done((bf16[4,32,512]{2,1,0:T(8,128)(2,1)S(1)}, bf16[4,32,512]{2,1,0:T(8,128)(2,1)S(1)}, u32[]{:S(2)}, u32[]{:S(2)}) %collective-permute-start.6) | collective-permute-done | bytes 131104 | tf_op jit(solution)/shard_map/ppermute | solution.py:140
  121.1 0.1 shard_map.91
  121.2 27.7 %all_to_all.17 = bf16[8,32,512]{2,1,0:T(8,128)(2,1)S(1)} all-to-all(bf16[8,32,512]{2,1,0:T(8,128)(2,1)S(1)} %shard_map.91), channel_id=1, replica_groups={{0,2,4,6,8,10,12,14},{1,3,5,7,9,11,13,15},{16,18,20,22,24,26,28,30},{17..., dimensions={0} | all-to-all | bytes 524288 | tf_op jit(solution)/shard_map/all_to_all | solution.py:196
  148.9 0.7 reduce_sum.12
  (4 shorter events, 0.0 us)
Async XLA Ops:
  0.6 44.1 %copy-start.1 = (bf16[512,832]{0,1:T(8,128)(2,1)S(1)}, bf16[512,832]{0,1:T(8,128)(2,1)}, u32[]{:S(2)}) copy-start(bf16[512,832]{0,1:T(8,128)(2,1)} %param.8) | copy-start | bytes 2555908
  0.6 44.1 %copy-start.2 = (bf16[512,832]{0,1:T(8,128)(2,1)S(1)}, bf16[512,832]{0,1:T(8,128)(2,1)}, u32[]{:S(2)}) copy-start(bf16[512,832]{0,1:T(8,128)(2,1)} %param.7) | copy-start | bytes 2555908
  38.8 10.0 %collective-permute-start = (bf16[4,2,32,512]{3,2,1,0:T(8,128)(2,1)S(1)}, bf16[4,2,32,512]{3,2,1,0:T(8,128)(2,1)S(1)}, u32[]{:S(2)}, u32[]{:S(2)}) collective-permute-start(bf16[4,2,32,512]{3,2,1,0:T(8,128)(2,1)S(1)} %bitcast.16), channel_id=1, source_target_pairs={{1,0},{2,1},{3,2},{4,3},{5,4},{6,5},{7,6},{8,7},{9,8},{10,9},{11,1... | collective-permute-start | bytes 786440 | tf_op jit(solution)/shard_map/ppermute | solution.py:140
  42.8 9.5 %collective-permute-start.1 = (bf16[4,2,32,512]{3,2,1,0:T(8,128)(2,1)S(1)}, bf16[4,2,32,512]{3,2,1,0:T(8,128)(2,1)S(1)}, u32[]{:S(2)}, u32[]{:S(2)}) collective-permute-start(bf16[4,2,32,512]{3,2,1,0:T(8,128)(2,1)S(1)} %bitcast.15), channel_id=1, source_target_pairs={{15,0},{0,1},{1,2},{2,3},{3,4},{4,5},{5,6},{6,7},{7,8},{8,9},{9,10... | collective-permute-start | bytes 786440 | tf_op jit(solution)/shard_map/ppermute | solution.py:140
  44.8 1.2 copy-start
  46.9 8.3 %collective-permute-start.2 = (f32[8,16,2496]{2,1,0:T(8,128)S(1)}, f32[8,16,2496]{2,1,0:T(8,128)S(1)}, u32[]{:S(2)}, u32[]{:S(2)}) collective-permute-start(f32[8,16,2496]{2,1,0:T(8,128)S(1)} %shard_map.84), channel_id=1, source_target_pairs={{0,16},{16,0},{1,17},{17,1},{2,18},{18,2},{3,19},{19,3},{4,20},{20... | collective-permute-start | bytes 3833864 | tf_op jit(solution)/shard_map/ppermute | solution.py:135
  53.2 4.9 %collective-permute-start.3 = (f32[8,16,2496]{2,1,0:T(8,128)S(1)}, f32[8,16,2496]{2,1,0:T(8,128)S(1)}, u32[]{:S(2)}, u32[]{:S(2)}) collective-permute-start(f32[8,16,2496]{2,1,0:T(8,128)S(1)} %shard_map.85), channel_id=1, source_target_pairs={{0,16},{16,0},{1,17},{17,1},{2,18},{18,2},{3,19},{19,3},{4,20},{20... | collective-permute-start | bytes 3833864 | tf_op jit(solution)/shard_map/ppermute | solution.py:135
  107.5 4.9 %collective-permute-start.5 = (bf16[16,16,2496]{2,1,0:T(8,128)(2,1)S(1)}, bf16[16,16,2496]{2,1,0:T(8,128)(2,1)S(1)}, u32[]{:S(2)}, u32[]{:S(2)}) collective-permute-start(bf16[16,16,2496]{2,1,0:T(8,128)(2,1)S(1)} %all_to_all.16.deltas.own), channel_id=1, source_target_pairs={{0,16},{16,0},{1,17},{17,1},{2,18},{18,2},{3,19},{19,3},{4,20},{20... | collective-permute-start | bytes 3833864 | tf_op jit(solution)/shard_map/ppermute | solution.py:135
  110.0 8.9 %collective-permute-start.4 = (bf16[4,32,512]{2,1,0:T(8,128)(2,1)S(1)}, bf16[4,32,512]{2,1,0:T(8,128)(2,1)S(1)}, u32[]{:S(2)}, u32[]{:S(2)}) collective-permute-start(bf16[4,32,512]{2,1,0:T(8,128)(2,1)S(1)} %get-tuple-element.13), channel_id=1, source_target_pairs={{1,0},{2,1},{3,2},{4,3},{5,4},{6,5},{7,6},{8,7},{9,8},{10,9},{11,1... | collective-permute-start | bytes 393224 | tf_op jit(solution)/shard_map/ppermute | solution.py:140
  113.0 8.1 %collective-permute-start.6 = (bf16[4,32,512]{2,1,0:T(8,128)(2,1)S(1)}, bf16[4,32,512]{2,1,0:T(8,128)(2,1)S(1)}, u32[]{:S(2)}, u32[]{:S(2)}) collective-permute-start(bf16[4,32,512]{2,1,0:T(8,128)(2,1)S(1)} %get-tuple-element.15), channel_id=1, source_target_pairs={{15,0},{0,1},{1,2},{2,3},{3,4},{4,5},{5,6},{6,7},{7,8},{8,9},{9,10... | collective-permute-start | bytes 393224 | tf_op jit(solution)/shard_map/ppermute | solution.py:140

commit v11 on v10

--- a/solution.py
+++ b/solution.py
@@ -48,10 +48,6 @@
     return flat(even[pl.ds(which * count, count), kind])
 
 
-def second_rows(which, kind, low, high):
-    return flat(jnp.where(which == 0, low[:, kind], high[:, kind]))
-
-
 def send_body(rows, weights, out):
     end = 0
     for kind, weight in enumerate(weights):
@@ -65,22 +61,20 @@
     send_body(lambda kind: first_rows(1 - where[0], kind, even), (pair, down), out)
 
 
-def send_second_body(where, low, high, pair, down, out):
-    send_body(lambda kind: second_rows(1 - where[0], kind, low, high), (pair, down), out)
-
-
-def half_rows(which, kind, even, low, high):
-    return jnp.concatenate(
-        [first_rows(which, kind, even), second_rows(which, kind, low, high)], 0
-    )
-
-
-def keep_body(where, even, low, high, pair, down, got_first, got_second, out):
+def send_second_body(theirs, pair, down, out):
+    send_body(lambda kind: flat(theirs[:, kind]), (pair, down), out)
+
+
+def half_rows(which, kind, even, odd):
+    return jnp.concatenate([first_rows(which, kind, even), flat(odd[:, kind])], 0)
+
+
+def keep_body(where, even, mine, pair, down, got_first, got_second, out):
     blocks, rows, _ = out.shape
     wide, mid = pair.shape[0], blocks // 2
     for kind, weight, lanes in ((0, pair, slice(0, wide)), (1, down, slice(wide, None))):
-        mine = half_rows(where[0], kind, even, low, high)
-        total = contract(mine, weight[...], 1, 1).reshape(blocks, rows, -1)
+        rows_in = half_rows(where[0], kind, even, mine)
+        total = contract(rows_in, weight[...], 1, 1).reshape(blocks, rows, -1)
         out[:mid, :, lanes] = (total[:mid] + got_first[:, :, lanes]).astype(BF16)
         out[mid:, :, lanes] = (total[mid:] + got_second[:, :, lanes]).astype(BF16)
 
@@ -115,14 +109,14 @@
         out[pl.ds(half * count, count)] = (keep[...] + got[...].astype(F32)).astype(BF16)
 
 
-def grads_body(where, a, b, c, own, other, gate_out, up_out, down_out, done):
+def grads_body(where, even, mine, theirs, own, other, gate_out, up_out, down_out, done):
     done[...] = jnp.zeros_like(done)
     units = gate_out.shape[0]
     deltas = [ref[...].reshape(-1, ref.shape[-1]) for ref in (own, other)]
 
     def total_of(kind, lanes):
-        halves = (where[0], 1 - where[0])
-        rows = jnp.concatenate([half_rows(h, kind, a, b, c) for h in halves], 0)
+        halves = ((where[0], mine), (1 - where[0], theirs))
+        rows = jnp.concatenate([half_rows(h, kind, even, odd) for h, odd in halves], 0)
         return contract(jnp.concatenate([m[:, lanes] for m in deltas], 0), rows, 0, 0).astype(BF16)
 
     pair = total_of(0, slice(0, 2 * units))
@@ -151,22 +145,23 @@
     parity = [list(range(i, n, 2)) for i in range(2)]
     both = jnp.stack([inputs, out_grad])
     even = lax.all_gather(both, "col", axis=0, axis_index_groups=parity)
-    low = from_neighbour(even[: n // 4], (1, 1))
-    high = from_neighbour(even[n // 4 :], (-1, -1))
-    held = (even, low, high)
+    count, core = n // 4, lax.axis_index("core")
+    parts_of = [lax.dynamic_slice_in_dim(even, c * count, count, 0) for c in (1 - core, core)]
+    theirs, mine = from_neighbour(parts_of[0], (-1, 1)), from_neighbour(parts_of[1], (1, -1))
 
     flops = 2 * half * units * width
     sds = jax.ShapeDtypeStruct
     sent = sds((n // 2, half // n, 3 * units), F32)
     weights = (pair, down_weight)
     first = swap_cores(call(send_first_body, sent, 3 * flops // 2, where, even, *weights))
-    second = swap_cores(call(send_second_body, sent, 3 * flops // 2, where, low, high, *weights))
+    second = swap_cores(call(send_second_body, sent, 3 * flops // 2, theirs, *weights))
     parts = call(
         keep_body,
         sds((n, half // n, 3 * units), BF16),
         3 * flops,
         where,
-        *held,
+        even,
+        mine,
         *weights,
         first,
         second,
@@ -187,7 +182,9 @@
         (grad, grad, grad, sds((8, 128), F32)),
         6 * flops,
         where,
-        *held,
+        even,
+        mine,
+        theirs,
         own,
         other,
     )

time: 150 us -> 152 us (1.013)
  waiting for transfers between devices: 8.66 us -> 10.3 us
    ppermute x4, waiting for transfers between devices: 5.61 us -> 9.86 us  [from_neighbour(): return lax.ppermute(value, ('core', 'col'), pairs)]
    ppermute x3, waiting for transfers between devices: 3.06 us -> 0.43 us  [swap_cores(): return lax.ppermute(value, 'core', [(0, 1), (1, 0)])]
where the time goes in v11:
time: 152 us
  blocking collectives  114 us (75%)
  starting transfers between devices  17.1 us (11%)
  waiting for transfers between devices  10.3 us (7%)
  Pallas kernels  6.96 us (5%)
  other arithmetic  1.67 us (1%)
    all_gather x1, blocking collectives, per_device(): even = lax.all_gather(both, 'col', axis=0, axis_index_groups=parity)  37.2 us
    all_to_all x1, blocking collectives, per_device(): pieces = lax.all_to_all(pieces, 'col', 0, 0, axis_index_groups=parity)  27.8 us
    all_to_all x1, blocking collectives, per_device(): parts = lax.all_to_all(parts, XY, 0, 0)  26.1 us
    all_to_all x1, blocking collectives, per_device(): own = lax.all_to_all(row, XY, 0, 0)  22.8 us
    ppermute x4, starting transfers between devices, from_neighbour(): return lax.ppermute(value, ('core', 'col'), pairs)  11.3 us
    ppermute x4, waiting for transfers between devices, from_neighbour(): return lax.ppermute(value, ('core', 'col'), pairs)  9.86 us
    pallas_call x8, Pallas kernels, call(): pl.pallas_call(body, out_shape=outs, in_specs=[SMEM if a.dtype == jnp.int...  6.96 us
    ppermute x3, starting transfers between devices, swap_cores(): return lax.ppermute(value, 'core', [(0, 1), (1, 0)])  5.75 us
  transfers between devices with their start and end apart: 7, of which 4 were waited for; matrix products, arithmetic and copies ran while one was open for 0% of the time, Pallas kernels for 4%

profile of v11, /device:TPU:8, one launch (start us, length us, event | category | flops | bytes accessed | tf_op | source)
XLA Modules:
  0.0 151.8 jit_solution(11043244239403553722)
XLA Ops:
  0.7 0.9 pad_maximum_fusion.1
  1.6 37.2 %all-gather = bf16[16,32,512]{2,1,0:T(8,128)(2,1)S(1)} all-gather(bf16[2,32,512]{2,1,0:T(8,128)(2,1)S(1)} %pad_maximum_fusion.1), channel_id=2, replica_groups={{0,2,4,6,8,10,12,14},{1,3,5,7,9,11,13,15},{16,18,20,22,24,26,28,30},{17..., dimensions={0}, use_global_device_ids=true | all-gather | bytes 589824 | tf_op jit(solution)/shard_map/all_gather | solution.py:147
  38.8 3.1 %collective-permute-start.2 = (bf16[4,2,32,512]{3,2,1,0:T(8,128)(2,1)S(1)}, bf16[4,2,32,512]{3,2,1,0:T(8,128)(2,1)S(1)}, u32[]{:S(2)}, u32[]{:S(2)}) collective-permute-start(bf16[4,2,32,512]{3,2,1,0:T(8,128)(2,1)S(1)} %get-tuple-element.20), channel_id=1, source_target_pairs={{15,0},{0,1},{1,2},{2,3},{3,4},{4,5},{5,6},{6,7},{7,8},{8,9},{9,10... | collective-permute-start | bytes 786440 | tf_op jit(solution)/shard_map/ppermute | solution.py:134
  41.9 0.0 copy-done.1
  42.0 0.0 copy-start
  42.0 0.1 pad_maximum_fusion.pair
  42.1 1.0 copy-done
  43.1 1.0 shard_map.84
  44.1 1.9 %collective-permute-start.1 = (f32[8,16,2496]{2,1,0:T(8,128)S(1)}, f32[8,16,2496]{2,1,0:T(8,128)S(1)}, u32[]{:S(2)}, u32[]{:S(2)}) collective-permute-start(f32[8,16,2496]{2,1,0:T(8,128)S(1)} %shard_map.84), channel_id=1, source_target_pairs={{0,16},{16,0},{1,17},{17,1},{2,18},{18,2},{3,19},{19,3},{4,20},{20... | collective-permute-start | bytes 3833864 | tf_op jit(solution)/shard_map/ppermute | solution.py:129
  46.0 2.3 %collective-permute-done.2.theirs = bf16[4,2,32,512]{3,2,1,0:T(8,128)(2,1)S(1)} collective-permute-done((bf16[4,2,32,512]{3,2,1,0:T(8,128)(2,1)S(1)}, bf16[4,2,32,512]{3,2,1,0:T(8,128)(2,1)S(1)}, u32[]{:S(2)}, u32[]{:S(2)}) %collective-permute-start.2) | collective-permute-done | bytes 262176 | tf_op jit(solution)/shard_map/ppermute | solution.py:134
  48.3 0.9 shard_map.85
  49.2 1.9 %collective-permute-start.3 = (f32[8,16,2496]{2,1,0:T(8,128)S(1)}, f32[8,16,2496]{2,1,0:T(8,128)S(1)}, u32[]{:S(2)}, u32[]{:S(2)}) collective-permute-start(f32[8,16,2496]{2,1,0:T(8,128)S(1)} %shard_map.85), channel_id=1, source_target_pairs={{0,16},{16,0},{1,17},{17,1},{2,18},{18,2},{3,19},{19,3},{4,20},{20... | collective-permute-start | bytes 3833864 | tf_op jit(solution)/shard_map/ppermute | solution.py:129
  51.2 2.8 %collective-permute-start = (bf16[4,2,32,512]{3,2,1,0:T(8,128)(2,1)S(1)}, bf16[4,2,32,512]{3,2,1,0:T(8,128)(2,1)S(1)}, u32[]{:S(2)}, u32[]{:S(2)}) collective-permute-start(bf16[4,2,32,512]{3,2,1,0:T(8,128)(2,1)S(1)} %get-tuple-element.21), channel_id=1, source_target_pairs={{1,0},{2,1},{3,2},{4,3},{5,4},{6,5},{7,6},{8,7},{9,8},{10,9},{11,1... | collective-permute-start | bytes 786440 | tf_op jit(solution)/shard_map/ppermute | solution.py:134
  53.9 5.5 %collective-permute-done.mine = bf16[4,2,32,512]{3,2,1,0:T(8,128)(2,1)S(1)} collective-permute-done((bf16[4,2,32,512]{3,2,1,0:T(8,128)(2,1)S(1)}, bf16[4,2,32,512]{3,2,1,0:T(8,128)(2,1)S(1)}, u32[]{:S(2)}, u32[]{:S(2)}) %collective-permute-start) | collective-permute-done | bytes 262176 | tf_op jit(solution)/shard_map/ppermute | solution.py:134
  59.4 0.0 collective-permute-done.1.got_first
  59.4 0.0 collective-permute-done.3.got_second
  59.4 1.0 shard_map.86
  60.4 26.1 %all_to_all.15.parts = bf16[16,16,2496]{2,1,0:T(8,128)(2,1)S(1)} all-to-all(bf16[16,16,2496]{2,1,0:T(8,128)(2,1)S(1)} %shard_map.86), channel_id=1, replica_groups=mesh['x'=4,'y'=4,'core'=2,'col'=16] {'x','y'}, dimensions={0} | all-to-all | bytes 2555904 | tf_op jit(solution)/shard_map/all_to_all | solution.py:169
  86.5 0.3 shard_map.87
  86.8 22.8 %all_to_all.16.deltas.own = bf16[16,16,2496]{2,1,0:T(8,128)(2,1)S(1)} all-to-all(bf16[16,16,2496]{2,1,0:T(8,128)(2,1)S(1)} %shard_map.87), channel_id=1, replica_groups=mesh['x'=4,'y'=4,'core'=2,'col'=16] {'x','y'}, dimensions={0} | all-to-all | bytes 2555904 | tf_op jit(solution)/shard_map/all_to_all | solution.py:171
  109.6 1.9 %collective-permute-start.5 = (bf16[16,16,2496]{2,1,0:T(8,128)(2,1)S(1)}, bf16[16,16,2496]{2,1,0:T(8,128)(2,1)S(1)}, u32[]{:S(2)}, u32[]{:S(2)}) collective-permute-start(bf16[16,16,2496]{2,1,0:T(8,128)(2,1)S(1)} %all_to_all.16.deltas.own), channel_id=1, source_target_pairs={{0,16},{16,0},{1,17},{17,1},{2,18},{18,2},{3,19},{19,3},{4,20},{20... | collective-permute-start | bytes 3833864 | tf_op jit(solution)/shard_map/ppermute | solution.py:129
  111.5 0.6 shard_map.88
  112.2 1.9 %collective-permute-start.4 = (bf16[4,32,512]{2,1,0:T(8,128)(2,1)S(1)}, bf16[4,32,512]{2,1,0:T(8,128)(2,1)S(1)}, u32[]{:S(2)}, u32[]{:S(2)}) collective-permute-start(bf16[4,32,512]{2,1,0:T(8,128)(2,1)S(1)} %get-tuple-element.13), channel_id=1, source_target_pairs={{1,0},{2,1},{3,2},{4,3},{5,4},{6,5},{7,6},{8,7},{9,8},{10,9},{11,1... | collective-permute-start | bytes 393224 | tf_op jit(solution)/shard_map/ppermute | solution.py:134
  114.1 0.4 collective-permute-done.5.deltas.other
  114.5 0.6 shard_map.89
  115.2 3.5 %collective-permute-start.6 = (bf16[4,32,512]{2,1,0:T(8,128)(2,1)S(1)}, bf16[4,32,512]{2,1,0:T(8,128)(2,1)S(1)}, u32[]{:S(2)}, u32[]{:S(2)}) collective-permute-start(bf16[4,32,512]{2,1,0:T(8,128)(2,1)S(1)} %get-tuple-element.15), channel_id=1, source_target_pairs={{15,0},{0,1},{1,2},{2,3},{3,4},{4,5},{5,6},{6,7},{7,8},{8,9},{9,10... | collective-permute-start | bytes 393224 | tf_op jit(solution)/shard_map/ppermute | solution.py:134
  118.7 2.4 %shard_map.90 = (bf16[832,512]{1,0:T(8,128)(2,1)}, bf16[832,512]{1,0:T(8,128)(2,1)}, bf16[832,512]{1,0:T(8,128)(2,1)}, f32[8,128]{1,0:T(8,128)S(1)}) custom-call(s32[1]{0:T(128)} %bitcast.where, bf16[8,2,32,512]{3,2,1,0:T(8,128)(2,1)S(1)} %bitcast.11, bf16[4,2,32,512]{3,2,1,0:T(8,128)(2,1)S(1)} %collective-permute-done.mine, ...), custom_call_target="tpu_custom_call" | custom-call | flops 1308622848 | bytes 6164484 | tf_op jit(solution)/shard_map/pallas_call | solution.py:32
  121.2 0.0 collective-permute-done.4.got_own
  121.2 2.1 %collective-permute-done.6.got_other = bf16[4,32,512]{2,1,0:T(8,128)(2,1)S(1)} collective-permute-done((bf16[4,32,512]{2,1,0:T(8,128)(2,1)S(1)}, bf16[4,32,512]{2,1,0:T(8,128)(2,1)S(1)}, u32[]{:S(2)}, u32[]{:S(2)}) %collective-permute-start.6) | collective-permute-done | bytes 131104 | tf_op jit(solution)/shard_map/ppermute | solution.py:134
  123.3 0.1 shard_map.91
  123.3 27.8 %all_to_all.17 = bf16[8,32,512]{2,1,0:T(8,128)(2,1)S(1)} all-to-all(bf16[8,32,512]{2,1,0:T(8,128)(2,1)S(1)} %shard_map.91), channel_id=1, replica_groups={{0,2,4,6,8,10,12,14},{1,3,5,7,9,11,13,15},{16,18,20,22,24,26,28,30},{17..., dimensions={0} | all-to-all | bytes 524288 | tf_op jit(solution)/shard_map/all_to_all | solution.py:193
  151.2 0.7 reduce_sum.12
  (4 shorter events, 0.0 us)
Async XLA Ops:
  0.6 41.3 %copy-start.1 = (bf16[512,832]{0,1:T(8,128)(2,1)S(1)}, bf16[512,832]{0,1:T(8,128)(2,1)}, u32[]{:S(2)}) copy-start(bf16[512,832]{0,1:T(8,128)(2,1)} %param.8) | copy-start | bytes 2555908
  0.6 41.3 %copy-start.2 = (bf16[512,832]{0,1:T(8,128)(2,1)S(1)}, bf16[512,832]{0,1:T(8,128)(2,1)}, u32[]{:S(2)}) copy-start(bf16[512,832]{0,1:T(8,128)(2,1)} %param.7) | copy-start | bytes 2555908
  38.8 9.5 %collective-permute-start.2 = (bf16[4,2,32,512]{3,2,1,0:T(8,128)(2,1)S(1)}, bf16[4,2,32,512]{3,2,1,0:T(8,128)(2,1)S(1)}, u32[]{:S(2)}, u32[]{:S(2)}) collective-permute-start(bf16[4,2,32,512]{3,2,1,0:T(8,128)(2,1)S(1)} %get-tuple-element.20), channel_id=1, source_target_pairs={{15,0},{0,1},{1,2},{2,3},{3,4},{4,5},{5,6},{6,7},{7,8},{8,9},{9,10... | collective-permute-start | bytes 786440 | tf_op jit(solution)/shard_map/ppermute | solution.py:134
  42.0 1.2 copy-start
  44.1 15.4 %collective-permute-start.1 = (f32[8,16,2496]{2,1,0:T(8,128)S(1)}, f32[8,16,2496]{2,1,0:T(8,128)S(1)}, u32[]{:S(2)}, u32[]{:S(2)}) collective-permute-start(f32[8,16,2496]{2,1,0:T(8,128)S(1)} %shard_map.84), channel_id=1, source_target_pairs={{0,16},{16,0},{1,17},{17,1},{2,18},{18,2},{3,19},{19,3},{4,20},{20... | collective-permute-start | bytes 3833864 | tf_op jit(solution)/shard_map/ppermute | solution.py:129
  49.2 10.2 %collective-permute-start.3 = (f32[8,16,2496]{2,1,0:T(8,128)S(1)}, f32[8,16,2496]{2,1,0:T(8,128)S(1)}, u32[]{:S(2)}, u32[]{:S(2)}) collective-permute-start(f32[8,16,2496]{2,1,0:T(8,128)S(1)} %shard_map.85), channel_id=1, source_target_pairs={{0,16},{16,0},{1,17},{17,1},{2,18},{18,2},{3,19},{19,3},{4,20},{20... | collective-permute-start | bytes 3833864 | tf_op jit(solution)/shard_map/ppermute | solution.py:129
  51.2 8.3 %collective-permute-start = (bf16[4,2,32,512]{3,2,1,0:T(8,128)(2,1)S(1)}, bf16[4,2,32,512]{3,2,1,0:T(8,128)(2,1)S(1)}, u32[]{:S(2)}, u32[]{:S(2)}) collective-permute-start(bf16[4,2,32,512]{3,2,1,0:T(8,128)(2,1)S(1)} %get-tuple-element.21), channel_id=1, source_target_pairs={{1,0},{2,1},{3,2},{4,3},{5,4},{6,5},{7,6},{8,7},{9,8},{10,9},{11,1... | collective-permute-start | bytes 786440 | tf_op jit(solution)/shard_map/ppermute | solution.py:134
  109.6 4.9 %collective-permute-start.5 = (bf16[16,16,2496]{2,1,0:T(8,128)(2,1)S(1)}, bf16[16,16,2496]{2,1,0:T(8,128)(2,1)S(1)}, u32[]{:S(2)}, u32[]{:S(2)}) collective-permute-start(bf16[16,16,2496]{2,1,0:T(8,128)(2,1)S(1)} %all_to_all.16.deltas.own), channel_id=1, source_target_pairs={{0,16},{16,0},{1,17},{17,1},{2,18},{18,2},{3,19},{19,3},{4,20},{20... | collective-permute-start | bytes 3833864 | tf_op jit(solution)/shard_map/ppermute | solution.py:129
  112.2 9.0 %collective-permute-start.4 = (bf16[4,32,512]{2,1,0:T(8,128)(2,1)S(1)}, bf16[4,32,512]{2,1,0:T(8,128)(2,1)S(1)}, u32[]{:S(2)}, u32[]{:S(2)}) collective-permute-start(bf16[4,32,512]{2,1,0:T(8,128)(2,1)S(1)} %get-tuple-element.13), channel_id=1, source_target_pairs={{1,0},{2,1},{3,2},{4,3},{5,4},{6,5},{7,6},{8,7},{9,8},{10,9},{11,1... | collective-permute-start | bytes 393224 | tf_op jit(solution)/shard_map/ppermute | solution.py:134
  115.2 8.1 %collective-permute-start.6 = (bf16[4,32,512]{2,1,0:T(8,128)(2,1)S(1)}, bf16[4,32,512]{2,1,0:T(8,128)(2,1)S(1)}, u32[]{:S(2)}, u32[]{:S(2)}) collective-permute-start(bf16[4,32,512]{2,1,0:T(8,128)(2,1)S(1)} %get-tuple-element.15), channel_id=1, source_target_pairs={{15,0},{0,1},{1,2},{2,3},{3,4},{4,5},{5,6},{6,7},{7,8},{8,9},{9,10... | collective-permute-start | bytes 393224 | tf_op jit(solution)/shard_map/ppermute | solution.py:134

commit v12 on v11

--- a/solution.py
+++ b/solution.py
@@ -61,7 +61,7 @@
     send_body(lambda kind: first_rows(1 - where[0], kind, even), (pair, down), out)
 
 
-def send_second_body(theirs, pair, down, out):
+def send_second_body(theirs, pair, down, _, out):
     send_body(lambda kind: flat(theirs[:, kind]), (pair, down), out)
 
 
@@ -154,7 +154,8 @@
     sent = sds((n // 2, half // n, 3 * units), F32)
     weights = (pair, down_weight)
     first = swap_cores(call(send_first_body, sent, 3 * flops // 2, where, even, *weights))
-    second = swap_cores(call(send_second_body, sent, 3 * flops // 2, theirs, *weights))
+    second = call(send_second_body, sent, 3 * flops // 2, theirs, *weights, after=(mine,))
+    second = swap_cores(second)
     parts = call(
         keep_body,
         sds((n, half // n, 3 * units), BF16),

time: 152 us -> 150 us (0.987)
    ppermute x4, waiting for transfers between devices: 9.86 us -> 5.6 us  [from_neighbour(): return lax.ppermute(value, ('core', 'col'), pairs)]
    ppermute x3, waiting for transfers between devices: 0.43 us -> 3.25 us  [swap_cores(): return lax.ppermute(value, 'core', [(0, 1), (1, 0)])]
where the time goes in v12:
time: 150 us
  blocking collectives  113 us (75%)
  starting transfers between devices  17.3 us (12%)
  waiting for transfers between devices  8.85 us (6%)
  Pallas kernels  6.95 us (5%)
  other arithmetic  1.67 us (1%)
    all_gather x1, blocking collectives, per_device(): even = lax.all_gather(both, 'col', axis=0, axis_index_groups=parity)  37.2 us
    all_to_all x1, blocking collectives, per_device(): pieces = lax.all_to_all(pieces, 'col', 0, 0, axis_index_groups=parity)  27.7 us
    all_to_all x1, blocking collectives, per_device(): parts = lax.all_to_all(parts, XY, 0, 0)  25.7 us
    all_to_all x1, blocking collectives, per_device(): own = lax.all_to_all(row, XY, 0, 0)  22.3 us
    ppermute x4, starting transfers between devices, from_neighbour(): return lax.ppermute(value, ('core', 'col'), pairs)  11.5 us
    pallas_call x8, Pallas kernels, call(): pl.pallas_call(body, out_shape=outs, in_specs=[SMEM if a.dtype == jnp.int...  6.95 us
    ppermute x3, starting transfers between devices, swap_cores(): return lax.ppermute(value, 'core', [(0, 1), (1, 0)])  5.75 us
    ppermute x4, waiting for transfers between devices, from_neighbour(): return lax.ppermute(value, ('core', 'col'), pairs)  5.6 us
  transfers between devices with their start and end apart: 7, of which 4 were waited for; matrix products, arithmetic and copies ran while one was open for 0% of the time, Pallas kernels for 4%

profile of v12, /device:TPU:8, one launch (start us, length us, event | category | flops | bytes accessed | tf_op | source)
XLA Modules:
  0.0 149.5 jit_solution(1409954526235219690)
XLA Ops:
  0.6 0.0 copy-start.1
  0.7 0.9 pad_maximum_fusion.1
  1.6 37.2 %all-gather = bf16[16,32,512]{2,1,0:T(8,128)(2,1)S(1)} all-gather(bf16[2,32,512]{2,1,0:T(8,128)(2,1)S(1)} %pad_maximum_fusion.1), channel_id=2, replica_groups={{0,2,4,6,8,10,12,14},{1,3,5,7,9,11,13,15},{16,18,20,22,24,26,28,30},{17..., dimensions={0}, use_global_device_ids=true | all-gather | bytes 589824 | tf_op jit(solution)/shard_map/all_gather | solution.py:147
  38.8 4.0 %collective-permute-start = (bf16[4,2,32,512]{3,2,1,0:T(8,128)(2,1)S(1)}, bf16[4,2,32,512]{3,2,1,0:T(8,128)(2,1)S(1)}, u32[]{:S(2)}, u32[]{:S(2)}) collective-permute-start(bf16[4,2,32,512]{3,2,1,0:T(8,128)(2,1)S(1)} %get-tuple-element.21), channel_id=1, source_target_pairs={{1,0},{2,1},{3,2},{4,3},{5,4},{6,5},{7,6},{8,7},{9,8},{10,9},{11,1... | collective-permute-start | bytes 786440 | tf_op jit(solution)/shard_map/ppermute | solution.py:134
  42.8 1.9 %collective-permute-start.2 = (bf16[4,2,32,512]{3,2,1,0:T(8,128)(2,1)S(1)}, bf16[4,2,32,512]{3,2,1,0:T(8,128)(2,1)S(1)}, u32[]{:S(2)}, u32[]{:S(2)}) collective-permute-start(bf16[4,2,32,512]{3,2,1,0:T(8,128)(2,1)S(1)} %get-tuple-element.20), channel_id=1, source_target_pairs={{15,0},{0,1},{1,2},{2,3},{3,4},{4,5},{5,6},{6,7},{7,8},{8,9},{9,10... | collective-permute-start | bytes 786440 | tf_op jit(solution)/shard_map/ppermute | solution.py:134
  44.8 0.0 copy-start
  44.8 0.1 pad_maximum_fusion.pair
  44.9 1.0 copy-done
  45.9 0.9 shard_map.84
  46.9 1.9 %collective-permute-start.1 = (f32[8,16,2496]{2,1,0:T(8,128)S(1)}, f32[8,16,2496]{2,1,0:T(8,128)S(1)}, u32[]{:S(2)}, u32[]{:S(2)}) collective-permute-start(f32[8,16,2496]{2,1,0:T(8,128)S(1)} %shard_map.84), channel_id=1, source_target_pairs={{0,16},{16,0},{1,17},{17,1},{2,18},{18,2},{3,19},{19,3},{4,20},{20... | collective-permute-start | bytes 3833864 | tf_op jit(solution)/shard_map/ppermute | solution.py:129
  48.8 0.0 collective-permute-done._.mine
  48.8 3.5 %collective-permute-done.2.theirs = bf16[4,2,32,512]{3,2,1,0:T(8,128)(2,1)S(1)} collective-permute-done((bf16[4,2,32,512]{3,2,1,0:T(8,128)(2,1)S(1)}, bf16[4,2,32,512]{3,2,1,0:T(8,128)(2,1)S(1)}, u32[]{:S(2)}, u32[]{:S(2)}) %collective-permute-start.2) | collective-permute-done | bytes 262176 | tf_op jit(solution)/shard_map/ppermute | solution.py:134
  52.3 1.0 shard_map.85
  53.2 1.9 %collective-permute-start.3 = (f32[8,16,2496]{2,1,0:T(8,128)S(1)}, f32[8,16,2496]{2,1,0:T(8,128)S(1)}, u32[]{:S(2)}, u32[]{:S(2)}) collective-permute-start(f32[8,16,2496]{2,1,0:T(8,128)S(1)} %shard_map.85), channel_id=1, source_target_pairs={{0,16},{16,0},{1,17},{17,1},{2,18},{18,2},{3,19},{19,3},{4,20},{20... | collective-permute-start | bytes 3833864 | tf_op jit(solution)/shard_map/ppermute | solution.py:129
  55.2 0.0 collective-permute-done.1.got_first
  55.2 3.0 %collective-permute-done.3.got_second = f32[8,16,2496]{2,1,0:T(8,128)S(1)} collective-permute-done((f32[8,16,2496]{2,1,0:T(8,128)S(1)}, f32[8,16,2496]{2,1,0:T(8,128)S(1)}, u32[]{:S(2)}, u32[]{:S(2)}) %collective-permute-start.3) | collective-permute-done | bytes 1277984 | tf_op jit(solution)/shard_map/ppermute | solution.py:129
  58.2 1.0 shard_map.86
  59.2 25.7 %all_to_all.15.parts = bf16[16,16,2496]{2,1,0:T(8,128)(2,1)S(1)} all-to-all(bf16[16,16,2496]{2,1,0:T(8,128)(2,1)S(1)} %shard_map.86), channel_id=1, replica_groups=mesh['x'=4,'y'=4,'core'=2,'col'=16] {'x','y'}, dimensions={0} | all-to-all | bytes 2555904 | tf_op jit(solution)/shard_map/all_to_all | solution.py:170
  84.8 0.3 shard_map.87
  85.1 22.3 %all_to_all.16.deltas.own = bf16[16,16,2496]{2,1,0:T(8,128)(2,1)S(1)} all-to-all(bf16[16,16,2496]{2,1,0:T(8,128)(2,1)S(1)} %shard_map.87), channel_id=1, replica_groups=mesh['x'=4,'y'=4,'core'=2,'col'=16] {'x','y'}, dimensions={0} | all-to-all | bytes 2555904 | tf_op jit(solution)/shard_map/all_to_all | solution.py:172
  107.5 1.9 %collective-permute-start.5 = (bf16[16,16,2496]{2,1,0:T(8,128)(2,1)S(1)}, bf16[16,16,2496]{2,1,0:T(8,128)(2,1)S(1)}, u32[]{:S(2)}, u32[]{:S(2)}) collective-permute-start(bf16[16,16,2496]{2,1,0:T(8,128)(2,1)S(1)} %all_to_all.16.deltas.own), channel_id=1, source_target_pairs={{0,16},{16,0},{1,17},{17,1},{2,18},{18,2},{3,19},{19,3},{4,20},{20... | collective-permute-start | bytes 3833864 | tf_op jit(solution)/shard_map/ppermute | solution.py:129
  109.4 0.6 shard_map.88
  110.0 2.1 %collective-permute-start.4 = (bf16[4,32,512]{2,1,0:T(8,128)(2,1)S(1)}, bf16[4,32,512]{2,1,0:T(8,128)(2,1)S(1)}, u32[]{:S(2)}, u32[]{:S(2)}) collective-permute-start(bf16[4,32,512]{2,1,0:T(8,128)(2,1)S(1)} %get-tuple-element.13), channel_id=1, source_target_pairs={{1,0},{2,1},{3,2},{4,3},{5,4},{6,5},{7,6},{8,7},{9,8},{10,9},{11,1... | collective-permute-start | bytes 393224 | tf_op jit(solution)/shard_map/ppermute | solution.py:134
  112.1 0.3 collective-permute-done.5.deltas.other
  112.4 0.6 shard_map.89
  113.0 3.5 %collective-permute-start.6 = (bf16[4,32,512]{2,1,0:T(8,128)(2,1)S(1)}, bf16[4,32,512]{2,1,0:T(8,128)(2,1)S(1)}, u32[]{:S(2)}, u32[]{:S(2)}) collective-permute-start(bf16[4,32,512]{2,1,0:T(8,128)(2,1)S(1)} %get-tuple-element.15), channel_id=1, source_target_pairs={{15,0},{0,1},{1,2},{2,3},{3,4},{4,5},{5,6},{6,7},{7,8},{8,9},{9,10... | collective-permute-start | bytes 393224 | tf_op jit(solution)/shard_map/ppermute | solution.py:134
  116.5 2.4 %shard_map.90 = (bf16[832,512]{1,0:T(8,128)(2,1)}, bf16[832,512]{1,0:T(8,128)(2,1)}, bf16[832,512]{1,0:T(8,128)(2,1)}, f32[8,128]{1,0:T(8,128)S(1)}) custom-call(s32[1]{0:T(128)} %bitcast.where, bf16[8,2,32,512]{3,2,1,0:T(8,128)(2,1)S(1)} %bitcast.11, bf16[4,2,32,512]{3,2,1,0:T(8,128)(2,1)S(1)} %collective-permute-done._.mine, ...), custom_call_target="tpu_custom_call" | custom-call | flops 1308622848 | bytes 6164484 | tf_op jit(solution)/shard_map/pallas_call | solution.py:32
  119.0 0.0 collective-permute-done.4.got_own
  119.0 2.1 %collective-permute-done.6.got_other = bf16[4,32,512]{2,1,0:T(8,128)(2,1)S(1)} collective-permute-done((bf16[4,32,512]{2,1,0:T(8,128)(2,1)S(1)}, bf16[4,32,512]{2,1,0:T(8,128)(2,1)S(1)}, u32[]{:S(2)}, u32[]{:S(2)}) %collective-permute-start.6) | collective-permute-done | bytes 131104 | tf_op jit(solution)/shard_map/ppermute | solution.py:134
  121.1 0.1 shard_map.91
  121.2 27.7 %all_to_all.17 = bf16[8,32,512]{2,1,0:T(8,128)(2,1)S(1)} all-to-all(bf16[8,32,512]{2,1,0:T(8,128)(2,1)S(1)} %shard_map.91), channel_id=1, replica_groups={{0,2,4,6,8,10,12,14},{1,3,5,7,9,11,13,15},{16,18,20,22,24,26,28,30},{17..., dimensions={0} | all-to-all | bytes 524288 | tf_op jit(solution)/shard_map/all_to_all | solution.py:194
  148.9 0.7 reduce_sum.12
  (4 shorter events, 0.0 us)
Async XLA Ops:
  0.6 44.1 %copy-start.1 = (bf16[512,832]{0,1:T(8,128)(2,1)S(1)}, bf16[512,832]{0,1:T(8,128)(2,1)}, u32[]{:S(2)}) copy-start(bf16[512,832]{0,1:T(8,128)(2,1)} %param.8) | copy-start | bytes 2555908
  0.6 44.1 %copy-start.2 = (bf16[512,832]{0,1:T(8,128)(2,1)S(1)}, bf16[512,832]{0,1:T(8,128)(2,1)}, u32[]{:S(2)}) copy-start(bf16[512,832]{0,1:T(8,128)(2,1)} %param.7) | copy-start | bytes 2555908
  38.8 10.0 %collective-permute-start = (bf16[4,2,32,512]{3,2,1,0:T(8,128)(2,1)S(1)}, bf16[4,2,32,512]{3,2,1,0:T(8,128)(2,1)S(1)}, u32[]{:S(2)}, u32[]{:S(2)}) collective-permute-start(bf16[4,2,32,512]{3,2,1,0:T(8,128)(2,1)S(1)} %get-tuple-element.21), channel_id=1, source_target_pairs={{1,0},{2,1},{3,2},{4,3},{5,4},{6,5},{7,6},{8,7},{9,8},{10,9},{11,1... | collective-permute-start | bytes 786440 | tf_op jit(solution)/shard_map/ppermute | solution.py:134
  42.8 9.5 %collective-permute-start.2 = (bf16[4,2,32,512]{3,2,1,0:T(8,128)(2,1)S(1)}, bf16[4,2,32,512]{3,2,1,0:T(8,128)(2,1)S(1)}, u32[]{:S(2)}, u32[]{:S(2)}) collective-permute-start(bf16[4,2,32,512]{3,2,1,0:T(8,128)(2,1)S(1)} %get-tuple-element.20), channel_id=1, source_target_pairs={{15,0},{0,1},{1,2},{2,3},{3,4},{4,5},{5,6},{6,7},{7,8},{8,9},{9,10... | collective-permute-start | bytes 786440 | tf_op jit(solution)/shard_map/ppermute | solution.py:134
  44.8 1.2 copy-start
  46.9 8.3 %collective-permute-start.1 = (f32[8,16,2496]{2,1,0:T(8,128)S(1)}, f32[8,16,2496]{2,1,0:T(8,128)S(1)}, u32[]{:S(2)}, u32[]{:S(2)}) collective-permute-start(f32[8,16,2496]{2,1,0:T(8,128)S(1)} %shard_map.84), channel_id=1, source_target_pairs={{0,16},{16,0},{1,17},{17,1},{2,18},{18,2},{3,19},{19,3},{4,20},{20... | collective-permute-start | bytes 3833864 | tf_op jit(solution)/shard_map/ppermute | solution.py:129
  53.2 4.9 %collective-permute-start.3 = (f32[8,16,2496]{2,1,0:T(8,128)S(1)}, f32[8,16,2496]{2,1,0:T(8,128)S(1)}, u32[]{:S(2)}, u32[]{:S(2)}) collective-permute-start(f32[8,16,2496]{2,1,0:T(8,128)S(1)} %shard_map.85), channel_id=1, source_target_pairs={{0,16},{16,0},{1,17},{17,1},{2,18},{18,2},{3,19},{19,3},{4,20},{20... | collective-permute-start | bytes 3833864 | tf_op jit(solution)/shard_map/ppermute | solution.py:129
  107.5 4.9 %collective-permute-start.5 = (bf16[16,16,2496]{2,1,0:T(8,128)(2,1)S(1)}, bf16[16,16,2496]{2,1,0:T(8,128)(2,1)S(1)}, u32[]{:S(2)}, u32[]{:S(2)}) collective-permute-start(bf16[16,16,2496]{2,1,0:T(8,128)(2,1)S(1)} %all_to_all.16.deltas.own), channel_id=1, source_target_pairs={{0,16},{16,0},{1,17},{17,1},{2,18},{18,2},{3,19},{19,3},{4,20},{20... | collective-permute-start | bytes 3833864 | tf_op jit(solution)/shard_map/ppermute | solution.py:129
  110.0 9.0 %collective-permute-start.4 = (bf16[4,32,512]{2,1,0:T(8,128)(2,1)S(1)}, bf16[4,32,512]{2,1,0:T(8,128)(2,1)S(1)}, u32[]{:S(2)}, u32[]{:S(2)}) collective-permute-start(bf16[4,32,512]{2,1,0:T(8,128)(2,1)S(1)} %get-tuple-element.13), channel_id=1, source_target_pairs={{1,0},{2,1},{3,2},{4,3},{5,4},{6,5},{7,6},{8,7},{9,8},{10,9},{11,1... | collective-permute-start | bytes 393224 | tf_op jit(solution)/shard_map/ppermute | solution.py:134
  113.0 8.1 %collective-permute-start.6 = (bf16[4,32,512]{2,1,0:T(8,128)(2,1)S(1)}, bf16[4,32,512]{2,1,0:T(8,128)(2,1)S(1)}, u32[]{:S(2)}, u32[]{:S(2)}) collective-permute-start(bf16[4,32,512]{2,1,0:T(8,128)(2,1)S(1)} %get-tuple-element.15), channel_id=1, source_target_pairs={{15,0},{0,1},{1,2},{2,3},{3,4},{4,5},{5,6},{6,7},{7,8},{8,9},{9,10... | collective-permute-start | bytes 393224 | tf_op jit(solution)/shard_map/ppermute | solution.py:134
